TPU v7x, 512 devices: a whole 4x4x16 slice. The times are simulated.
512 devices in a mesh: section: 4 (over y), resp: 128 (over z, x, core).
Axes of the slice: x: 4, y: 4, z: 16, core: 2. Of those that a mesh axis runs over, the one named last changes fastest.
Arguments:
- queries: bfloat16 [4, 8192, 4096], P('section', 'resp'), may hold values from -100 to 100
- resp_kv: bfloat16 [4, 8192, 1024], P('section', 'resp'), may hold values from -4 to 4
- prefix_kv: bfloat16 [4, 65536, 1024], P('section', 'resp'), may hold values from -6 to 6
- owner: int32 [4, 4], P('section'), may hold values from 0 to 127, as said below
- seg_len: int32 [256, 4], P('resp'), may hold values from 1 to 16, 32 in all within a row
Outputs:
- out: bfloat16 [4, 8192, 4096], P('section', 'resp')
Inputs may be any that keep to these rules, and one draw needn't show every extreme that they name: owner[l, p] is one of the devices p * 32 to (p + 1) * 32 - 1, those holding prompt p's responses.
All inputs are finite; a program needn't handle non-finite values.
Results may differ from a plain program's by a relative error of at most 0.0099.
Values may be sent and summed in bfloat16 or wider, within the bound.
No kernel may reach another device: no remote copies, remote signals or barrier semaphores. Data moves between devices by JAX's collectives and lax.ppermute only.
A program may use at most 64 MiB of HBM per device.

v0:
```python
import math

import jax
import jax.numpy as jnp
from jax import lax
from jax.sharding import PartitionSpec as P

HQ = 32
HEAD_SIZE = 128
TOKM = 32
MB = 2
PROMPTS = 4


EPS = 1e-06


def swapped(x, axis, stride):
    return lax.ppermute(x, axis, [(i, i ^ 1 << stride) for i in range(lax.axis_size(axis))])


def from_behind(block, axis, distance):
    devices = range(lax.axis_size(axis))
    route = [(i - distance, i) for i in devices if i - distance in devices]
    return lax.ppermute(block, axis, route)


def same_response(lengths, count_of_rows):
    ends = jnp.cumsum(lengths)
    position = jnp.arange(count_of_rows, dtype=jnp.int32)
    response = jnp.sum((position[:, None] >= ends[None, :]).astype(jnp.int32), axis=1)
    return (response[:, None] == response[None, :]) & (position[None, :] <= position[:, None])


def attend(mixed, prefix, local_rows, local_lengths):
    count_of_rows = mixed.shape[0]
    kv_width = prefix.shape[1] // 2
    groups = kv_width // HEAD_SIZE
    heads_of_query = mixed.reshape(count_of_rows, groups, HQ // groups, HEAD_SIZE)
    distant_keys = prefix[:, :kv_width].reshape(-1, groups, HEAD_SIZE)
    distant_values = prefix[:, kv_width:].reshape(-1, groups, HEAD_SIZE)
    nearby_keys = local_rows[:, :kv_width].reshape(-1, groups, HEAD_SIZE)
    nearby_values = local_rows[:, kv_width:].reshape(-1, groups, HEAD_SIZE)
    scaling = 1.0 / math.sqrt(HEAD_SIZE)
    far_scores = (
        jnp.einsum(
            "fiqv,civ->iqfc", heads_of_query, distant_keys, preferred_element_type=jnp.float32
        )
        * scaling
    )
    near_scores = (
        jnp.einsum(
            "fiqv,civ->iqfc", heads_of_query, nearby_keys, preferred_element_type=jnp.float32
        )
        * scaling
    )
    allowed = same_response(local_lengths, count_of_rows)
    near_scores = jnp.where(allowed[None, None], near_scores, -jnp.inf)
    row_top = jnp.maximum(
        jnp.max(far_scores, axis=3, keepdims=True), jnp.max(near_scores, axis=3, keepdims=True)
    )
    far_exp = jnp.exp(far_scores - row_top)
    near_exp = jnp.exp(near_scores - row_top)
    row_total = jnp.sum(far_exp, axis=3, keepdims=True) + jnp.sum(near_exp, axis=3, keepdims=True)
    distant_weights = (far_exp / row_total).astype(jnp.bfloat16)
    nearby_weights = (near_exp / row_total).astype(jnp.bfloat16)
    attended_output = jnp.einsum(
        "euzm,meh->zeuh", distant_weights, distant_values, preferred_element_type=jnp.float32
    )
    attended_output = attended_output + jnp.einsum(
        "euzm,meh->zeuh", nearby_weights, nearby_values, preferred_element_type=jnp.float32
    )
    attended_output = attended_output.reshape(count_of_rows, -1)
    square = jnp.mean(attended_output * attended_output, axis=1, keepdims=True)
    return (attended_output * lax.rsqrt(square + EPS)).astype(jnp.bfloat16)


def local(queries, resp_kv, prefix_kv, owner, seg_len):
    section_index = lax.axis_index("section")
    section_count = lax.axis_size("section")
    devices = lax.axis_size("resp")
    group_size = devices // PROMPTS
    bit_count = group_size.bit_length() - 1
    my_place = lax.axis_index("resp")
    my_rank = my_place % group_size
    my_block = my_place // group_size
    root_rank = (
        jnp.sum(jnp.where(jnp.arange(PROMPTS, dtype=jnp.int32) == my_block, owner[0], 0))
        % group_size
    )
    current = prefix_kv[0]
    for bit_level in range(bit_count):
        incoming = swapped(current, "resp", bit_level)
        holder = (my_rank ^ root_rank) >> bit_level == 0
        current = jnp.where(holder, current, incoming)
    micro_queries = queries[0].reshape(MB, TOKM, -1)
    micro_local = resp_kv[0].reshape(MB, TOKM, -1)
    carried = jnp.zeros((TOKM, micro_queries.shape[2]), jnp.bfloat16)
    results = jnp.zeros_like(micro_queries)
    tick_count = MB + section_count - 1
    for tick_step in range(tick_count):
        micro_index = tick_step - section_index
        is_valid = (micro_index >= 0) & (micro_index < MB)
        clamp_index = jnp.clip(micro_index, 0, MB - 1)
        query_rows = lax.dynamic_index_in_dim(micro_queries, clamp_index, 0, keepdims=False)
        local_rows = lax.dynamic_index_in_dim(micro_local, clamp_index, 0, keepdims=False)
        local_lengths = lax.dynamic_index_in_dim(seg_len, clamp_index, 0, keepdims=False)
        mixed = (query_rows.astype(jnp.float32) + carried.astype(jnp.float32)).astype(jnp.bfloat16)
        normed = attend(mixed, current, local_rows, local_lengths)
        updated = lax.dynamic_update_index_in_dim(results, normed, clamp_index, 0)
        results = jnp.where(is_valid, updated, results)
        if tick_step + 1 < tick_count:
            carried = from_behind(normed, "section", 1)
    return results.reshape(1, MB * TOKM, -1)


def solution(mesh):
    return jax.shard_map(
        local,
        mesh=mesh,
        in_specs=(
            P("section", "resp", None),
            P("section", "resp", None),
            P("section", "resp", None),
            P("section", None),
            P("resp", None),
        ),
        out_specs=P("section", "resp", None),
        check_vma=False,
    )
```

profile of v0, /device:TPU:24, one launch (start us, length us, event | category | flops | bytes accessed | tf_op | source)
XLA Modules:
  0.0 195.3 jit_solution(11151582965238591638)
XLA Ops:
  0.0 1.5 copy.56
  1.5 1.9 collective-permute-start
  3.5 0.6 fusion.87
  6.2 3.5 %collective-permute-start.1 = (bf16[512,1024]{0,1:T(8,128)(2,1)S(1)}, bf16[512,1024]{0,1:T(8,128)(2,1)}, u32[]{:S(2)}, u32[]{:S(2)}) collective-permute-start(bf16[512,1024]{0,1:T(8,128)(2,1)S(1)} %broadcast_select_fusion), channel_id=1, source_target_pairs={{0,2},{1,3},{2,0},{3,1},{4,6},{5,7},{6,4},{7,5},{8,10},{9,11},{10,... | collective-permute-start | bytes 3145736 | tf_op jit(solution)/shard_map/ppermute | solution.py:19
  9.8 24.1 %collective-permute-done.1 = bf16[512,1024]{0,1:T(8,128)(2,1)} collective-permute-done((bf16[512,1024]{0,1:T(8,128)(2,1)S(1)}, bf16[512,1024]{0,1:T(8,128)(2,1)}, u32[]{:S(2)}, u32[]{:S(2)}) %collective-permute-start.1) | collective-permute-done | bytes 1048608 | tf_op jit(solution)/shard_map/ppermute | solution.py:19
  33.9 1.3 broadcast_select_fusion.1
  35.3 5.1 %collective-permute-start.2 = (bf16[512,1024]{0,1:T(8,128)(2,1)S(1)}, bf16[512,1024]{0,1:T(8,128)(2,1)}, u32[]{:S(2)}, u32[]{:S(2)}) collective-permute-start(bf16[512,1024]{0,1:T(8,128)(2,1)S(1)} %broadcast_select_fusion.1), channel_id=1, source_target_pairs={{0,4},{1,5},{2,6},{3,7},{4,0},{5,1},{6,2},{7,3},{8,12},{9,13},{10,... | collective-permute-start | bytes 3145736 | tf_op jit(solution)/shard_map/ppermute | solution.py:19
  41.2 22.5 %collective-permute-done.2 = bf16[512,1024]{0,1:T(8,128)(2,1)} collective-permute-done((bf16[512,1024]{0,1:T(8,128)(2,1)S(1)}, bf16[512,1024]{0,1:T(8,128)(2,1)}, u32[]{:S(2)}, u32[]{:S(2)}) %collective-permute-start.2) | collective-permute-done | bytes 1048608 | tf_op jit(solution)/shard_map/ppermute | solution.py:19
  63.7 1.3 broadcast_select_fusion.2
  65.0 3.8 %collective-permute-start.3 = (bf16[512,1024]{0,1:T(8,128)(2,1)S(1)}, bf16[512,1024]{0,1:T(8,128)(2,1)}, u32[]{:S(2)}, u32[]{:S(2)}) collective-permute-start(bf16[512,1024]{0,1:T(8,128)(2,1)S(1)} %broadcast_select_fusion.2), channel_id=1, source_target_pairs={{0,8},{1,9},{2,10},{3,11},{4,12},{5,13},{6,14},{7,15},{8,0},{9,1},... | collective-permute-start | bytes 3145736 | tf_op jit(solution)/shard_map/ppermute | solution.py:19
  69.3 21.8 %collective-permute-done.3 = bf16[512,1024]{0,1:T(8,128)(2,1)} collective-permute-done((bf16[512,1024]{0,1:T(8,128)(2,1)S(1)}, bf16[512,1024]{0,1:T(8,128)(2,1)}, u32[]{:S(2)}, u32[]{:S(2)}) %collective-permute-start.3) | collective-permute-done | bytes 1048608 | tf_op jit(solution)/shard_map/ppermute | solution.py:19
  91.1 1.3 broadcast_select_fusion.3
  92.4 5.2 %collective-permute-start.4 = (bf16[512,1024]{0,1:T(8,128)(2,1)S(1)}, bf16[512,1024]{0,1:T(8,128)(2,1)}, u32[]{:S(2)}, u32[]{:S(2)}) collective-permute-start(bf16[512,1024]{0,1:T(8,128)(2,1)S(1)} %broadcast_select_fusion.3), channel_id=1, source_target_pairs={{0,16},{1,17},{2,18},{3,19},{4,20},{5,21},{6,22},{7,23},{8,24},{9,... | collective-permute-start | bytes 3145736 | tf_op jit(solution)/shard_map/ppermute | solution.py:19
  98.5 0.5 fusion.104
  99.0 42.6 %collective-permute-done.4 = bf16[512,1024]{0,1:T(8,128)(2,1)} collective-permute-done((bf16[512,1024]{0,1:T(8,128)(2,1)S(1)}, bf16[512,1024]{0,1:T(8,128)(2,1)}, u32[]{:S(2)}, u32[]{:S(2)}) %collective-permute-start.4) | collective-permute-done | bytes 1048608 | tf_op jit(solution)/shard_map/ppermute | solution.py:19
  141.8 0.5 bitcast_reduce_fusion.4
  142.3 0.6 fusion.5
  143.3 1.0 multiply_reduce_fusion.4
  144.3 0.3 copy.64
  145.0 1.3 collective-permute-start.5
  146.5 7.6 %collective-permute-done.5 = bf16[32,4096]{1,0:T(8,128)(2,1)S(1)} collective-permute-done((bf16[32,4096]{1,0:T(8,128)(2,1)S(1)}, bf16[32,4096]{1,0:T(8,128)(2,1)S(1)}, u32[]{:S(2)}, u32[]{:S(2)}) %collective-permute-start.5) | collective-permute-done | bytes 262176 | tf_op jit(solution)/shard_map/ppermute | solution.py:25
  154.2 0.5 bitcast_reduce_fusion.3
  154.8 0.5 fusion.105
  155.3 0.6 fusion.6
  156.4 1.0 multiply_reduce_fusion.3
  157.3 0.3 copy.73
  158.1 1.3 collective-permute-start.6
  159.5 6.8 %collective-permute-done.6 = bf16[32,4096]{1,0:T(8,128)(2,1)S(1)} collective-permute-done((bf16[32,4096]{1,0:T(8,128)(2,1)S(1)}, bf16[32,4096]{1,0:T(8,128)(2,1)S(1)}, u32[]{:S(2)}, u32[]{:S(2)}) %collective-permute-start.6) | collective-permute-done | bytes 262176 | tf_op jit(solution)/shard_map/ppermute | solution.py:25
  166.5 0.5 bitcast_reduce_fusion.2
  167.0 0.5 fusion.106
  167.5 0.6 fusion.7
  168.6 1.0 multiply_reduce_fusion.2
  169.5 0.3 copy.82
  170.3 1.5 collective-permute-start.7
  171.9 6.6 %collective-permute-done.7 = bf16[32,4096]{1,0:T(8,128)(2,1)S(1)} collective-permute-done((bf16[32,4096]{1,0:T(8,128)(2,1)S(1)}, bf16[32,4096]{1,0:T(8,128)(2,1)S(1)}, u32[]{:S(2)}, u32[]{:S(2)}) %collective-permute-start.7) | collective-permute-done | bytes 262176 | tf_op jit(solution)/shard_map/ppermute | solution.py:25
  178.7 0.5 bitcast_reduce_fusion.1
  179.2 0.5 fusion.107
  179.7 0.6 fusion.8
  180.8 1.0 multiply_reduce_fusion.1
  181.7 0.3 copy.91
  182.5 1.3 collective-permute-start.8
  183.9 6.8 %collective-permute-done.8 = bf16[32,4096]{1,0:T(8,128)(2,1)S(1)} collective-permute-done((bf16[32,4096]{1,0:T(8,128)(2,1)S(1)}, bf16[32,4096]{1,0:T(8,128)(2,1)S(1)}, u32[]{:S(2)}, u32[]{:S(2)}) %collective-permute-start.8) | collective-permute-done | bytes 262176 | tf_op jit(solution)/shard_map/ppermute | solution.py:25
  190.9 0.5 bitcast_reduce_fusion
  191.4 0.5 fusion.108
  192.0 0.6 fusion.9
  193.0 1.0 multiply_reduce_fusion
  194.0 0.3 copy.100
  194.6 0.8 copy-done
  (93 shorter events, 7.3 us)
Async XLA Ops:
  0.0 3.5 %copy-start.4 = (s32[1,4]{1,0:T(1,128)S(1)}, s32[1,4]{1,0:T(1,128)}, u32[]{:S(2)}) copy-start(s32[1,4]{1,0:T(1,128)} %param.8) | copy-start | bytes 52
  1.5 4.6 %collective-permute-start = (bf16[512,1024]{0,1:T(8,128)(2,1)S(1)}, bf16[512,1024]{0,1:T(8,128)(2,1)S(1)}, u32[]{:S(2)}, u32[]{:S(2)}) collective-permute-start(bf16[512,1024]{0,1:T(8,128)(2,1)S(1)} %bitcast.236), channel_id=1, source_target_pairs={{0,1},{1,0},{2,3},{3,2},{4,5},{5,4},{6,7},{7,6},{8,9},{9,8},{10,11... | collective-permute-start | bytes 3145736 | tf_op jit(solution)/shard_map/ppermute | solution.py:19
  6.2 34.2 %copy-start.3 = (s32[2,4]{1,0:T(2,128)S(1)}, s32[2,4]{1,0:T(2,128)}, u32[]{:S(2)}) copy-start(s32[2,4]{1,0:T(2,128)} %param.9) | copy-start | bytes 100
  6.2 34.9 %copy-start.1 = (bf16[1,64,4096]{2,1,0:T(8,128)(2,1)S(1)}, bf16[1,64,4096]{2,1,0:T(8,128)(2,1)}, u32[]{:S(2)}) copy-start(bf16[1,64,4096]{2,1,0:T(8,128)(2,1)} %param.5) | copy-start | bytes 1572868
  6.2 27.7 %collective-permute-start.1 = (bf16[512,1024]{0,1:T(8,128)(2,1)S(1)}, bf16[512,1024]{0,1:T(8,128)(2,1)}, u32[]{:S(2)}, u32[]{:S(2)}) collective-permute-start(bf16[512,1024]{0,1:T(8,128)(2,1)S(1)} %broadcast_select_fusion), channel_id=1, source_target_pairs={{0,2},{1,3},{2,0},{3,1},{4,6},{5,7},{6,4},{7,5},{8,10},{9,11},{10,... | collective-permute-start | bytes 3145736 | tf_op jit(solution)/shard_map/ppermute | solution.py:19
  35.3 33.9 %copy-start.2 = (bf16[1,64,1024]{2,1,0:T(8,128)(2,1)S(1)}, bf16[1,64,1024]{2,1,0:T(8,128)(2,1)}, u32[]{:S(2)}) copy-start(bf16[1,64,1024]{2,1,0:T(8,128)(2,1)} %param.6) | copy-start | bytes 393220
  35.3 28.4 %collective-permute-start.2 = (bf16[512,1024]{0,1:T(8,128)(2,1)S(1)}, bf16[512,1024]{0,1:T(8,128)(2,1)}, u32[]{:S(2)}, u32[]{:S(2)}) collective-permute-start(bf16[512,1024]{0,1:T(8,128)(2,1)S(1)} %broadcast_select_fusion.1), channel_id=1, source_target_pairs={{0,4},{1,5},{2,6},{3,7},{4,0},{5,1},{6,2},{7,3},{8,12},{9,13},{10,... | collective-permute-start | bytes 3145736 | tf_op jit(solution)/shard_map/ppermute | solution.py:19
  65.0 26.1 %collective-permute-start.3 = (bf16[512,1024]{0,1:T(8,128)(2,1)S(1)}, bf16[512,1024]{0,1:T(8,128)(2,1)}, u32[]{:S(2)}, u32[]{:S(2)}) collective-permute-start(bf16[512,1024]{0,1:T(8,128)(2,1)S(1)} %broadcast_select_fusion.2), channel_id=1, source_target_pairs={{0,8},{1,9},{2,10},{3,11},{4,12},{5,13},{6,14},{7,15},{8,0},{9,1},... | collective-permute-start | bytes 3145736 | tf_op jit(solution)/shard_map/ppermute | solution.py:19
  92.4 49.2 %collective-permute-start.4 = (bf16[512,1024]{0,1:T(8,128)(2,1)S(1)}, bf16[512,1024]{0,1:T(8,128)(2,1)}, u32[]{:S(2)}, u32[]{:S(2)}) collective-permute-start(bf16[512,1024]{0,1:T(8,128)(2,1)S(1)} %broadcast_select_fusion.3), channel_id=1, source_target_pairs={{0,16},{1,17},{2,18},{3,19},{4,20},{5,21},{6,22},{7,23},{8,24},{9,... | collective-permute-start | bytes 3145736 | tf_op jit(solution)/shard_map/ppermute | solution.py:19
  145.0 9.1 %collective-permute-start.5 = (bf16[32,4096]{1,0:T(8,128)(2,1)S(1)}, bf16[32,4096]{1,0:T(8,128)(2,1)S(1)}, u32[]{:S(2)}, u32[]{:S(2)}) collective-permute-start(bf16[32,4096]{1,0:T(8,128)(2,1)S(1)} %fusion.28), channel_id=1, source_target_pairs={{0,128},{128,256},{256,384},{1,129},{129,257},{257,385},{2,130},{1... | collective-permute-start | bytes 786440 | tf_op jit(solution)/shard_map/ppermute | solution.py:25
  158.1 8.3 %collective-permute-start.6 = (bf16[32,4096]{1,0:T(8,128)(2,1)S(1)}, bf16[32,4096]{1,0:T(8,128)(2,1)S(1)}, u32[]{:S(2)}, u32[]{:S(2)}) collective-permute-start(bf16[32,4096]{1,0:T(8,128)(2,1)S(1)} %fusion.27), channel_id=1, source_target_pairs={{0,128},{128,256},{256,384},{1,129},{129,257},{257,385},{2,130},{1... | collective-permute-start | bytes 786440 | tf_op jit(solution)/shard_map/ppermute | solution.py:25
  170.3 8.3 %collective-permute-start.7 = (bf16[32,4096]{1,0:T(8,128)(2,1)S(1)}, bf16[32,4096]{1,0:T(8,128)(2,1)S(1)}, u32[]{:S(2)}, u32[]{:S(2)}) collective-permute-start(bf16[32,4096]{1,0:T(8,128)(2,1)S(1)} %fusion.26), channel_id=1, source_target_pairs={{0,128},{128,256},{256,384},{1,129},{129,257},{257,385},{2,130},{1... | collective-permute-start | bytes 786440 | tf_op jit(solution)/shard_map/ppermute | solution.py:25
  182.5 8.3 %collective-permute-start.8 = (bf16[32,4096]{1,0:T(8,128)(2,1)S(1)}, bf16[32,4096]{1,0:T(8,128)(2,1)S(1)}, u32[]{:S(2)}, u32[]{:S(2)}) collective-permute-start(bf16[32,4096]{1,0:T(8,128)(2,1)S(1)} %fusion.25), channel_id=1, source_target_pairs={{0,128},{128,256},{256,384},{1,129},{129,257},{257,385},{2,130},{1... | collective-permute-start | bytes 786440 | tf_op jit(solution)/shard_map/ppermute | solution.py:25
  194.5 0.8 copy-start
where the time goes:
time: 198 us; the launch traced here: 195 us
  waiting for transfers between devices  139 us (70%)
  starting transfers between devices  24.9 us (13%)
  other arithmetic  12.4 us (6%)
  matrix products  11.5 us (6%)
  local copies, waits for them, and re-layouts  4.91 us (2%)
  between operations  2.73 us (1%)
    ppermute x5, waiting for transfers between devices, swapped(): lax.ppermute(x, axis, [(i, i ^ 1 << stride) for i in range(lax.axis_size(...  111 us
    ppermute x4, waiting for transfers between devices, from_behind(): return lax.ppermute(block, axis, route)  27.9 us
    ppermute x5, starting transfers between devices, swapped(): lax.ppermute(x, axis, [(i, i ^ 1 << stride) for i in range(lax.axis_size(...  19.5 us
    ppermute x4, starting transfers between devices, from_behind(): return lax.ppermute(block, axis, route)  5.35 us
    dot_general x5, matrix products, attend(): jnp.einsum('euzm,meh->zeuh', distant_weights, distant_values, preferred_e...  4.84 us
    select_n x5, other arithmetic, local(): current = jnp.where(holder, current, incoming)  4.23 us
  transfers between devices with their start and end apart: 9, of which 8 were waited for; matrix products, arithmetic and copies ran while one was open for 2% of the time, Pallas kernels for 0%

commit v1 on v0

v1 whole, which is shorter than its diff:
```python
import math

import jax
import jax.numpy as jnp
from jax import lax
from jax.experimental import pallas as pl
from jax.experimental.pallas import tpu as pltpu
from jax.sharding import Mesh, PartitionSpec as P

HQ = 32
KVH = 4
GROUP = HQ // KVH
HEAD_SIZE = 128
WIDTH = HQ * HEAD_SIZE
KVW = KVH * HEAD_SIZE
PLEN = 512
TOKM = 32
RESPS = 4
PROMPTS = 4
EPS = 1e-06
EXP2_SCALE = math.log2(math.e) / math.sqrt(HEAD_SIZE)

SECTION = ("yh", "yl")
RESP = ("p", "zh", "zl", "x", "c")
PLANE = ("zl", "x")
SPREAD = ("yl", *PLANE)


def swap(x, axis):
    return lax.ppermute(x, axis, [(0, 1), (1, 0)])


def product(a, b, over):
    return lax.dot_general(a, b, (((over,), (over,)), ((), ())), preferred_element_type=jnp.float32)


def over_rows(reduce, blocks):
    pair = jnp.maximum if reduce is jnp.max else jnp.add
    wide = reduce(pair(blocks[0], blocks[1]), axis=0, keepdims=True)
    return pair(wide, reduce(blocks[2], axis=0, keepdims=True))


def attend(x, keys, values, near_mask, att_ref):
    rows = x.shape[0]
    groups = range(KVH)
    heads = [x[:, h * HEAD_SIZE : (h + 1) * HEAD_SIZE] for h in range(HQ)]
    queries = [jnp.concatenate(heads[g * GROUP : (g + 1) * GROUP], axis=0) for g in groups]
    scores = [[product(k, queries[g], 1) for k in keys(g)] for g in groups]
    for g in groups:
        scores[g][2] = scores[g][2] + near_mask
    top = [over_rows(jnp.max, scores[g]) for g in groups]
    raised = [[jnp.exp2((s - top[g]) * EXP2_SCALE) for s in scores[g]] for g in groups]
    share = [1.0 / over_rows(jnp.sum, raised[g]) for g in groups]
    weights = [[(e * share[g]).astype(jnp.bfloat16) for e in raised[g]] for g in groups]
    total = jnp.zeros((1, GROUP * rows), jnp.float32)
    for g in groups:
        out = sum(product(v, w, 0) for v, w in zip(values(g), weights[g], strict=True))
        att_ref[g] = out
        total = total + jnp.sum(out * out, axis=0, keepdims=True)
    reach = rows
    while reach < GROUP * rows:
        total = total + pltpu.roll(total, reach, 1)
        reach *= 2
    return lax.rsqrt(total * (1.0 / WIDTH) + EPS)


def pair_kernel(place_ref, seg_ref, own_ref, other_ref, *refs):
    if len(refs) == 6:
        carried_ref, kv0_ref, kv1_ref, a_ref, b_ref, att_ref = refs
        carried = carried_ref[...].astype(jnp.float32)
    else:
        kv0_ref, kv1_ref, b_ref, a_ref, att_ref = refs
        carried = 0.0
    micro, second = place_ref[0], place_ref[1]

    at_key = lax.broadcasted_iota(jnp.int32, (TOKM, TOKM), 0)
    at_query = lax.broadcasted_iota(jnp.int32, (TOKM, TOKM), 1)
    of_key, of_query = jnp.zeros_like(at_key), jnp.zeros_like(at_query)
    end = jnp.int32(0)
    for i in range(RESPS):
        end = end + seg_ref[micro, i]
        of_key = of_key + (at_key >= end).astype(jnp.int32)
        of_query = of_query + (at_query >= end).astype(jnp.int32)
    allowed = (of_key == of_query) & (at_key <= at_query)
    near_mask = jnp.where(allowed, 0.0, -jnp.inf).astype(jnp.float32)
    near_mask = jnp.concatenate([near_mask] * GROUP, axis=1)

    for layer, out_ref in enumerate((a_ref, b_ref)):
        is_own = second == layer
        query = jnp.where(is_own, own_ref[:, :WIDTH], other_ref[:, :WIDTH]).astype(jnp.float32)
        near = jnp.where(is_own, own_ref[:, WIDTH:], other_ref[:, WIDTH:])
        x = (query + carried).astype(jnp.bfloat16)

        def blocks(first, layer=layer, near=near):
            def of_group(g):
                lanes = slice(first + g * HEAD_SIZE, first + (g + 1) * HEAD_SIZE)
                return [kv0_ref[layer, :, lanes], kv1_ref[layer, :, lanes], near[:, lanes]]

            return of_group

        scaling = attend(x, blocks(0), blocks(KVW), near_mask, att_ref)
        for g in range(KVH):
            normed = (att_ref[g] * scaling).T.astype(jnp.bfloat16)
            for at in range(GROUP):
                h = g * GROUP + at
                out_ref[:, h * HEAD_SIZE : (h + 1) * HEAD_SIZE] = normed[at * TOKM : (at + 1) * TOKM]
        if layer == 0:
            carried = a_ref[...].astype(jnp.float32)


def attend_pair(place, seg_len, own, other, carried, kv0, kv1):
    vmem = pl.BlockSpec(memory_space=pltpu.VMEM)
    smem = pl.BlockSpec(memory_space=pltpu.SMEM)
    out = jax.ShapeDtypeStruct((TOKM, WIDTH), jnp.bfloat16)
    scratch = [pltpu.VMEM((KVH, HEAD_SIZE, GROUP * TOKM), jnp.float32)]
    if carried is None:
        middle, outs, scratch = [], (out,), [pltpu.VMEM(out.shape, out.dtype), *scratch]
    else:
        middle, outs = [carried], (out, out)
    return pl.pallas_call(
        pair_kernel,
        out_shape=outs,
        in_specs=[smem, smem] + [vmem] * (4 + len(middle)),
        out_specs=(vmem,) * len(outs),
        scratch_shapes=scratch,
        compiler_params=pltpu.CompilerParams(vmem_limit_bytes=12 * 1024 * 1024),
        cost_estimate=pl.CostEstimate(
            flops=2 * 4 * HQ * TOKM * (PLEN + TOKM) * HEAD_SIZE,
            bytes_accessed=4 * 1024 * 1024,
            transcendentals=2 * HQ * TOKM * (PLEN + TOKM),
        ),
    )(place, seg_len, own, other, *middle, kv0, kv1)


def spread_prefix(prefix, is_owner, is_other_core, beside):
    half = PLEN // 2
    parts = math.prod(lax.axis_size(axis) for axis in PLANE)
    arrived = swap(prefix, "c")
    zero = jnp.zeros((), jnp.bfloat16)
    mine = jnp.where(is_owner, prefix[:half], jnp.where(is_other_core, arrived[half:], zero))
    pieces = lax.all_to_all(mine.reshape(parts, half // parts, -1), PLANE, 0, 0)
    piece = jnp.sum(pieces, axis=0)
    piece = piece + swap(piece, "zh")
    piece, beside = lax.optimization_barrier((piece, beside))
    copies = lax.axis_size("yl") * parts
    gathered = lax.all_to_all(jnp.broadcast_to(piece[None], (copies, *piece.shape)), SPREAD, 0, 0)
    gathered = gathered.reshape(lax.axis_size("yl"), -1, gathered.shape[2])
    return gathered, swap(gathered, "c"), beside


def local(queries, resp_kv, prefix_kv, owner, seg_len):
    at = {axis: lax.axis_index(axis) for axis in SECTION + RESP}
    place = jnp.int32(0)
    for axis in RESP:
        place = place * lax.axis_size(axis) + at[axis]
    owner_here = lax.dynamic_index_in_dim(owner[0], at["p"], 0, keepdims=False)
    micro = at["yl"] ^ at["yh"]
    where = jnp.stack([micro, at["yl"]]).astype(jnp.int32)

    def rows_of(which):
        arrays = (queries[0], resp_kv[0])
        return jnp.concatenate(
            [lax.dynamic_slice_in_dim(a, which * TOKM, TOKM, 0) for a in arrays], axis=1
        )

    own, theirs = rows_of(micro), rows_of(1 - micro)
    other = swap(theirs, "yl")
    kv0, kv1, other = spread_prefix(
        prefix_kv[0], owner_here == place, owner_here == (place ^ 1), other
    )

    fixed = (where, seg_len, own, other)
    (second,) = attend_pair(*fixed, None, kv0, kv1)
    carried = lax.ppermute(second, SECTION, [(0, 3), (1, 2)])
    first, second = attend_pair(*fixed, carried, kv0, kv1)

    is_second = at["yl"] == 1
    kept = jnp.where(is_second, second, first)
    got = swap(jnp.where(is_second, first, second), "yl")
    low = jnp.where(micro == 0, kept, got)
    high = jnp.where(micro == 0, got, kept)
    return jnp.concatenate([low, high], axis=0)[None]


def solution(mesh):
    fine = Mesh(mesh.devices.reshape(2, 2, PROMPTS, 2, 2, 4, 2), SECTION + RESP)
    return jax.shard_map(
        local,
        mesh=fine,
        in_specs=(
            P(SECTION, RESP, None),
            P(SECTION, RESP, None),
            P(SECTION, RESP, None),
            P(SECTION, None),
            P(RESP, None),
        ),
        out_specs=P(SECTION, RESP, None),
        check_vma=False,
    )
```

time: 198 us -> 83.7 us (0.42); the launches traced: 195 us -> 83.3 us
  waiting for transfers between devices: 139 us -> 31.1 us
  blocking collectives: 0 us -> 18.7 us
  matrix products: 11.5 us -> 0 us
  other arithmetic: 12.4 us -> 3.04 us
  Pallas kernels: 0 us -> 7.22 us
  local copies, waits for them, and re-layouts: 4.91 us -> 0.78 us
  starting transfers between devices: 24.9 us -> 21 us
    ppermute x9 -> x6, waiting for transfers between devices: 139 us -> 24.2 us  [the longest x5 14 us: swap(): return lax.ppermute(x, axis, [(0, 1), (1, 0)])]
    all_to_all x0 -> x1, blocking collectives: none -> 18.7 us  [spread_prefix(): lax.all_to_all(jnp.broadcast_to(piece[None], (copies, *piece.shape)), SPR...]
    dot_general x20 -> x0, matrix products: 11.5 us -> none  [the longest x5 4.84 us: attend(): jnp.einsum('euzm,meh->zeuh', distant_weights, distant_values, preferred_e...]
    ppermute x9 -> x6, starting transfers between devices: 24.9 us -> 15.2 us  [the longest x5 13.9 us: swap(): return lax.ppermute(x, axis, [(0, 1), (1, 0)])]
    pallas_call x0 -> x2, Pallas kernels: none -> 7.22 us  [attend_pair(): pl.pallas_call(pair_kernel, out_shape=outs, in_specs=[smem, smem] + [vmem...]
    all_to_all x0 -> x1, waiting for transfers between devices: none -> 6.94 us  [spread_prefix(): pieces = lax.all_to_all(mine.reshape(parts, half // parts, -1), PLANE, 0, 0)]
    all_to_all x0 -> x1, starting transfers between devices: none -> 5.79 us  [spread_prefix(): pieces = lax.all_to_all(mine.reshape(parts, half // parts, -1), PLANE, 0, 0)]
    reduce_sum x16 -> x1, other arithmetic: 4.65 us -> 0.08 us  [spread_prefix(): piece = jnp.sum(pieces, axis=0)]
  transfers between devices with their start and end apart: 9 -> 7, of which waited for: 8 -> 6; matrix products, arithmetic and copies ran while one was open for 2% -> 1% of each run, Pallas kernels for 0% -> 0%
where the time goes in v1:
time: 83.7 us; the launch traced here: 83.3 us
  waiting for transfers between devices  31.1 us (37%)
  starting transfers between devices  21 us (25%)
  blocking collectives  18.7 us (22%)
  Pallas kernels  7.22 us (9%)
  other arithmetic  3.04 us (4%)
  between operations  1.47 us (2%)
    all_to_all x1, blocking collectives, spread_prefix(): lax.all_to_all(jnp.broadcast_to(piece[None], (copies, *piece.shape)), SPR...  18.7 us
    ppermute x5, waiting for transfers between devices, swap(): return lax.ppermute(x, axis, [(0, 1), (1, 0)])  14 us
    ppermute x5, starting transfers between devices, swap(): return lax.ppermute(x, axis, [(0, 1), (1, 0)])  13.9 us
    ppermute x1, waiting for transfers between devices, local(): carried = lax.ppermute(second, SECTION, [(0, 3), (1, 2)])  10.2 us
    pallas_call x2, Pallas kernels, attend_pair(): pl.pallas_call(pair_kernel, out_shape=outs, in_specs=[smem, smem] + [vmem...  7.22 us
    all_to_all x1, waiting for transfers between devices, spread_prefix(): pieces = lax.all_to_all(mine.reshape(parts, half // parts, -1), PLANE, 0, 0)  6.94 us
    all_to_all x1, starting transfers between devices, spread_prefix(): pieces = lax.all_to_all(mine.reshape(parts, half // parts, -1), PLANE, 0, 0)  5.79 us
    select_n x1, other arithmetic, spread_prefix(): jnp.where(is_owner, prefix[:half], jnp.where(is_other_core, arrived[half:...  1.91 us
  transfers between devices with their start and end apart: 7, of which 6 were waited for; matrix products, arithmetic and copies ran while one was open for 1% of the time, Pallas kernels for 0%

profile of v1, /device:TPU:24, one launch (start us, length us, event | category | flops | bytes accessed | tf_op | source)
XLA Modules:
  0.0 83.3 jit_solution(2607671261081343381)
XLA Ops:
  0.0 0.0 copy-start
  0.0 2.0 %collective-permute-start = (bf16[512,1024]{1,0:T(8,128)(2,1)}, bf16[512,1024]{1,0:T(8,128)(2,1)S(1)}, u32[]{:S(2)}, u32[]{:S(2)}) collective-permute-start(bf16[512,1024]{1,0:T(8,128)(2,1)} %bitcast.21), channel_id=1, source_target_pairs={{0,1},{1,0},{2,3},{3,2},{4,5},{5,4},{6,7},{7,6},{8,9},{9,8},{10,11... | collective-permute-start | bytes 3145736 | tf_op jit(solution)/shard_map/ppermute | solution.py:30
  2.1 0.0 copy-done
  2.1 0.6 constant_dynamic-slice_fusion
  4.0 0.9 %collective-permute-done = bf16[512,1024]{1,0:T(8,128)(2,1)S(1)} collective-permute-done((bf16[512,1024]{1,0:T(8,128)(2,1)}, bf16[512,1024]{1,0:T(8,128)(2,1)S(1)}, u32[]{:S(2)}, u32[]{:S(2)}) %collective-permute-start) | collective-permute-done | bytes 1048608 | tf_op jit(solution)/shard_map/ppermute | solution.py:30
  4.9 1.9 %fusion = bf16[256,1024]{1,0:T(8,128)(2,1)} fusion(bf16[512,1024]{1,0:T(8,128)(2,1)S(1)} %collective-permute-done, bf16[1,512,1024]{2,1,0:T(8,128)(2,1)} %param.7, pred[]{:T(512)S(6)} %eq.16, pred[]{:T(512)S(6)} %eq.15), kind=kLoop, calls=%fused_computation.1 | loop fusion | flops 524288 | bytes 1572866 | tf_op jit(solution)/shard_map/jit(_where)/select_n | solution.py:140
  6.8 0.0 copy-start.3
  6.8 0.0 copy-start.2
  6.8 5.8 %all-to-all-start = ((bf16[8,32,1024]{2,1,0:T(8,128)(2,1)}), bf16[8,32,1024]{2,1,0:T(8,128)(2,1)S(1)}, u32[]{:S(2)}, u32[]{:S(2)}) async-start(bf16[8,32,1024]{2,1,0:T(8,128)(2,1)} %bitcast.7), calls=%async_computation | async-start | bytes 1048576 | tf_op jit(solution)/shard_map/all_to_all | solution.py:141
  12.6 0.0 copy-done.3
  12.6 0.0 copy-done.2
  12.7 2.7 %collective-permute-start.2 = (bf16[32,5120]{1,0:T(8,128)(2,1)S(1)}, bf16[32,5120]{1,0:T(8,128)(2,1)S(1)}, u32[]{:S(2)}, u32[]{:S(2)}) collective-permute-start(bf16[32,5120]{1,0:T(8,128)(2,1)S(1)} %pad_maximum_fusion.1), channel_id=1, source_target_pairs={{0,128},{128,0},{1,129},{129,1},{2,130},{130,2},{3,131},{131,3},{4... | collective-permute-start | bytes 983048 | tf_op jit(solution)/shard_map/ppermute | solution.py:30
  15.4 6.9 %all-to-all-done = bf16[8,32,1024]{2,1,0:T(8,128)(2,1)S(1)} async-done(((bf16[8,32,1024]{2,1,0:T(8,128)(2,1)}), bf16[8,32,1024]{2,1,0:T(8,128)(2,1)S(1)}, u32[]{:S(2)}, u32[]{:S(2)}) %all-to-all-start) | async-done | bytes 524320 | tf_op jit(solution)/shard_map/all_to_all | solution.py:141
  22.3 0.1 reduce_sum.12
  22.4 5.2 %collective-permute-start.1 = (bf16[32,1024]{1,0:T(8,128)(2,1)S(1)}, bf16[32,1024]{1,0:T(8,128)(2,1)S(1)}, u32[]{:S(2)}, u32[]{:S(2)}) collective-permute-start(bf16[32,1024]{1,0:T(8,128)(2,1)S(1)} %reduce_sum.12), channel_id=1, source_target_pairs={{0,16},{16,0},{1,17},{17,1},{2,18},{18,2},{3,19},{19,3},{4,20},{20... | collective-permute-start | bytes 196616 | tf_op jit(solution)/shard_map/ppermute | solution.py:30
  27.6 3.3 %collective-permute-done.1 = bf16[32,1024]{1,0:T(8,128)(2,1)S(1)} collective-permute-done((bf16[32,1024]{1,0:T(8,128)(2,1)S(1)}, bf16[32,1024]{1,0:T(8,128)(2,1)S(1)}, u32[]{:S(2)}, u32[]{:S(2)}) %collective-permute-start.1) | collective-permute-done | bytes 65568 | tf_op jit(solution)/shard_map/ppermute | solution.py:30
  30.9 0.0 collective-permute-done.2.other_ref
  30.9 0.1 broadcast_in_dim.14
  31.0 18.7 %all_to_all.10 = bf16[16,32,1024]{2,1,0:T(8,128)(2,1)S(1)} all-to-all(bf16[16,32,1024]{2,1,0:T(8,128)(2,1)S(1)} %broadcast_in_dim.14), channel_id=1, replica_groups=mesh['yh'=2,'yl'=2,'p'=4,'zh'=2,'zl'=2,'x'=4,'c'=2] {'yl','zl','x'}, dimensions={0} | all-to-all | bytes 2097152 | tf_op jit(solution)/shard_map/all_to_all | solution.py:146
  49.7 1.9 %collective-permute-start.3 = (bf16[2,256,1024]{2,1,0:T(8,128)(2,1)S(1)}, bf16[2,256,1024]{2,1,0:T(8,128)(2,1)S(1)}, u32[]{:S(2)}, u32[]{:S(2)}) collective-permute-start(bf16[2,256,1024]{2,1,0:T(8,128)(2,1)S(1)} %bitcast.18), channel_id=1, source_target_pairs={{0,1},{1,0},{2,3},{3,2},{4,5},{5,4},{6,7},{7,6},{8,9},{9,8},{10,11... | collective-permute-start | bytes 3145736 | tf_op jit(solution)/shard_map/ppermute | solution.py:30
  51.7 0.1 pad_add_fusion.place_ref
  51.7 0.0 copy-start.1
  51.8 2.5 %collective-permute-done.3.refs_1_.refs_2_ = bf16[2,256,1024]{2,1,0:T(8,128)(2,1)S(1)} collective-permute-done((bf16[2,256,1024]{2,1,0:T(8,128)(2,1)S(1)}, bf16[2,256,1024]{2,1,0:T(8,128)(2,1)S(1)}, u32[]{:S(2)}, u32[]{:S(2)}) %collective-permute-start.3) | collective-permute-done | bytes 1048608 | tf_op jit(solution)/shard_map/ppermute | solution.py:30
  54.3 0.0 copy-done.1
  54.3 3.6 %shard_map.55 = bf16[32,4096]{1,0:T(8,128)(2,1)S(1)} custom-call(s32[2]{0:T(128)S(1)} %pad_add_fusion.place_ref, s32[2,4]{1,0:T(2,128)S(1)} %copy-done.1, bf16[32,5120]{1,0:T(8,128)(2,1)S(1)} %pad_maximum_fusion.own_ref, bf16[32,5120]{1,0:T(8,128)(2,1)S(1)} %collective-permute-done.2.other_ref, bf16[2,256,1024]{2,1,0:T(8,128)(2,1)S(1)} %bitcast.19, ...), custom_call_target="tpu_custom_call" | custom-call | flops 570425344 | bytes 4194304 | tf_op jit(solution)/shard_map/pallas_call | solution.py:120
  57.9 1.3 %collective-permute-start.4 = (bf16[32,4096]{1,0:T(8,128)(2,1)S(1)}, bf16[32,4096]{1,0:T(8,128)(2,1)S(1)}, u32[]{:S(2)}, u32[]{:S(2)}) collective-permute-start(bf16[32,4096]{1,0:T(8,128)(2,1)S(1)} %shard_map.55), channel_id=1, source_target_pairs={{0,384},{128,256},{1,385},{129,257},{2,386},{130,258},{3,387},{131... | collective-permute-start | bytes 786440 | tf_op jit(solution)/shard_map/ppermute | solution.py:174
  59.2 10.2 %collective-permute-done.4.refs_0_ = bf16[32,4096]{1,0:T(8,128)(2,1)S(1)} collective-permute-done((bf16[32,4096]{1,0:T(8,128)(2,1)S(1)}, bf16[32,4096]{1,0:T(8,128)(2,1)S(1)}, u32[]{:S(2)}, u32[]{:S(2)}) %collective-permute-start.4) | collective-permute-done | bytes 262176 | tf_op jit(solution)/shard_map/ppermute | solution.py:174
  69.3 3.6 %shard_map.56 = (bf16[32,4096]{1,0:T(8,128)(2,1)S(1)}, bf16[32,4096]{1,0:T(8,128)(2,1)S(1)}) custom-call(s32[2]{0:T(128)S(1)} %pad_add_fusion.place_ref, s32[2,4]{1,0:T(2,128)S(1)} %copy-done.1, bf16[32,5120]{1,0:T(8,128)(2,1)S(1)} %pad_maximum_fusion.own_ref, bf16[32,5120]{1,0:T(8,128)(2,1)S(1)} %collective-permute-done.2.other_ref, ...), custom_call_target="tpu_custom_call" | custom-call | flops 570425344 | bytes 4194304 | tf_op jit(solution)/shard_map/pallas_call | solution.py:120
  73.0 2.2 %collective-permute-start.5 = (bf16[32,4096]{1,0:T(8,128)(2,1)S(1)}, bf16[32,4096]{1,0:T(8,128)(2,1)S(1)}, u32[]{:S(2)}, u32[]{:S(2)}) collective-permute-start(bf16[32,4096]{1,0:T(8,128)(2,1)S(1)} %broadcast_select_fusion), channel_id=1, source_target_pairs={{0,128},{128,0},{1,129},{129,1},{2,130},{130,2},{3,131},{131,3},{4... | collective-permute-start | bytes 786440 | tf_op jit(solution)/shard_map/ppermute | solution.py:30
  75.2 7.2 %collective-permute-done.5 = bf16[32,4096]{1,0:T(8,128)(2,1)S(1)} collective-permute-done((bf16[32,4096]{1,0:T(8,128)(2,1)S(1)}, bf16[32,4096]{1,0:T(8,128)(2,1)S(1)}, u32[]{:S(2)}, u32[]{:S(2)}) %collective-permute-start.5) | collective-permute-done | bytes 262176 | tf_op jit(solution)/shard_map/ppermute | solution.py:30
  82.5 0.8 maximum_bitcast_fusion
  (7 shorter events, 0.2 us)
Async XLA Ops:
  0.0 2.1 %copy-start = (s32[1,4]{1,0:T(1,128)S(1)}, s32[1,4]{1,0:T(1,128)}, u32[]{:S(2)}) copy-start(s32[1,4]{1,0:T(1,128)} %param.8) | copy-start | bytes 52
  0.0 4.9 %collective-permute-start = (bf16[512,1024]{1,0:T(8,128)(2,1)}, bf16[512,1024]{1,0:T(8,128)(2,1)S(1)}, u32[]{:S(2)}, u32[]{:S(2)}) collective-permute-start(bf16[512,1024]{1,0:T(8,128)(2,1)} %bitcast.21), channel_id=1, source_target_pairs={{0,1},{1,0},{2,3},{3,2},{4,5},{5,4},{6,7},{7,6},{8,9},{9,8},{10,11... | collective-permute-start | bytes 3145736 | tf_op jit(solution)/shard_map/ppermute | solution.py:30
  6.8 5.8 %copy-start.3 = (bf16[1,64,1024]{2,1,0:T(8,128)(2,1)S(1)}, bf16[1,64,1024]{2,1,0:T(8,128)(2,1)}, u32[]{:S(2)}) copy-start(bf16[1,64,1024]{2,1,0:T(8,128)(2,1)} %param.6) | copy-start | bytes 393220
  6.8 5.8 %copy-start.2 = (bf16[1,64,4096]{2,1,0:T(8,128)(2,1)S(1)}, bf16[1,64,4096]{2,1,0:T(8,128)(2,1)}, u32[]{:S(2)}) copy-start(bf16[1,64,4096]{2,1,0:T(8,128)(2,1)} %param.5) | copy-start | bytes 1572868
  6.8 15.5 %all-to-all-start = ((bf16[8,32,1024]{2,1,0:T(8,128)(2,1)}), bf16[8,32,1024]{2,1,0:T(8,128)(2,1)S(1)}, u32[]{:S(2)}, u32[]{:S(2)}) async-start(bf16[8,32,1024]{2,1,0:T(8,128)(2,1)} %bitcast.7), calls=%async_computation | async-start | bytes 1048576 | tf_op jit(solution)/shard_map/all_to_all | solution.py:141
  12.7 18.2 %collective-permute-start.2 = (bf16[32,5120]{1,0:T(8,128)(2,1)S(1)}, bf16[32,5120]{1,0:T(8,128)(2,1)S(1)}, u32[]{:S(2)}, u32[]{:S(2)}) collective-permute-start(bf16[32,5120]{1,0:T(8,128)(2,1)S(1)} %pad_maximum_fusion.1), channel_id=1, source_target_pairs={{0,128},{128,0},{1,129},{129,1},{2,130},{130,2},{3,131},{131,3},{4... | collective-permute-start | bytes 983048 | tf_op jit(solution)/shard_map/ppermute | solution.py:30
  22.4 8.5 %collective-permute-start.1 = (bf16[32,1024]{1,0:T(8,128)(2,1)S(1)}, bf16[32,1024]{1,0:T(8,128)(2,1)S(1)}, u32[]{:S(2)}, u32[]{:S(2)}) collective-permute-start(bf16[32,1024]{1,0:T(8,128)(2,1)S(1)} %reduce_sum.12), channel_id=1, source_target_pairs={{0,16},{16,0},{1,17},{17,1},{2,18},{18,2},{3,19},{19,3},{4,20},{20... | collective-permute-start | bytes 196616 | tf_op jit(solution)/shard_map/ppermute | solution.py:30
  49.7 4.5 %collective-permute-start.3 = (bf16[2,256,1024]{2,1,0:T(8,128)(2,1)S(1)}, bf16[2,256,1024]{2,1,0:T(8,128)(2,1)S(1)}, u32[]{:S(2)}, u32[]{:S(2)}) collective-permute-start(bf16[2,256,1024]{2,1,0:T(8,128)(2,1)S(1)} %bitcast.18), channel_id=1, source_target_pairs={{0,1},{1,0},{2,3},{3,2},{4,5},{5,4},{6,7},{7,6},{8,9},{9,8},{10,11... | collective-permute-start | bytes 3145736 | tf_op jit(solution)/shard_map/ppermute | solution.py:30
  51.7 2.6 %copy-start.1 = (s32[2,4]{1,0:T(2,128)S(1)}, s32[2,4]{1,0:T(2,128)}, u32[]{:S(2)}) copy-start(s32[2,4]{1,0:T(2,128)} %seg_ref.3) | copy-start | bytes 100
  57.9 11.5 %collective-permute-start.4 = (bf16[32,4096]{1,0:T(8,128)(2,1)S(1)}, bf16[32,4096]{1,0:T(8,128)(2,1)S(1)}, u32[]{:S(2)}, u32[]{:S(2)}) collective-permute-start(bf16[32,4096]{1,0:T(8,128)(2,1)S(1)} %shard_map.55), channel_id=1, source_target_pairs={{0,384},{128,256},{1,385},{129,257},{2,386},{130,258},{3,387},{131... | collective-permute-start | bytes 786440 | tf_op jit(solution)/shard_map/ppermute | solution.py:174
  73.0 9.4 %collective-permute-start.5 = (bf16[32,4096]{1,0:T(8,128)(2,1)S(1)}, bf16[32,4096]{1,0:T(8,128)(2,1)S(1)}, u32[]{:S(2)}, u32[]{:S(2)}) collective-permute-start(bf16[32,4096]{1,0:T(8,128)(2,1)S(1)} %broadcast_select_fusion), channel_id=1, source_target_pairs={{0,128},{128,0},{1,129},{129,1},{2,130},{130,2},{3,131},{131,3},{4... | collective-permute-start | bytes 786440 | tf_op jit(solution)/shard_map/ppermute | solution.py:30

commit v2 on v1

--- a/solution.py
+++ b/solution.py
@@ -64,21 +64,27 @@
     return lax.rsqrt(total * (1.0 / WIDTH) + EPS)
 
 
-def pair_kernel(place_ref, seg_ref, own_ref, other_ref, *refs):
+def place_in_pair():
+    second = lax.axis_index("yl")
+    return second ^ lax.axis_index("yh"), second
+
+
+def pair_kernel(seg_ref, own_ref, other_ref, *refs):
     if len(refs) == 6:
         carried_ref, kv0_ref, kv1_ref, a_ref, b_ref, att_ref = refs
         carried = carried_ref[...].astype(jnp.float32)
     else:
         kv0_ref, kv1_ref, b_ref, a_ref, att_ref = refs
         carried = 0.0
-    micro, second = place_ref[0], place_ref[1]
+    micro, second = place_in_pair()
 
     at_key = lax.broadcasted_iota(jnp.int32, (TOKM, TOKM), 0)
     at_query = lax.broadcasted_iota(jnp.int32, (TOKM, TOKM), 1)
     of_key, of_query = jnp.zeros_like(at_key), jnp.zeros_like(at_query)
-    end = jnp.int32(0)
+    lengths = seg_ref[pl.ds(micro, 1), :]
+    end = jnp.zeros((1, 1), jnp.int32)
     for i in range(RESPS):
-        end = end + seg_ref[micro, i]
+        end = end + lengths[:, i : i + 1]
         of_key = of_key + (at_key >= end).astype(jnp.int32)
         of_query = of_query + (at_query >= end).astype(jnp.int32)
     allowed = (of_key == of_query) & (at_key <= at_query)
@@ -108,9 +114,8 @@
             carried = a_ref[...].astype(jnp.float32)
 
 
-def attend_pair(place, seg_len, own, other, carried, kv0, kv1):
+def attend_pair(seg_len, own, other, carried, kv0, kv1):
     vmem = pl.BlockSpec(memory_space=pltpu.VMEM)
-    smem = pl.BlockSpec(memory_space=pltpu.SMEM)
     out = jax.ShapeDtypeStruct((TOKM, WIDTH), jnp.bfloat16)
     scratch = [pltpu.VMEM((KVH, HEAD_SIZE, GROUP * TOKM), jnp.float32)]
     if carried is None:
@@ -120,7 +125,7 @@
     return pl.pallas_call(
         pair_kernel,
         out_shape=outs,
-        in_specs=[smem, smem] + [vmem] * (4 + len(middle)),
+        in_specs=[vmem] * (5 + len(middle)),
         out_specs=(vmem,) * len(outs),
         scratch_shapes=scratch,
         compiler_params=pltpu.CompilerParams(vmem_limit_bytes=12 * 1024 * 1024),
@@ -129,15 +134,15 @@
             bytes_accessed=4 * 1024 * 1024,
             transcendentals=2 * HQ * TOKM * (PLEN + TOKM),
         ),
-    )(place, seg_len, own, other, *middle, kv0, kv1)
+    )(seg_len, own, other, *middle, kv0, kv1)
 
 
 def spread_prefix(prefix, is_owner, is_other_core, beside):
     half = PLEN // 2
     parts = math.prod(lax.axis_size(axis) for axis in PLANE)
-    arrived = swap(prefix, "c")
+    arrived = swap(prefix[half:], "c")
     zero = jnp.zeros((), jnp.bfloat16)
-    mine = jnp.where(is_owner, prefix[:half], jnp.where(is_other_core, arrived[half:], zero))
+    mine = jnp.where(is_owner, prefix[:half], jnp.where(is_other_core, arrived, zero))
     pieces = lax.all_to_all(mine.reshape(parts, half // parts, -1), PLANE, 0, 0)
     piece = jnp.sum(pieces, axis=0)
     piece = piece + swap(piece, "zh")
@@ -154,8 +159,7 @@
     for axis in RESP:
         place = place * lax.axis_size(axis) + at[axis]
     owner_here = lax.dynamic_index_in_dim(owner[0], at["p"], 0, keepdims=False)
-    micro = at["yl"] ^ at["yh"]
-    where = jnp.stack([micro, at["yl"]]).astype(jnp.int32)
+    micro, second = place_in_pair()
 
     def rows_of(which):
         arrays = (queries[0], resp_kv[0])
@@ -169,14 +173,13 @@
         prefix_kv[0], owner_here == place, owner_here == (place ^ 1), other
     )
 
-    fixed = (where, seg_len, own, other)
-    (second,) = attend_pair(*fixed, None, kv0, kv1)
-    carried = lax.ppermute(second, SECTION, [(0, 3), (1, 2)])
-    first, second = attend_pair(*fixed, carried, kv0, kv1)
-
-    is_second = at["yl"] == 1
-    kept = jnp.where(is_second, second, first)
-    got = swap(jnp.where(is_second, first, second), "yl")
+    fixed = (seg_len, own, other)
+    (last,) = attend_pair(*fixed, None, kv0, kv1)
+    carried = lax.ppermute(last, SECTION, [(0, 3), (1, 2)])
+    first, last = attend_pair(*fixed, carried, kv0, kv1)
+
+    kept = jnp.where(second == 1, last, first)
+    got = swap(jnp.where(second == 1, first, last), "yl")
     low = jnp.where(micro == 0, kept, got)
     high = jnp.where(micro == 0, got, kept)
     return jnp.concatenate([low, high], axis=0)[None]

time: 83.7 us -> 82.4 us (0.984)
  local copies, waits for them, and re-layouts: 0.78 us -> 1.95 us
  other arithmetic: 3.04 us -> 1.91 us
  Pallas kernels: 7.22 us -> 6.18 us
    slice x0 -> x1, local copies, waits for them, and re-layouts: none -> 1.16 us  [spread_prefix(): arrived = swap(prefix[half:], 'c')]
    select_n x2, other arithmetic: 1.94 us -> 0.88 us  [the longest x1 0.85 us: spread_prefix(): jnp.where(is_owner, prefix[:half], jnp.where(is_other_core, arrived, zero))]
    pallas_call x2, Pallas kernels: 7.22 us -> 6.18 us  [attend_pair(): pl.pallas_call(pair_kernel, out_shape=outs, in_specs=[vmem] * (5 + len(mi...]
  transfers between devices with their start and end apart: 7 -> 7, of which waited for: 6 -> 5; matrix products, arithmetic and copies ran while one was open for 1% -> 1% of each run, Pallas kernels for 0% -> 0%
where the time goes in v2:
time: 82.4 us; the launch traced here: 82 us
  waiting for transfers between devices  31 us (38%)
  starting transfers between devices  20.8 us (25%)
  blocking collectives  18.7 us (23%)
  Pallas kernels  6.18 us (7%)
  local copies, waits for them, and re-layouts  1.95 us (2%)
  other arithmetic  1.91 us (2%)
  between operations  1.5 us (2%)
    all_to_all x1, blocking collectives, spread_prefix(): lax.all_to_all(jnp.broadcast_to(piece[None], (copies, *piece.shape)), SPR...  18.7 us
    ppermute x5, starting transfers between devices, swap(): return lax.ppermute(x, axis, [(0, 1), (1, 0)])  13.7 us
    ppermute x5, waiting for transfers between devices, swap(): return lax.ppermute(x, axis, [(0, 1), (1, 0)])  13.5 us
    ppermute x1, waiting for transfers between devices, local(): carried = lax.ppermute(last, SECTION, [(0, 3), (1, 2)])  10.3 us
    all_to_all x1, waiting for transfers between devices, spread_prefix(): pieces = lax.all_to_all(mine.reshape(parts, half // parts, -1), PLANE, 0, 0)  7.31 us
    pallas_call x2, Pallas kernels, attend_pair(): pl.pallas_call(pair_kernel, out_shape=outs, in_specs=[vmem] * (5 + len(mi...  6.18 us
    all_to_all x1, starting transfers between devices, spread_prefix(): pieces = lax.all_to_all(mine.reshape(parts, half // parts, -1), PLANE, 0, 0)  5.79 us
  transfers between devices with their start and end apart: 7, of which 5 were waited for; matrix products, arithmetic and copies ran while one was open for 1% of the time, Pallas kernels for 0%

profile of v2, /device:TPU:24, one launch (start us, length us, event | category | flops | bytes accessed | tf_op | source)
XLA Modules:
  0.0 82.0 jit_solution(11409267920233507943)
XLA Ops:
  0.0 0.0 copy-start
  0.0 0.0 copy-start.2
  0.0 1.2 %slice_bitcast_fusion = bf16[256,1024]{1,0:T(8,128)(2,1)S(1)} fusion(bf16[1,512,1024]{2,1,0:T(8,128)(2,1)} %param.7), kind=kLoop, calls=%fused_computation.2 | loop fusion | bytes 1048576 | tf_op jit(solution)/shard_map/slice | solution.py:143
  1.2 1.9 %collective-permute-start = (bf16[256,1024]{1,0:T(8,128)(2,1)S(1)}, bf16[256,1024]{1,0:T(8,128)(2,1)S(1)}, u32[]{:S(2)}, u32[]{:S(2)}) collective-permute-start(bf16[256,1024]{1,0:T(8,128)(2,1)S(1)} %slice_bitcast_fusion), channel_id=1, source_target_pairs={{0,1},{1,0},{2,3},{3,2},{4,5},{5,4},{6,7},{7,6},{8,9},{9,8},{10,11... | collective-permute-start | bytes 1572872 | tf_op jit(solution)/shard_map/ppermute | solution.py:30
  3.1 0.0 copy-done
  3.1 0.6 constant_dynamic-slice_fusion
  5.0 0.0 collective-permute-done
  5.0 0.0 copy-done.2
  5.0 0.9 %bitcast_select_fusion = bf16[256,1024]{1,0:T(8,128)(2,1)} fusion(bf16[256,1024]{1,0:T(8,128)(2,1)S(1)} %collective-permute-done, bf16[1,512,1024]{2,1,0:T(8,128)(2,1)S(1)} %copy-done.2, pred[]{:T(512)S(6)} %eq.17, pred[]{:T(512)S(6)} %eq.16), kind=kLoop, calls=%fused_computation.1 | loop fusion | flops 524288 | bytes 1572866 | tf_op jit(solution)/shard_map/jit(_where)/select_n | solution.py:145
  5.9 0.0 copy-start.4
  5.9 0.0 copy-start.3
  5.9 5.8 %all-to-all-start = ((bf16[8,32,1024]{2,1,0:T(8,128)(2,1)}), bf16[8,32,1024]{2,1,0:T(8,128)(2,1)S(1)}, u32[]{:S(2)}, u32[]{:S(2)}) async-start(bf16[8,32,1024]{2,1,0:T(8,128)(2,1)} %bitcast.5), calls=%async_computation | async-start | bytes 1048576 | tf_op jit(solution)/shard_map/all_to_all | solution.py:146
  11.7 0.0 copy-done.4
  11.7 0.0 copy-done.3
  11.8 2.7 %collective-permute-start.2 = (bf16[32,5120]{1,0:T(8,128)(2,1)S(1)}, bf16[32,5120]{1,0:T(8,128)(2,1)S(1)}, u32[]{:S(2)}, u32[]{:S(2)}) collective-permute-start(bf16[32,5120]{1,0:T(8,128)(2,1)S(1)} %pad_maximum_fusion.1), channel_id=1, source_target_pairs={{0,128},{128,0},{1,129},{129,1},{2,130},{130,2},{3,131},{131,3},{4... | collective-permute-start | bytes 983048 | tf_op jit(solution)/shard_map/ppermute | solution.py:30
  14.5 7.3 %all-to-all-done = bf16[8,32,1024]{2,1,0:T(8,128)(2,1)S(1)} async-done(((bf16[8,32,1024]{2,1,0:T(8,128)(2,1)}), bf16[8,32,1024]{2,1,0:T(8,128)(2,1)S(1)}, u32[]{:S(2)}, u32[]{:S(2)}) %all-to-all-start) | async-done | bytes 524320 | tf_op jit(solution)/shard_map/all_to_all | solution.py:146
  21.8 0.1 reduce_sum.12
  21.8 5.2 %collective-permute-start.1 = (bf16[32,1024]{1,0:T(8,128)(2,1)S(1)}, bf16[32,1024]{1,0:T(8,128)(2,1)S(1)}, u32[]{:S(2)}, u32[]{:S(2)}) collective-permute-start(bf16[32,1024]{1,0:T(8,128)(2,1)S(1)} %reduce_sum.12), channel_id=1, source_target_pairs={{0,16},{16,0},{1,17},{17,1},{2,18},{18,2},{3,19},{19,3},{4,20},{20... | collective-permute-start | bytes 196616 | tf_op jit(solution)/shard_map/ppermute | solution.py:30
  27.0 3.4 %collective-permute-done.1 = bf16[32,1024]{1,0:T(8,128)(2,1)S(1)} collective-permute-done((bf16[32,1024]{1,0:T(8,128)(2,1)S(1)}, bf16[32,1024]{1,0:T(8,128)(2,1)S(1)}, u32[]{:S(2)}, u32[]{:S(2)}) %collective-permute-start.1) | collective-permute-done | bytes 65568 | tf_op jit(solution)/shard_map/ppermute | solution.py:30
  30.4 0.0 collective-permute-done.2.other_ref
  30.4 0.1 broadcast_in_dim.14
  30.5 18.7 %all_to_all.10 = bf16[16,32,1024]{2,1,0:T(8,128)(2,1)S(1)} all-to-all(bf16[16,32,1024]{2,1,0:T(8,128)(2,1)S(1)} %broadcast_in_dim.14), channel_id=1, replica_groups=mesh['yh'=2,'yl'=2,'p'=4,'zh'=2,'zl'=2,'x'=4,'c'=2] {'yl','zl','x'}, dimensions={0} | all-to-all | bytes 2097152 | tf_op jit(solution)/shard_map/all_to_all | solution.py:151
  49.2 1.9 %collective-permute-start.3 = (bf16[2,256,1024]{2,1,0:T(8,128)(2,1)S(1)}, bf16[2,256,1024]{2,1,0:T(8,128)(2,1)S(1)}, u32[]{:S(2)}, u32[]{:S(2)}) collective-permute-start(bf16[2,256,1024]{2,1,0:T(8,128)(2,1)S(1)} %bitcast.17), channel_id=1, source_target_pairs={{0,1},{1,0},{2,3},{3,2},{4,5},{5,4},{6,7},{7,6},{8,9},{9,8},{10,11... | collective-permute-start | bytes 3145736 | tf_op jit(solution)/shard_map/ppermute | solution.py:30
  51.2 0.0 copy-start.1
  51.2 2.6 %collective-permute-done.3.refs_1_.refs_2_ = bf16[2,256,1024]{2,1,0:T(8,128)(2,1)S(1)} collective-permute-done((bf16[2,256,1024]{2,1,0:T(8,128)(2,1)S(1)}, bf16[2,256,1024]{2,1,0:T(8,128)(2,1)S(1)}, u32[]{:S(2)}, u32[]{:S(2)}) %collective-permute-start.3) | collective-permute-done | bytes 1048608 | tf_op jit(solution)/shard_map/ppermute | solution.py:30
  53.8 0.0 copy-done.1
  53.8 3.1 %shard_map.55 = bf16[32,4096]{1,0:T(8,128)(2,1)S(1)} custom-call(s32[2,4]{1,0:T(2,128)S(1)} %copy-done.1, bf16[32,5120]{1,0:T(8,128)(2,1)S(1)} %pad_maximum_fusion.own_ref, bf16[32,5120]{1,0:T(8,128)(2,1)S(1)} %collective-permute-done.2.other_ref, bf16[2,256,1024]{2,1,0:T(8,128)(2,1)S(1)} %bitcast.18, ...), custom_call_target="tpu_custom_call" | custom-call | flops 570425344 | bytes 4194304 | tf_op jit(solution)/shard_map/pallas_call | solution.py:125
  56.9 1.3 %collective-permute-start.4 = (bf16[32,4096]{1,0:T(8,128)(2,1)S(1)}, bf16[32,4096]{1,0:T(8,128)(2,1)S(1)}, u32[]{:S(2)}, u32[]{:S(2)}) collective-permute-start(bf16[32,4096]{1,0:T(8,128)(2,1)S(1)} %shard_map.55), channel_id=1, source_target_pairs={{0,384},{128,256},{1,385},{129,257},{2,386},{130,258},{3,387},{131... | collective-permute-start | bytes 786440 | tf_op jit(solution)/shard_map/ppermute | solution.py:178
  58.2 10.3 %collective-permute-done.4.refs_0_ = bf16[32,4096]{1,0:T(8,128)(2,1)S(1)} collective-permute-done((bf16[32,4096]{1,0:T(8,128)(2,1)S(1)}, bf16[32,4096]{1,0:T(8,128)(2,1)S(1)}, u32[]{:S(2)}, u32[]{:S(2)}) %collective-permute-start.4) | collective-permute-done | bytes 262176 | tf_op jit(solution)/shard_map/ppermute | solution.py:178
  68.5 3.1 %shard_map.56 = (bf16[32,4096]{1,0:T(8,128)(2,1)S(1)}, bf16[32,4096]{1,0:T(8,128)(2,1)S(1)}) custom-call(s32[2,4]{1,0:T(2,128)S(1)} %copy-done.1, bf16[32,5120]{1,0:T(8,128)(2,1)S(1)} %pad_maximum_fusion.own_ref, bf16[32,5120]{1,0:T(8,128)(2,1)S(1)} %collective-permute-done.2.other_ref, bf16[32,4096]{1,0:T(8,128)(2,1)S(1)} %collective-permute-done.4.refs_0_, ...), custom_call_target="tpu_custom_call" | custom-call | flops 570425344 | bytes 4194304 | tf_op jit(solution)/shard_map/pallas_call | solution.py:125
  71.6 2.0 %collective-permute-start.5 = (bf16[32,4096]{1,0:T(8,128)(2,1)S(1)}, bf16[32,4096]{1,0:T(8,128)(2,1)S(1)}, u32[]{:S(2)}, u32[]{:S(2)}) collective-permute-start(bf16[32,4096]{1,0:T(8,128)(2,1)S(1)} %broadcast_select_fusion), channel_id=1, source_target_pairs={{0,128},{128,0},{1,129},{129,1},{2,130},{130,2},{3,131},{131,3},{4... | collective-permute-start | bytes 786440 | tf_op jit(solution)/shard_map/ppermute | solution.py:30
  73.6 7.5 %collective-permute-done.5 = bf16[32,4096]{1,0:T(8,128)(2,1)S(1)} collective-permute-done((bf16[32,4096]{1,0:T(8,128)(2,1)S(1)}, bf16[32,4096]{1,0:T(8,128)(2,1)S(1)}, u32[]{:S(2)}, u32[]{:S(2)}) %collective-permute-start.5) | collective-permute-done | bytes 262176 | tf_op jit(solution)/shard_map/ppermute | solution.py:30
  81.2 0.8 %maximum_bitcast_fusion = bf16[1,64,4096]{2,1,0:T(8,128)(2,1)} fusion(bf16[32,4096]{1,0:T(8,128)(2,1)S(1)} %get-tuple-element.14, bf16[32,4096]{1,0:T(8,128)(2,1)S(1)} %get-tuple-element.13), kind=kLoop, calls=%fused_computation | loop fusion | flops 1048576 | bytes 1048576 | tf_op jit(solution)/shard_map/broadcast_in_dim | solution.py:185
  (7 shorter events, 0.2 us)
Async XLA Ops:
  0.0 3.1 %copy-start = (s32[1,4]{1,0:T(1,128)S(1)}, s32[1,4]{1,0:T(1,128)}, u32[]{:S(2)}) copy-start(s32[1,4]{1,0:T(1,128)} %param.8) | copy-start | bytes 52
  0.0 5.0 %copy-start.2 = (bf16[1,512,1024]{2,1,0:T(8,128)(2,1)S(1)}, bf16[1,512,1024]{2,1,0:T(8,128)(2,1)}, u32[]{:S(2)}) copy-start(bf16[1,512,1024]{2,1,0:T(8,128)(2,1)} %param.7) | copy-start | bytes 3145732
  1.2 3.8 %collective-permute-start = (bf16[256,1024]{1,0:T(8,128)(2,1)S(1)}, bf16[256,1024]{1,0:T(8,128)(2,1)S(1)}, u32[]{:S(2)}, u32[]{:S(2)}) collective-permute-start(bf16[256,1024]{1,0:T(8,128)(2,1)S(1)} %slice_bitcast_fusion), channel_id=1, source_target_pairs={{0,1},{1,0},{2,3},{3,2},{4,5},{5,4},{6,7},{7,6},{8,9},{9,8},{10,11... | collective-permute-start | bytes 1572872 | tf_op jit(solution)/shard_map/ppermute | solution.py:30
  5.9 5.8 %copy-start.4 = (bf16[1,64,1024]{2,1,0:T(8,128)(2,1)S(1)}, bf16[1,64,1024]{2,1,0:T(8,128)(2,1)}, u32[]{:S(2)}) copy-start(bf16[1,64,1024]{2,1,0:T(8,128)(2,1)} %param.6) | copy-start | bytes 393220
  5.9 5.8 %copy-start.3 = (bf16[1,64,4096]{2,1,0:T(8,128)(2,1)S(1)}, bf16[1,64,4096]{2,1,0:T(8,128)(2,1)}, u32[]{:S(2)}) copy-start(bf16[1,64,4096]{2,1,0:T(8,128)(2,1)} %param.5) | copy-start | bytes 1572868
  5.9 15.9 %all-to-all-start = ((bf16[8,32,1024]{2,1,0:T(8,128)(2,1)}), bf16[8,32,1024]{2,1,0:T(8,128)(2,1)S(1)}, u32[]{:S(2)}, u32[]{:S(2)}) async-start(bf16[8,32,1024]{2,1,0:T(8,128)(2,1)} %bitcast.5), calls=%async_computation | async-start | bytes 1048576 | tf_op jit(solution)/shard_map/all_to_all | solution.py:146
  11.8 18.6 %collective-permute-start.2 = (bf16[32,5120]{1,0:T(8,128)(2,1)S(1)}, bf16[32,5120]{1,0:T(8,128)(2,1)S(1)}, u32[]{:S(2)}, u32[]{:S(2)}) collective-permute-start(bf16[32,5120]{1,0:T(8,128)(2,1)S(1)} %pad_maximum_fusion.1), channel_id=1, source_target_pairs={{0,128},{128,0},{1,129},{129,1},{2,130},{130,2},{3,131},{131,3},{4... | collective-permute-start | bytes 983048 | tf_op jit(solution)/shard_map/ppermute | solution.py:30
  21.8 8.5 %collective-permute-start.1 = (bf16[32,1024]{1,0:T(8,128)(2,1)S(1)}, bf16[32,1024]{1,0:T(8,128)(2,1)S(1)}, u32[]{:S(2)}, u32[]{:S(2)}) collective-permute-start(bf16[32,1024]{1,0:T(8,128)(2,1)S(1)} %reduce_sum.12), channel_id=1, source_target_pairs={{0,16},{16,0},{1,17},{17,1},{2,18},{18,2},{3,19},{19,3},{4,20},{20... | collective-permute-start | bytes 196616 | tf_op jit(solution)/shard_map/ppermute | solution.py:30
  49.2 4.5 %collective-permute-start.3 = (bf16[2,256,1024]{2,1,0:T(8,128)(2,1)S(1)}, bf16[2,256,1024]{2,1,0:T(8,128)(2,1)S(1)}, u32[]{:S(2)}, u32[]{:S(2)}) collective-permute-start(bf16[2,256,1024]{2,1,0:T(8,128)(2,1)S(1)} %bitcast.17), channel_id=1, source_target_pairs={{0,1},{1,0},{2,3},{3,2},{4,5},{5,4},{6,7},{7,6},{8,9},{9,8},{10,11... | collective-permute-start | bytes 3145736 | tf_op jit(solution)/shard_map/ppermute | solution.py:30
  51.2 2.6 %copy-start.1 = (s32[2,4]{1,0:T(2,128)S(1)}, s32[2,4]{1,0:T(2,128)}, u32[]{:S(2)}) copy-start(s32[2,4]{1,0:T(2,128)} %seg_ref.3) | copy-start | bytes 100
  56.9 11.6 %collective-permute-start.4 = (bf16[32,4096]{1,0:T(8,128)(2,1)S(1)}, bf16[32,4096]{1,0:T(8,128)(2,1)S(1)}, u32[]{:S(2)}, u32[]{:S(2)}) collective-permute-start(bf16[32,4096]{1,0:T(8,128)(2,1)S(1)} %shard_map.55), channel_id=1, source_target_pairs={{0,384},{128,256},{1,385},{129,257},{2,386},{130,258},{3,387},{131... | collective-permute-start | bytes 786440 | tf_op jit(solution)/shard_map/ppermute | solution.py:178
  71.6 9.6 %collective-permute-start.5 = (bf16[32,4096]{1,0:T(8,128)(2,1)S(1)}, bf16[32,4096]{1,0:T(8,128)(2,1)S(1)}, u32[]{:S(2)}, u32[]{:S(2)}) collective-permute-start(bf16[32,4096]{1,0:T(8,128)(2,1)S(1)} %broadcast_select_fusion), channel_id=1, source_target_pairs={{0,128},{128,0},{1,129},{129,1},{2,130},{130,2},{3,131},{131,3},{4... | collective-permute-start | bytes 786440 | tf_op jit(solution)/shard_map/ppermute | solution.py:30

commit v3 on v2

v3 whole, which is shorter than its diff:
```python
import functools
import math

import jax
import jax.numpy as jnp
from jax import lax
from jax.experimental import pallas as pl
from jax.experimental.pallas import tpu as pltpu
from jax.sharding import Mesh, PartitionSpec as P

HQ = 32
KVH = 4
GROUP = HQ // KVH
HEAD_SIZE = 128
WIDTH = HQ * HEAD_SIZE
KVW = KVH * HEAD_SIZE
PLEN = 512
TOKM = 32
RESPS = 4
PROMPTS = 4
EPS = 1e-06
EXP2_SCALE = math.log2(math.e) / math.sqrt(HEAD_SIZE)

SECTION = ("yh", "yl")
RESP = ("p", "zh", "zl", "x", "c")
PLANE = ("zl", "x", "c")
SPREAD = ("yl", "zl", "x")


def swap(x, axis):
    return lax.ppermute(x, axis, [(0, 1), (1, 0)])


def product(a, b, over):
    return lax.dot_general(a, b, (((over,), (over,)), ((), ())), preferred_element_type=jnp.float32)


def over_rows(reduce, blocks):
    pair = jnp.maximum if reduce is jnp.max else jnp.add
    wide = reduce(pair(blocks[0], blocks[1]), axis=0, keepdims=True)
    return pair(wide, reduce(blocks[2], axis=0, keepdims=True))


def attend(x, keys, values, near_mask, att_ref):
    rows = x.shape[0]
    groups = range(KVH)
    heads = [x[:, h * HEAD_SIZE : (h + 1) * HEAD_SIZE] for h in range(HQ)]
    queries = [jnp.concatenate(heads[g * GROUP : (g + 1) * GROUP], axis=0) for g in groups]
    scores = [[product(k, queries[g], 1) for k in keys(g)] for g in groups]
    for g in groups:
        scores[g][2] = scores[g][2] + near_mask
    top = [over_rows(jnp.max, scores[g]) for g in groups]
    raised = [[jnp.exp2((s - top[g]) * EXP2_SCALE) for s in scores[g]] for g in groups]
    share = [1.0 / over_rows(jnp.sum, raised[g]) for g in groups]
    weights = [[(e * share[g]).astype(jnp.bfloat16) for e in raised[g]] for g in groups]
    total = jnp.zeros((1, GROUP * rows), jnp.float32)
    for g in groups:
        out = sum(product(v, w, 0) for v, w in zip(values(g), weights[g], strict=True))
        att_ref[g] = out
        total = total + jnp.sum(out * out, axis=0, keepdims=True)
    reach = rows
    while reach < GROUP * rows:
        total = total + pltpu.roll(total, reach, 1)
        reach *= 2
    return lax.rsqrt(total * (1.0 / WIDTH) + EPS)


def pair_kernel(micro, seg_ref, q_ref, rkv_ref, other_ref, *refs):
    carried = 0.0
    done_ref = None
    if len(refs) == 4:
        kv0_ref, kv1_ref, out_ref, att_ref = refs
    elif len(refs) == 5:
        carried_ref, kv0_ref, kv1_ref, out_ref, att_ref = refs
    else:
        carried_ref, done_ref, kv0_ref, kv1_ref, out_ref, att_ref = refs
    ends = len(refs) > 4
    if ends:
        carried = carried_ref[...].astype(jnp.float32)
    second = lax.axis_index("yl")
    rows = slice(micro * TOKM, (micro + 1) * TOKM)

    at_key = lax.broadcasted_iota(jnp.int32, (TOKM, TOKM), 0)
    at_query = lax.broadcasted_iota(jnp.int32, (TOKM, TOKM), 1)
    of_key, of_query = jnp.zeros_like(at_key), jnp.zeros_like(at_query)
    end = jnp.zeros((1, 1), jnp.int32)
    for i in range(RESPS):
        end = end + seg_ref[micro : micro + 1, i : i + 1]
        of_key = of_key + (at_key >= end).astype(jnp.int32)
        of_query = of_query + (at_query >= end).astype(jnp.int32)
    allowed = (of_key == of_query) & (at_key <= at_query)
    near_mask = jnp.where(allowed, 0.0, -jnp.inf).astype(jnp.float32)
    near_mask = jnp.concatenate([near_mask] * GROUP, axis=1)

    outs = []
    for layer in range(2):
        is_own = second == layer
        query = jnp.where(is_own, q_ref[rows, :], other_ref[rows, :WIDTH]).astype(jnp.float32)
        near = jnp.where(is_own, rkv_ref[rows, :], other_ref[rows, WIDTH:])
        x = (query + carried).astype(jnp.bfloat16)

        def blocks(first, layer=layer, near=near):
            def of_group(g):
                lanes = slice(first + g * HEAD_SIZE, first + (g + 1) * HEAD_SIZE)
                return [kv0_ref[layer, :, lanes], kv1_ref[layer, :, lanes], near[:, lanes]]

            return of_group

        scaling = attend(x, blocks(0), blocks(KVW), near_mask, att_ref)
        heads = []
        for g in range(KVH):
            normed = (att_ref[g] * scaling).T.astype(jnp.bfloat16)
            heads += [normed[at * TOKM : (at + 1) * TOKM] for at in range(GROUP)]
        outs.append(jnp.concatenate(heads, axis=1))
        carried = outs[0].astype(jnp.float32)
    result = jnp.where(second == 0, outs[0], outs[1]) if ends else outs[1]
    if done_ref is None:
        out_ref[...] = result
    else:
        out_ref[:TOKM] = done_ref[...]
        out_ref[TOKM:] = result


def attend_pair(micro, fixed, kv, carried=None, done=None):
    vmem = pl.BlockSpec(memory_space=pltpu.VMEM)
    rows = TOKM if done is None else 2 * TOKM
    middle = [x for x in (carried, done) if x is not None]
    return pl.pallas_call(
        functools.partial(pair_kernel, micro),
        out_shape=jax.ShapeDtypeStruct((rows, WIDTH), jnp.bfloat16),
        in_specs=[vmem] * (len(fixed) + len(middle) + len(kv)),
        out_specs=vmem,
        scratch_shapes=[pltpu.VMEM((KVH, HEAD_SIZE, GROUP * TOKM), jnp.float32)],
        compiler_params=pltpu.CompilerParams(vmem_limit_bytes=12 * 1024 * 1024),
        cost_estimate=pl.CostEstimate(
            flops=2 * 4 * HQ * TOKM * (PLEN + TOKM) * HEAD_SIZE,
            bytes_accessed=4 * 1024 * 1024,
            transcendentals=2 * HQ * TOKM * (PLEN + TOKM),
        ),
    )(*fixed, *middle, *kv)


def spread_prefix(prefix, owner_piece, in_half, beside):
    parts = math.prod(lax.axis_size(axis) for axis in PLANE)
    pieces = lax.all_to_all(prefix.reshape(parts, PLEN // parts, -1), PLANE, 0, 0)
    piece = lax.dynamic_index_in_dim(pieces, owner_piece, 0, keepdims=False)
    piece = jnp.where(in_half, piece, swap(piece, "zh"))
    piece, beside = lax.optimization_barrier((piece, beside))
    copies = math.prod(lax.axis_size(axis) for axis in SPREAD)
    gathered = lax.all_to_all(jnp.broadcast_to(piece[None], (copies, *piece.shape)), SPREAD, 0, 0)
    gathered = gathered.reshape(lax.axis_size("yl"), -1, gathered.shape[2])
    return gathered, swap(gathered, "c"), beside


def local(queries, resp_kv, prefix_kv, owner, seg_len):
    at = {axis: lax.axis_index(axis) for axis in ("p", "zh")}
    owner_rank = jnp.sum(jnp.where(jnp.arange(PROMPTS) == at["p"], owner[0], 0))
    parts = math.prod(lax.axis_size(axis) for axis in PLANE)
    owner_piece = owner_rank % parts
    in_half = owner_rank // parts % lax.axis_size("zh") == at["zh"]

    other = swap(jnp.concatenate([queries[0], resp_kv[0]], axis=1), "yl")
    kv0, kv1, other = spread_prefix(prefix_kv[0], owner_piece, in_half, other)

    fixed, kv = (seg_len, queries[0], resp_kv[0], other), (kv0, kv1)
    hop = [(0, 3), (1, 2)]
    carried0 = lax.ppermute(attend_pair(0, fixed, kv), SECTION, hop)
    carried1 = lax.ppermute(attend_pair(1, fixed, kv), SECTION, hop)
    done = attend_pair(0, fixed, kv, carried0)
    return attend_pair(1, fixed, kv, carried1, done)[None]


def solution(mesh):
    fine = Mesh(mesh.devices.reshape(2, 2, PROMPTS, 2, 2, 4, 2), SECTION + RESP)
    return jax.shard_map(
        local,
        mesh=fine,
        in_specs=(
            P(SECTION, RESP, None),
            P(SECTION, RESP, None),
            P(SECTION, RESP, None),
            P(SECTION, None),
            P(RESP, None),
        ),
        out_specs=P(SECTION, RESP, None),
        check_vma=False,
    )
```

time: 82.4 us -> 80.1 us (0.972)
  Pallas kernels: 6.18 us -> 12.9 us
  waiting for transfers between devices: 31 us -> 24.9 us
  starting transfers between devices: 20.8 us -> 18.2 us
  local copies, waits for them, and re-layouts: 1.95 us -> 0.14 us
  blocking collectives: 18.7 us -> 20.1 us
  between operations: 1.5 us -> 2.79 us
  other arithmetic: 1.91 us -> 0.69 us
    ppermute x5 -> x3, waiting for transfers between devices: 13.5 us -> 5.22 us  [swap(): return lax.ppermute(x, axis, [(0, 1), (1, 0)])]
    pallas_call x2 -> x4, Pallas kernels: 6.18 us -> 12.9 us  [attend_pair(): pl.pallas_call(functools.partial(pair_kernel, micro), out_shape=jax.Shape...]
    ppermute x5 -> x3, starting transfers between devices: 13.7 us -> 9.73 us  [swap(): return lax.ppermute(x, axis, [(0, 1), (1, 0)])]
    all_to_all x1, waiting for transfers between devices: 7.31 us -> 11.3 us  [spread_prefix(): lax.all_to_all(prefix.reshape(parts, PLEN // parts, -1), PLANE, 0, 0)]
    ppermute x1 -> x2, waiting for transfers between devices: 10.3 us -> 8.39 us  [the longest x1 6.63 us: local(): carried0 = lax.ppermute(attend_pair(0, fixed, kv), SECTION, hop)]
    all_to_all x1, blocking collectives: 18.7 us -> 20.1 us  [spread_prefix(): lax.all_to_all(jnp.broadcast_to(piece[None], (copies, *piece.shape)), SPR...]
    ppermute x1 -> x2, starting transfers between devices: 1.29 us -> 2.58 us  [the longest x1 1.29 us: local(): carried0 = lax.ppermute(attend_pair(0, fixed, kv), SECTION, hop)]
    slice x1 -> x0, local copies, waits for them, and re-layouts: 1.16 us -> none  [spread_prefix(): arrived = swap(prefix[half:], 'c')]
  transfers between devices with their start and end apart: 7 -> 6, of which waited for: 5 -> 5; matrix products, arithmetic and copies ran while one was open for 1% -> 1% of each run, Pallas kernels for 0% -> 8%
where the time goes in v3:
time: 80.1 us; the launch traced here: 79.7 us
  waiting for transfers between devices  24.9 us (31%)
  blocking collectives  20.1 us (25%)
  starting transfers between devices  18.2 us (23%)
  Pallas kernels  12.9 us (16%)
  between operations  2.79 us (3%)
    all_to_all x1, blocking collectives, spread_prefix(): lax.all_to_all(jnp.broadcast_to(piece[None], (copies, *piece.shape)), SPR...  20.1 us
    pallas_call x4, Pallas kernels, attend_pair(): pl.pallas_call(functools.partial(pair_kernel, micro), out_shape=jax.Shape...  12.9 us
    all_to_all x1, waiting for transfers between devices, spread_prefix(): lax.all_to_all(prefix.reshape(parts, PLEN // parts, -1), PLANE, 0, 0)  11.3 us
    ppermute x3, starting transfers between devices, swap(): return lax.ppermute(x, axis, [(0, 1), (1, 0)])  9.73 us
    ppermute x1, waiting for transfers between devices, local(): carried0 = lax.ppermute(attend_pair(0, fixed, kv), SECTION, hop)  6.63 us
    all_to_all x1, starting transfers between devices, spread_prefix(): lax.all_to_all(prefix.reshape(parts, PLEN // parts, -1), PLANE, 0, 0)  5.89 us
    ppermute x3, waiting for transfers between devices, swap(): return lax.ppermute(x, axis, [(0, 1), (1, 0)])  5.22 us
    ppermute x1, waiting for transfers between devices, local(): carried1 = lax.ppermute(attend_pair(1, fixed, kv), SECTION, hop)  1.77 us
  transfers between devices with their start and end apart: 6, of which 5 were waited for; matrix products, arithmetic and copies ran while one was open for 1% of the time, Pallas kernels for 8%

profile of v3, /device:TPU:24, one launch (start us, length us, event | category | flops | bytes accessed | tf_op | source)
XLA Modules:
  0.0 79.7 jit_solution(9351220683700143366)
XLA Ops:
  0.0 0.0 copy-start
  0.0 0.0 copy-start.1
  0.0 5.9 %all-to-all-start = ((bf16[16,32,1024]{2,1,0:T(8,128)(2,1)}), bf16[16,32,1024]{2,1,0:T(8,128)(2,1)S(1)}, u32[]{:S(2)}, u32[]{:S(2)}) async-start(bf16[16,32,1024]{2,1,0:T(8,128)(2,1)} %bitcast.26), calls=%async_computation | async-start | bytes 2097152 | tf_op jit(solution)/shard_map/all_to_all | solution.py:145
  5.9 0.0 copy-start.3
  5.9 0.0 copy-done
  5.9 0.0 copy-done.1
  6.0 2.7 %collective-permute-start.1 = (bf16[64,5120]{1,0:T(8,128)(2,1)S(1)}, bf16[64,5120]{1,0:T(8,128)(2,1)S(1)}, u32[]{:S(2)}, u32[]{:S(2)}) collective-permute-start(bf16[64,5120]{1,0:T(8,128)(2,1)S(1)} %pad_maximum_fusion), channel_id=1, source_target_pairs={{0,128},{128,0},{1,129},{129,1},{2,130},{130,2},{3,131},{131,3},{4... | collective-permute-start | bytes 1966088 | tf_op jit(solution)/shard_map/ppermute | solution.py:31
  8.7 0.0 copy-done.3
  8.7 0.6 fusion
  11.3 11.3 %all-to-all-done = bf16[16,32,1024]{2,1,0:T(8,128)(2,1)S(1)} async-done(((bf16[16,32,1024]{2,1,0:T(8,128)(2,1)}), bf16[16,32,1024]{2,1,0:T(8,128)(2,1)S(1)}, u32[]{:S(2)}, u32[]{:S(2)}) %all-to-all-start) | async-done | bytes 1048608 | tf_op jit(solution)/shard_map/all_to_all | solution.py:145
  22.5 5.2 %collective-permute-start = (bf16[32,1024]{1,0:T(8,128)(2,1)S(1)}, bf16[32,1024]{1,0:T(8,128)(2,1)S(1)}, u32[]{:S(2)}, u32[]{:S(2)}) collective-permute-start(bf16[32,1024]{1,0:T(8,128)(2,1)S(1)} %dynamic-slice_bitcast_fusion), channel_id=1, source_target_pairs={{0,16},{16,0},{1,17},{17,1},{2,18},{18,2},{3,19},{19,3},{4,20},{20... | collective-permute-start | bytes 196616 | tf_op jit(solution)/shard_map/ppermute | solution.py:31
  28.4 2.6 %collective-permute-done = bf16[32,1024]{1,0:T(8,128)(2,1)S(1)} collective-permute-done((bf16[32,1024]{1,0:T(8,128)(2,1)S(1)}, bf16[32,1024]{1,0:T(8,128)(2,1)S(1)}, u32[]{:S(2)}, u32[]{:S(2)}) %collective-permute-start) | collective-permute-done | bytes 65568 | tf_op jit(solution)/shard_map/ppermute | solution.py:31
  31.0 0.0 collective-permute-done.1.other_ref
  31.0 0.1 broadcast_in_dim.14
  31.1 0.0 copy-start.2
  31.1 20.1 %all_to_all.10 = bf16[16,32,1024]{2,1,0:T(8,128)(2,1)S(1)} all-to-all(bf16[16,32,1024]{2,1,0:T(8,128)(2,1)S(1)} %broadcast_in_dim.14), channel_id=1, replica_groups=mesh['yh'=2,'yl'=2,'p'=4,'zh'=2,'zl'=2,'x'=4,'c'=2] {'yl','zl','x'}, dimensions={0} | all-to-all | bytes 2097152 | tf_op jit(solution)/shard_map/all_to_all | solution.py:150
  51.2 1.9 %collective-permute-start.2 = (bf16[2,256,1024]{2,1,0:T(8,128)(2,1)S(1)}, bf16[2,256,1024]{2,1,0:T(8,128)(2,1)S(1)}, u32[]{:S(2)}, u32[]{:S(2)}) collective-permute-start(bf16[2,256,1024]{2,1,0:T(8,128)(2,1)S(1)} %bitcast.11), channel_id=1, source_target_pairs={{0,1},{1,0},{2,3},{3,2},{4,5},{5,4},{6,7},{7,6},{8,9},{9,8},{10,11... | collective-permute-start | bytes 3145736 | tf_op jit(solution)/shard_map/ppermute | solution.py:31
  53.2 2.6 %collective-permute-done.2.refs_1_.refs_2_.refs_3_ = bf16[2,256,1024]{2,1,0:T(8,128)(2,1)S(1)} collective-permute-done((bf16[2,256,1024]{2,1,0:T(8,128)(2,1)S(1)}, bf16[2,256,1024]{2,1,0:T(8,128)(2,1)S(1)}, u32[]{:S(2)}, u32[]{:S(2)}) %collective-permute-start.2) | collective-permute-done | bytes 1048608 | tf_op jit(solution)/shard_map/ppermute | solution.py:31
  55.8 0.0 copy-done.2
  55.8 3.0 %shard_map.56 = bf16[32,4096]{1,0:T(8,128)(2,1)S(1)} custom-call(s32[2,4]{1,0:T(2,128)S(1)} %copy-done.2, bf16[64,4096]{1,0:T(8,128)(2,1)S(1)} %bitcast.17, bf16[64,1024]{1,0:T(8,128)(2,1)S(1)} %bitcast.22, bf16[64,5120]{1,0:T(8,128)(2,1)S(1)} %collective-permute-done.1.other_ref, bf16[2,256,1024]{2,1,0:T(8,128)(2,1)S(1)} %bitcast.12, ...), custom_call_target="tpu_custom_call" | custom-call | flops 570425344 | bytes 4194304 | tf_op jit(solution)/shard_map/pallas_call | solution.py:128
  58.8 1.3 %collective-permute-start.4 = (bf16[32,4096]{1,0:T(8,128)(2,1)S(1)}, bf16[32,4096]{1,0:T(8,128)(2,1)S(1)}, u32[]{:S(2)}, u32[]{:S(2)}) collective-permute-start(bf16[32,4096]{1,0:T(8,128)(2,1)S(1)} %shard_map.56), channel_id=1, source_target_pairs={{0,384},{128,256},{1,385},{129,257},{2,386},{130,258},{3,387},{131... | collective-permute-start | bytes 786440 | tf_op jit(solution)/shard_map/ppermute | solution.py:167
  60.1 3.0 %shard_map.55 = bf16[32,4096]{1,0:T(8,128)(2,1)S(1)} custom-call(s32[2,4]{1,0:T(2,128)S(1)} %copy-done.2, bf16[64,4096]{1,0:T(8,128)(2,1)S(1)} %bitcast.18, bf16[64,1024]{1,0:T(8,128)(2,1)S(1)} %bitcast.23, bf16[64,5120]{1,0:T(8,128)(2,1)S(1)} %collective-permute-done.1.other_ref, bf16[2,256,1024]{2,1,0:T(8,128)(2,1)S(1)} %bitcast.13, ...), custom_call_target="tpu_custom_call" | custom-call | flops 570425344 | bytes 4194304 | tf_op jit(solution)/shard_map/pallas_call | solution.py:128
  63.1 1.3 %collective-permute-start.3 = (bf16[32,4096]{1,0:T(8,128)(2,1)S(1)}, bf16[32,4096]{1,0:T(8,128)(2,1)S(1)}, u32[]{:S(2)}, u32[]{:S(2)}) collective-permute-start(bf16[32,4096]{1,0:T(8,128)(2,1)S(1)} %shard_map.55), channel_id=1, source_target_pairs={{0,384},{128,256},{1,385},{129,257},{2,386},{130,258},{3,387},{131... | collective-permute-start | bytes 786440 | tf_op jit(solution)/shard_map/ppermute | solution.py:168
  64.4 6.6 %collective-permute-done.4.refs_0_ = bf16[32,4096]{1,0:T(8,128)(2,1)S(1)} collective-permute-done((bf16[32,4096]{1,0:T(8,128)(2,1)S(1)}, bf16[32,4096]{1,0:T(8,128)(2,1)S(1)}, u32[]{:S(2)}, u32[]{:S(2)}) %collective-permute-start.4) | collective-permute-done | bytes 262176 | tf_op jit(solution)/shard_map/ppermute | solution.py:167
  71.1 3.0 %shard_map.57.refs_1_ = bf16[32,4096]{1,0:T(8,128)(2,1)S(1)} custom-call(s32[2,4]{1,0:T(2,128)S(1)} %copy-done.2, bf16[64,4096]{1,0:T(8,128)(2,1)S(1)} %bitcast.19, bf16[64,1024]{1,0:T(8,128)(2,1)S(1)} %bitcast.24, bf16[64,5120]{1,0:T(8,128)(2,1)S(1)} %collective-permute-done.1.other_ref, bf16[32,4096]{1,0:T(8,128)(2,1)S(1)} %collective-permute-done.4.refs_0_, ...), custom_call_target="tpu_custom_call" | custom-call | flops 570425344 | bytes 4194304 | tf_op jit(solution)/shard_map/pallas_call | solution.py:128
  74.1 1.8 %collective-permute-done.3.refs_0_ = bf16[32,4096]{1,0:T(8,128)(2,1)S(1)} collective-permute-done((bf16[32,4096]{1,0:T(8,128)(2,1)S(1)}, bf16[32,4096]{1,0:T(8,128)(2,1)S(1)}, u32[]{:S(2)}, u32[]{:S(2)}) %collective-permute-start.3) | collective-permute-done | bytes 262176 | tf_op jit(solution)/shard_map/ppermute | solution.py:168
  75.9 3.8 %shard_map.58 = bf16[64,4096]{1,0:T(8,128)(2,1)} custom-call(s32[2,4]{1,0:T(2,128)S(1)} %copy-done.2, bf16[64,4096]{1,0:T(8,128)(2,1)S(1)} %bitcast.20, bf16[64,1024]{1,0:T(8,128)(2,1)S(1)} %bitcast.25, bf16[64,5120]{1,0:T(8,128)(2,1)S(1)} %collective-permute-done.1.other_ref, bf16[32,4096]{1,0:T(8,128)(2,1)S(1)} %collective-permute-done.3.refs_0_, ...), custom_call_target="tpu_custom_call" | custom-call | flops 570425344 | bytes 4194304 | tf_op jit(solution)/shard_map/pallas_call | solution.py:128
  (3 shorter events, 0.1 us)
Async XLA Ops:
  0.0 5.9 %copy-start = (bf16[1,64,4096]{2,1,0:T(8,128)(2,1)S(1)}, bf16[1,64,4096]{2,1,0:T(8,128)(2,1)}, u32[]{:S(2)}) copy-start(bf16[1,64,4096]{2,1,0:T(8,128)(2,1)} %param.5) | copy-start | bytes 1572868
  0.0 5.9 %copy-start.1 = (bf16[1,64,1024]{2,1,0:T(8,128)(2,1)S(1)}, bf16[1,64,1024]{2,1,0:T(8,128)(2,1)}, u32[]{:S(2)}) copy-start(bf16[1,64,1024]{2,1,0:T(8,128)(2,1)} %param.6) | copy-start | bytes 393220
  0.0 22.5 %all-to-all-start = ((bf16[16,32,1024]{2,1,0:T(8,128)(2,1)}), bf16[16,32,1024]{2,1,0:T(8,128)(2,1)S(1)}, u32[]{:S(2)}, u32[]{:S(2)}) async-start(bf16[16,32,1024]{2,1,0:T(8,128)(2,1)} %bitcast.26), calls=%async_computation | async-start | bytes 2097152 | tf_op jit(solution)/shard_map/all_to_all | solution.py:145
  5.9 2.8 %copy-start.3 = (s32[1,4]{1,0:T(1,128)S(1)}, s32[1,4]{1,0:T(1,128)}, u32[]{:S(2)}) copy-start(s32[1,4]{1,0:T(1,128)} %param.8) | copy-start | bytes 52
  6.0 25.0 %collective-permute-start.1 = (bf16[64,5120]{1,0:T(8,128)(2,1)S(1)}, bf16[64,5120]{1,0:T(8,128)(2,1)S(1)}, u32[]{:S(2)}, u32[]{:S(2)}) collective-permute-start(bf16[64,5120]{1,0:T(8,128)(2,1)S(1)} %pad_maximum_fusion), channel_id=1, source_target_pairs={{0,128},{128,0},{1,129},{129,1},{2,130},{130,2},{3,131},{131,3},{4... | collective-permute-start | bytes 1966088 | tf_op jit(solution)/shard_map/ppermute | solution.py:31
  22.5 8.5 %collective-permute-start = (bf16[32,1024]{1,0:T(8,128)(2,1)S(1)}, bf16[32,1024]{1,0:T(8,128)(2,1)S(1)}, u32[]{:S(2)}, u32[]{:S(2)}) collective-permute-start(bf16[32,1024]{1,0:T(8,128)(2,1)S(1)} %dynamic-slice_bitcast_fusion), channel_id=1, source_target_pairs={{0,16},{16,0},{1,17},{17,1},{2,18},{18,2},{3,19},{19,3},{4,20},{20... | collective-permute-start | bytes 196616 | tf_op jit(solution)/shard_map/ppermute | solution.py:31
  31.1 24.7 %copy-start.2 = (s32[2,4]{1,0:T(2,128)S(1)}, s32[2,4]{1,0:T(2,128)}, u32[]{:S(2)}) copy-start(s32[2,4]{1,0:T(2,128)} %seg_ref.7) | copy-start | bytes 100
  51.2 4.5 %collective-permute-start.2 = (bf16[2,256,1024]{2,1,0:T(8,128)(2,1)S(1)}, bf16[2,256,1024]{2,1,0:T(8,128)(2,1)S(1)}, u32[]{:S(2)}, u32[]{:S(2)}) collective-permute-start(bf16[2,256,1024]{2,1,0:T(8,128)(2,1)S(1)} %bitcast.11), channel_id=1, source_target_pairs={{0,1},{1,0},{2,3},{3,2},{4,5},{5,4},{6,7},{7,6},{8,9},{9,8},{10,11... | collective-permute-start | bytes 3145736 | tf_op jit(solution)/shard_map/ppermute | solution.py:31
  58.8 12.3 %collective-permute-start.4 = (bf16[32,4096]{1,0:T(8,128)(2,1)S(1)}, bf16[32,4096]{1,0:T(8,128)(2,1)S(1)}, u32[]{:S(2)}, u32[]{:S(2)}) collective-permute-start(bf16[32,4096]{1,0:T(8,128)(2,1)S(1)} %shard_map.56), channel_id=1, source_target_pairs={{0,384},{128,256},{1,385},{129,257},{2,386},{130,258},{3,387},{131... | collective-permute-start | bytes 786440 | tf_op jit(solution)/shard_map/ppermute | solution.py:167
  63.1 12.7 %collective-permute-start.3 = (bf16[32,4096]{1,0:T(8,128)(2,1)S(1)}, bf16[32,4096]{1,0:T(8,128)(2,1)S(1)}, u32[]{:S(2)}, u32[]{:S(2)}) collective-permute-start(bf16[32,4096]{1,0:T(8,128)(2,1)S(1)} %shard_map.55), channel_id=1, source_target_pairs={{0,384},{128,256},{1,385},{129,257},{2,386},{130,258},{3,387},{131... | collective-permute-start | bytes 786440 | tf_op jit(solution)/shard_map/ppermute | solution.py:168

commit v4 on v3

v4 whole, which is shorter than its diff:
```python
import functools
import math

import jax
import jax.numpy as jnp
from jax import lax
from jax.experimental import pallas as pl
from jax.experimental.pallas import tpu as pltpu
from jax.sharding import Mesh, PartitionSpec as P

HQ = 32
KVH = 4
GROUP = HQ // KVH
HEAD_SIZE = 128
WIDTH = HQ * HEAD_SIZE
KVW = KVH * HEAD_SIZE
PLEN = 512
TOKM = 32
MB = 2
LANES = GROUP * TOKM
EARLY = 6
RESPS = 4
PROMPTS = 4
EPS = 1e-06
EXP2_SCALE = math.log2(math.e) / math.sqrt(HEAD_SIZE)

SECTION = ("yh", "yl")
RESP = ("p", "zh", "zl", "x", "c")
PLANE = ("zl", "x")
SPREAD = ("yl", *PLANE)


def swap(x, axis):
    return lax.ppermute(x, axis, [(0, 1), (1, 0)])


def product(a, b, a_over, b_over):
    over = (((a_over,), (b_over,)), ((), ()))
    return lax.dot_general(a, b, over, preferred_element_type=jnp.float32)


def over_rows(reduce, blocks):
    pair = jnp.maximum if reduce is jnp.max else jnp.add
    wide = reduce(pair(blocks[0], blocks[1]), axis=0, keepdims=True)
    return pair(wide, reduce(blocks[2], axis=0, keepdims=True))


def attend(x, keys, values, near_mask, att_ref):
    groups = range(KVH)
    lanes = x[0].shape[1]
    scores = [[product(k, x[g], 1, 0) for k in keys(g)] for g in groups]
    for g in groups:
        scores[g][2] = scores[g][2] + near_mask
    top = [over_rows(jnp.max, scores[g]) for g in groups]
    raised = [[jnp.exp2((s - top[g]) * EXP2_SCALE) for s in scores[g]] for g in groups]
    share = [1.0 / over_rows(jnp.sum, raised[g]) for g in groups]
    weights = [[(e * share[g]).astype(jnp.bfloat16) for e in raised[g]] for g in groups]
    total = jnp.zeros((1, lanes), jnp.float32)
    for g in groups:
        out = sum(product(v, w, 0, 0) for v, w in zip(values(g), weights[g], strict=True))
        att_ref[g] = out
        total = total + jnp.sum(out * out, axis=0, keepdims=True)
    reach = TOKM
    while reach < lanes:
        total = total + pltpu.roll(total, reach, 1)
        reach *= 2
    scaling = lax.rsqrt(total * (1.0 / WIDTH) + EPS)
    return [(att_ref[g] * scaling).astype(jnp.bfloat16) for g in groups]


def pack_kernel(q_ref, rkv_ref, early_ref, late_ref):
    for micro in range(MB):
        rows = slice(micro * TOKM, (micro + 1) * TOKM)
        for g in range(KVH):
            heads = [
                q_ref[rows, h * HEAD_SIZE : (h + 1) * HEAD_SIZE]
                for h in range(g * GROUP, (g + 1) * GROUP)
            ]
            is_late, first = query_rows(micro, g)
            out_ref = late_ref if is_late else early_ref
            out_ref[first : first + HEAD_SIZE] = jnp.concatenate(heads, axis=0).T
        for part in range(2 * KVW // LANES):
            first = near_rows(micro, part)
            early_ref[first : first + TOKM] = rkv_ref[rows, part * LANES : (part + 1) * LANES]


def query_rows(micro, g):
    place = micro * KVH + g
    is_late = place >= EARLY
    return is_late, (place - EARLY if is_late else place) * HEAD_SIZE


def near_rows(micro, part):
    return EARLY * HEAD_SIZE + (micro * (2 * KVW // LANES) + part) * TOKM


def packed(q, rkv):
    vmem = pl.BlockSpec(memory_space=pltpu.VMEM)
    sizes = near_rows(MB, 0), (MB * KVH - EARLY) * HEAD_SIZE
    return pl.pallas_call(
        pack_kernel,
        out_shape=tuple(jax.ShapeDtypeStruct((size, LANES), jnp.bfloat16) for size in sizes),
        in_specs=[vmem, vmem],
        out_specs=(vmem, vmem),
        compiler_params=pltpu.CompilerParams(vmem_limit_bytes=12 * 1024 * 1024),
        cost_estimate=pl.CostEstimate(flops=0, bytes_accessed=1280 * 1024, transcendentals=0),
    )(q, rkv)


def pair_kernel(micro, seg_ref, own_ref, other_ref, *refs):
    late_refs, carried_ref, done_ref = (), None, None
    if micro == 1:
        *late_refs, refs = refs[0], refs[1], refs[2:]
    if len(refs) == 4:
        kv0_ref, kv1_ref, out_ref, att_ref = refs
    elif len(refs) == 5:
        carried_ref, kv0_ref, kv1_ref, out_ref, att_ref = refs
    else:
        carried_ref, done_ref, kv0_ref, kv1_ref, out_ref, att_ref, rows_ref, sems = refs
        copies = [
            pltpu.make_async_copy(source, out_ref.at[pl.ds(i * TOKM, TOKM)], sems.at[i])
            for i, source in enumerate((done_ref, rows_ref))
        ]
        copies[0].start()
    second = lax.axis_index("yl")

    at_key = lax.broadcasted_iota(jnp.int32, (TOKM, TOKM), 0)
    at_query = lax.broadcasted_iota(jnp.int32, (TOKM, TOKM), 1)
    of_key, of_query = jnp.zeros_like(at_key), jnp.zeros_like(at_query)
    end = jnp.zeros((1, 1), jnp.int32)
    for i in range(RESPS):
        end = end + seg_ref[micro : micro + 1, i : i + 1]
        of_key = of_key + (at_key >= end).astype(jnp.int32)
        of_query = of_query + (at_query >= end).astype(jnp.int32)
    allowed = (of_key == of_query) & (at_key <= at_query)
    near_mask = jnp.where(allowed, 0.0, -jnp.inf).astype(jnp.float32)
    near_mask = jnp.concatenate([near_mask] * GROUP, axis=1)

    def group_rows(g):
        return slice(g * HEAD_SIZE, (g + 1) * HEAD_SIZE)

    outs = []
    for layer in range(2):
        is_own = second == layer

        def one_of_both(first, count, lanes=slice(None), refs=(own_ref, other_ref), is_own=is_own):
            own, other = (ref[first : first + count, lanes] for ref in refs)
            return jnp.where(is_own, own, other)

        x = []
        for g in range(KVH):
            is_late, first = query_rows(micro, g)
            early = own_ref, other_ref
            query = one_of_both(first, HEAD_SIZE, refs=late_refs if is_late else early)
            if layer == 1:
                query = query.astype(jnp.float32) + outs[0][g].astype(jnp.float32)
            elif carried_ref is not None:
                query = query.astype(jnp.float32) + carried_ref[group_rows(g)].astype(jnp.float32)
            x.append(query.astype(jnp.bfloat16))

        def blocks(column, layer=layer, one_of_both=one_of_both):
            def of_group(g):
                lanes = slice(column + g * HEAD_SIZE, column + (g + 1) * HEAD_SIZE)
                first = near_rows(micro, lanes.start // LANES)
                inside = slice(lanes.start % LANES, lanes.start % LANES + HEAD_SIZE)
                near = one_of_both(first, TOKM, inside)
                return [kv0_ref[layer, :, lanes], kv1_ref[layer, :, lanes], near]

            return of_group

        outs.append(attend(x, blocks(0), blocks(KVW), near_mask, att_ref))
    if carried_ref is None:
        for g in range(KVH):
            out_ref[group_rows(g)] = outs[1][g]
        return
    if done_ref is None:
        rows_ref = out_ref
    for g in range(KVH):
        normed = jnp.where(second == 0, outs[0][g], outs[1][g]).T
        for at in range(GROUP):
            h = g * GROUP + at
            rows_ref[:, h * HEAD_SIZE : (h + 1) * HEAD_SIZE] = normed[at * TOKM : (at + 1) * TOKM]
    if done_ref is not None:
        copies[1].start()
        copies[0].wait()
        copies[1].wait()


def attend_pair(micro, fixed, kv, carried=None, done=None):
    vmem = pl.BlockSpec(memory_space=pltpu.VMEM)
    middle = [x for x in (carried, done) if x is not None]
    scratch = [pltpu.VMEM((KVH, HEAD_SIZE, LANES), jnp.float32)]
    shape, out_spec = (TOKM, WIDTH), vmem
    if carried is None:
        shape = (KVH * HEAD_SIZE, LANES)
    elif done is not None:
        shape, out_spec = (MB * TOKM, WIDTH), pl.BlockSpec(memory_space=pl.ANY)
        scratch += [pltpu.VMEM((TOKM, WIDTH), jnp.bfloat16), pltpu.SemaphoreType.DMA((2,))]
    return pl.pallas_call(
        functools.partial(pair_kernel, micro),
        out_shape=jax.ShapeDtypeStruct(shape, jnp.bfloat16),
        in_specs=[vmem] * (len(fixed) + len(middle) + len(kv)),
        out_specs=out_spec,
        scratch_shapes=scratch,
        compiler_params=pltpu.CompilerParams(vmem_limit_bytes=12 * 1024 * 1024),
        cost_estimate=pl.CostEstimate(
            flops=2 * 4 * HQ * TOKM * (PLEN + TOKM) * HEAD_SIZE,
            bytes_accessed=4 * 1024 * 1024,
            transcendentals=2 * HQ * TOKM * (PLEN + TOKM),
        ),
    )(*fixed, *middle, *kv)


def spread_prefix(prefix, is_owner, is_other_core, beside):
    half = PLEN // 2
    parts = math.prod(lax.axis_size(axis) for axis in PLANE)
    arrived = swap(prefix[half:], "c")
    zero = jnp.zeros((), jnp.bfloat16)
    mine = jnp.where(is_owner, prefix[:half], jnp.where(is_other_core, arrived, zero))
    pieces = lax.all_to_all(mine.reshape(parts, half // parts, -1), PLANE, 0, 0)
    piece = jnp.sum(pieces, axis=0)
    piece = piece + swap(piece, "zh")
    piece, beside = lax.optimization_barrier((piece, beside))
    copies = lax.axis_size("yl") * parts
    gathered = lax.all_to_all(jnp.broadcast_to(piece[None], (copies, *piece.shape)), SPREAD, 0, 0)
    gathered = gathered.reshape(lax.axis_size("yl"), -1, gathered.shape[2])
    return gathered, swap(gathered, "c"), beside


def local(queries, resp_kv, prefix_kv, owner, seg_len):
    at = {axis: lax.axis_index(axis) for axis in RESP}
    place = jnp.int32(0)
    for axis in RESP:
        place = place * lax.axis_size(axis) + at[axis]
    owner_here = lax.dynamic_index_in_dim(owner[0], at["p"], 0, keepdims=False)

    early, late = packed(queries[0], resp_kv[0])
    *kv, early_other = spread_prefix(
        prefix_kv[0], owner_here == place, owner_here == (place ^ 1), swap(early, "yl")
    )

    fixed = [(seg_len, early, early_other)]
    fixed.append((*fixed[0], late, swap(late, "yl")))
    hop = [(0, 3), (1, 2)]
    carried = [lax.ppermute(attend_pair(m, fixed[m], kv), SECTION, hop) for m in range(MB)]
    done = attend_pair(0, fixed[0], kv, carried[0])
    return attend_pair(1, fixed[1], kv, carried[1], done)[None]


def solution(mesh):
    fine = Mesh(mesh.devices.reshape(2, 2, PROMPTS, 2, 2, 4, 2), SECTION + RESP)
    return jax.shard_map(
        local,
        mesh=fine,
        in_specs=(
            P(SECTION, RESP, None),
            P(SECTION, RESP, None),
            P(SECTION, RESP, None),
            P(SECTION, None),
            P(RESP, None),
        ),
        out_specs=P(SECTION, RESP, None),
        check_vma=False,
    )
```

time: 80.1 us -> 79 us (0.986)
  waiting for transfers between devices: 24.9 us -> 19.2 us
  starting transfers between devices: 18.2 us -> 23.5 us
  local copies, waits for them, and re-layouts: 0.14 us -> 1.88 us
  between operations: 2.79 us -> 1.48 us
  blocking collectives: 20.1 us -> 18.8 us
    ppermute x3 -> x5, starting transfers between devices: 9.73 us -> 15.2 us  [swap(): return lax.ppermute(x, axis, [(0, 1), (1, 0)])]
    all_to_all x1, waiting for transfers between devices: 11.3 us -> 7.22 us  [spread_prefix(): pieces = lax.all_to_all(mine.reshape(parts, half // parts, -1), PLANE, 0, 0)]
    ppermute x3 -> x5, waiting for transfers between devices: 5.22 us -> 3.57 us  [swap(): return lax.ppermute(x, axis, [(0, 1), (1, 0)])]
    all_to_all x1, blocking collectives: 20.1 us -> 18.8 us  [spread_prefix(): lax.all_to_all(jnp.broadcast_to(piece[None], (copies, *piece.shape)), SPR...]
    slice x0 -> x1, local copies, waits for them, and re-layouts: none -> 1.16 us  [spread_prefix(): arrived = swap(prefix[half:], 'c')]
    select_n x1, other arithmetic: 0.01 us -> 0.85 us  [spread_prefix(): jnp.where(is_owner, prefix[:half], jnp.where(is_other_core, arrived, zero))]
  transfers between devices with their start and end apart: 6 -> 8, of which waited for: 5 -> 5; matrix products, arithmetic and copies ran while one was open for 1% -> 1% of each run, Pallas kernels for 8% -> 11%
where the time goes in v4:
time: 79 us; the launch traced here: 78.5 us
  starting transfers between devices  23.5 us (30%)
  waiting for transfers between devices  19.2 us (24%)
  blocking collectives  18.8 us (24%)
  Pallas kernels  12.7 us (16%)
  local copies, waits for them, and re-layouts  1.88 us (2%)
  between operations  1.48 us (2%)
  other arithmetic  0.95 us (1%)
    all_to_all x1, blocking collectives, spread_prefix(): lax.all_to_all(jnp.broadcast_to(piece[None], (copies, *piece.shape)), SPR...  18.8 us
    ppermute x5, starting transfers between devices, swap(): return lax.ppermute(x, axis, [(0, 1), (1, 0)])  15.2 us
    pallas_call x4, Pallas kernels, attend_pair(): pl.pallas_call(functools.partial(pair_kernel, micro), out_shape=jax.Shape...  12.5 us
    ppermute x2, waiting for transfers between devices, local(): lax.ppermute(attend_pair(m, fixed[m], kv), SECTION, hop)  8.45 us
    all_to_all x1, waiting for transfers between devices, spread_prefix(): pieces = lax.all_to_all(mine.reshape(parts, half // parts, -1), PLANE, 0, 0)  7.22 us
    all_to_all x1, starting transfers between devices, spread_prefix(): pieces = lax.all_to_all(mine.reshape(parts, half // parts, -1), PLANE, 0, 0)  5.79 us
    ppermute x5, waiting for transfers between devices, swap(): return lax.ppermute(x, axis, [(0, 1), (1, 0)])  3.57 us
    ppermute x2, starting transfers between devices, local(): lax.ppermute(attend_pair(m, fixed[m], kv), SECTION, hop)  2.58 us
  transfers between devices with their start and end apart: 8, of which 5 were waited for; matrix products, arithmetic and copies ran while one was open for 1% of the time, Pallas kernels for 11%

profile of v4, /device:TPU:24, one launch (start us, length us, event | category | flops | bytes accessed | tf_op | source)
XLA Modules:
  0.0 78.5 jit_solution(12898866158474212047)
XLA Ops:
  0.0 0.0 copy-start
  0.0 0.0 copy-start.4
  0.0 1.2 %slice_bitcast_fusion = bf16[256,1024]{1,0:T(8,128)(2,1)S(1)} fusion(bf16[1,512,1024]{2,1,0:T(8,128)(2,1)} %param.7), kind=kLoop, calls=%fused_computation.1 | loop fusion | bytes 1048576 | tf_op jit(solution)/shard_map/slice | solution.py:217
  1.2 1.9 %collective-permute-start = (bf16[256,1024]{1,0:T(8,128)(2,1)S(1)}, bf16[256,1024]{1,0:T(8,128)(2,1)S(1)}, u32[]{:S(2)}, u32[]{:S(2)}) collective-permute-start(bf16[256,1024]{1,0:T(8,128)(2,1)S(1)} %slice_bitcast_fusion), channel_id=1, source_target_pairs={{0,1},{1,0},{2,3},{3,2},{4,5},{5,4},{6,7},{7,6},{8,9},{9,8},{10,11... | collective-permute-start | bytes 1572872 | tf_op jit(solution)/shard_map/ppermute | solution.py:34
  3.1 0.0 copy-done
  3.1 0.6 constant_dynamic-slice_fusion
  5.0 0.0 collective-permute-done
  5.0 0.0 copy-done.4
  5.0 0.9 %bitcast_select_fusion = bf16[256,1024]{1,0:T(8,128)(2,1)} fusion(bf16[256,1024]{1,0:T(8,128)(2,1)S(1)} %collective-permute-done, bf16[1,512,1024]{2,1,0:T(8,128)(2,1)S(1)} %copy-done.4, pred[]{:T(512)S(6)} %eq.7, pred[]{:T(512)S(6)} %eq.6), kind=kLoop, calls=%fused_computation | loop fusion | flops 524288 | bytes 1572866 | tf_op jit(solution)/shard_map/jit(_where)/select_n | solution.py:219
  5.9 0.0 copy-start.1
  5.9 0.0 copy-start.2
  5.9 5.8 %all-to-all-start = ((bf16[8,32,1024]{2,1,0:T(8,128)(2,1)}), bf16[8,32,1024]{2,1,0:T(8,128)(2,1)S(1)}, u32[]{:S(2)}, u32[]{:S(2)}) async-start(bf16[8,32,1024]{2,1,0:T(8,128)(2,1)} %bitcast.5), calls=%async_computation | async-start | bytes 1048576 | tf_op jit(solution)/shard_map/all_to_all | solution.py:220
  11.7 0.0 copy-done.1
  11.7 0.0 copy-done.2
  11.7 0.2 shard_map.55
  11.9 2.7 %collective-permute-start.2 = (bf16[1024,256]{1,0:T(8,128)(2,1)S(1)}, bf16[1024,256]{1,0:T(8,128)(2,1)S(1)}, u32[]{:S(2)}, u32[]{:S(2)}) collective-permute-start(bf16[1024,256]{1,0:T(8,128)(2,1)S(1)} %get-tuple-element.9.own_ref), channel_id=1, source_target_pairs={{0,128},{128,0},{1,129},{129,1},{2,130},{130,2},{3,131},{131,3},{4... | collective-permute-start | bytes 1572872 | tf_op jit(solution)/shard_map/ppermute | solution.py:34
  14.5 7.2 %all-to-all-done = bf16[8,32,1024]{2,1,0:T(8,128)(2,1)S(1)} async-done(((bf16[8,32,1024]{2,1,0:T(8,128)(2,1)}), bf16[8,32,1024]{2,1,0:T(8,128)(2,1)S(1)}, u32[]{:S(2)}, u32[]{:S(2)}) %all-to-all-start) | async-done | bytes 524320 | tf_op jit(solution)/shard_map/all_to_all | solution.py:220
  21.8 0.1 reduce_sum.12
  21.8 5.2 %collective-permute-start.1 = (bf16[32,1024]{1,0:T(8,128)(2,1)S(1)}, bf16[32,1024]{1,0:T(8,128)(2,1)S(1)}, u32[]{:S(2)}, u32[]{:S(2)}) collective-permute-start(bf16[32,1024]{1,0:T(8,128)(2,1)S(1)} %reduce_sum.12), channel_id=1, source_target_pairs={{0,16},{16,0},{1,17},{17,1},{2,18},{18,2},{3,19},{19,3},{4,20},{20... | collective-permute-start | bytes 196616 | tf_op jit(solution)/shard_map/ppermute | solution.py:34
  27.0 3.4 %collective-permute-done.1 = bf16[32,1024]{1,0:T(8,128)(2,1)S(1)} collective-permute-done((bf16[32,1024]{1,0:T(8,128)(2,1)S(1)}, bf16[32,1024]{1,0:T(8,128)(2,1)S(1)}, u32[]{:S(2)}, u32[]{:S(2)}) %collective-permute-start.1) | collective-permute-done | bytes 65568 | tf_op jit(solution)/shard_map/ppermute | solution.py:34
  30.4 0.0 collective-permute-done.2.other_ref
  30.4 0.1 broadcast_in_dim.14
  30.5 18.8 %all_to_all.10 = bf16[16,32,1024]{2,1,0:T(8,128)(2,1)S(1)} all-to-all(bf16[16,32,1024]{2,1,0:T(8,128)(2,1)S(1)} %broadcast_in_dim.14), channel_id=1, replica_groups=mesh['yh'=2,'yl'=2,'p'=4,'zh'=2,'zl'=2,'x'=4,'c'=2] {'yl','zl','x'}, dimensions={0} | all-to-all | bytes 2097152 | tf_op jit(solution)/shard_map/all_to_all | solution.py:225
  49.3 0.0 copy-start.3
  49.3 2.0 %collective-permute-start.4 = (bf16[2,256,1024]{2,1,0:T(8,128)(2,1)S(1)}, bf16[2,256,1024]{2,1,0:T(8,128)(2,1)S(1)}, u32[]{:S(2)}, u32[]{:S(2)}) collective-permute-start(bf16[2,256,1024]{2,1,0:T(8,128)(2,1)S(1)} %bitcast.10), channel_id=1, source_target_pairs={{0,1},{1,0},{2,3},{3,2},{4,5},{5,4},{6,7},{7,6},{8,9},{9,8},{10,11... | collective-permute-start | bytes 3145736 | tf_op jit(solution)/shard_map/ppermute | solution.py:34
  51.4 3.4 %collective-permute-start.3 = (bf16[256,256]{1,0:T(8,128)(2,1)S(1)}, bf16[256,256]{1,0:T(8,128)(2,1)S(1)}, u32[]{:S(2)}, u32[]{:S(2)}) collective-permute-start(bf16[256,256]{1,0:T(8,128)(2,1)S(1)} %get-tuple-element.11.refs_0_), channel_id=1, source_target_pairs={{0,128},{128,0},{1,129},{129,1},{2,130},{130,2},{3,131},{131,3},{4... | collective-permute-start | bytes 393224 | tf_op jit(solution)/shard_map/ppermute | solution.py:34
  54.7 0.0 collective-permute-done.4.refs_3_.refs_1_.refs_2_.refs_5_
  54.7 0.0 copy-done.3
  54.8 2.9 %shard_map.57 = bf16[512,256]{1,0:T(8,128)(2,1)S(1)} custom-call(s32[2,4]{1,0:T(2,128)S(1)} %copy-done.3, bf16[1024,256]{1,0:T(8,128)(2,1)S(1)} %get-tuple-element.9.own_ref, bf16[1024,256]{1,0:T(8,128)(2,1)S(1)} %collective-permute-done.2.other_ref, bf16[2,256,1024]{2,1,0:T(8,128)(2,1)S(1)} %bitcast.11, ...), custom_call_target="tpu_custom_call" | custom-call | flops 570425344 | bytes 4194304 | tf_op jit(solution)/shard_map/pallas_call | solution.py:199
  57.6 1.3 %collective-permute-start.6 = (bf16[512,256]{1,0:T(8,128)(2,1)S(1)}, bf16[512,256]{1,0:T(8,128)(2,1)S(1)}, u32[]{:S(2)}, u32[]{:S(2)}) collective-permute-start(bf16[512,256]{1,0:T(8,128)(2,1)S(1)} %shard_map.57), channel_id=1, source_target_pairs={{0,384},{128,256},{1,385},{129,257},{2,386},{130,258},{3,387},{131... | collective-permute-start | bytes 786440 | tf_op jit(solution)/shard_map/ppermute | solution.py:245
  58.9 0.2 collective-permute-done.3.refs_1_
  59.1 2.9 %shard_map.56 = bf16[512,256]{1,0:T(8,128)(2,1)S(1)} custom-call(s32[2,4]{1,0:T(2,128)S(1)} %copy-done.3, bf16[1024,256]{1,0:T(8,128)(2,1)S(1)} %get-tuple-element.9.own_ref, bf16[1024,256]{1,0:T(8,128)(2,1)S(1)} %collective-permute-done.2.other_ref, bf16[256,256]{1,0:T(8,128)(2,1)S(1)} %get-tuple-element.11.refs_0_, ...), custom_call_target="tpu_custom_call" | custom-call | flops 570425344 | bytes 4194304 | tf_op jit(solution)/shard_map/pallas_call | solution.py:199
  62.0 1.3 %collective-permute-start.5 = (bf16[512,256]{1,0:T(8,128)(2,1)S(1)}, bf16[512,256]{1,0:T(8,128)(2,1)S(1)}, u32[]{:S(2)}, u32[]{:S(2)}) collective-permute-start(bf16[512,256]{1,0:T(8,128)(2,1)S(1)} %shard_map.56), channel_id=1, source_target_pairs={{0,384},{128,256},{1,385},{129,257},{2,386},{130,258},{3,387},{131... | collective-permute-start | bytes 786440 | tf_op jit(solution)/shard_map/ppermute | solution.py:245
  63.3 6.5 %collective-permute-done.6.refs_0_ = bf16[512,256]{1,0:T(8,128)(2,1)S(1)} collective-permute-done((bf16[512,256]{1,0:T(8,128)(2,1)S(1)}, bf16[512,256]{1,0:T(8,128)(2,1)S(1)}, u32[]{:S(2)}, u32[]{:S(2)}) %collective-permute-start.6) | collective-permute-done | bytes 262176 | tf_op jit(solution)/shard_map/ppermute | solution.py:245
  69.9 3.0 %shard_map.58.refs_3_ = bf16[32,4096]{1,0:T(8,128)(2,1)S(1)} custom-call(s32[2,4]{1,0:T(2,128)S(1)} %copy-done.3, bf16[1024,256]{1,0:T(8,128)(2,1)S(1)} %get-tuple-element.9.own_ref, bf16[1024,256]{1,0:T(8,128)(2,1)S(1)} %collective-permute-done.2.other_ref, bf16[512,256]{1,0:T(8,128)(2,1)S(1)} %collective-permute-done.6.refs_0_, ...), custom_call_target="tpu_custom_call" | custom-call | flops 570425344 | bytes 4194304 | tf_op jit(solution)/shard_map/pallas_call | solution.py:199
  72.9 1.9 %collective-permute-done.5.refs_2_ = bf16[512,256]{1,0:T(8,128)(2,1)S(1)} collective-permute-done((bf16[512,256]{1,0:T(8,128)(2,1)S(1)}, bf16[512,256]{1,0:T(8,128)(2,1)S(1)}, u32[]{:S(2)}, u32[]{:S(2)}) %collective-permute-start.5) | collective-permute-done | bytes 262176 | tf_op jit(solution)/shard_map/ppermute | solution.py:245
  74.8 3.7 %shard_map.59 = bf16[64,4096]{1,0:T(8,128)(2,1)} custom-call(s32[2,4]{1,0:T(2,128)S(1)} %copy-done.3, bf16[1024,256]{1,0:T(8,128)(2,1)S(1)} %get-tuple-element.9.own_ref, bf16[1024,256]{1,0:T(8,128)(2,1)S(1)} %collective-permute-done.2.other_ref, bf16[256,256]{1,0:T(8,128)(2,1)S(1)} %get-tuple-element.11.refs_0_, ...), custom_call_target="tpu_custom_call" | custom-call | flops 570425344 | bytes 4194304 | tf_op jit(solution)/shard_map/pallas_call | solution.py:199
  (1 shorter events, 0.0 us)
Async XLA Ops:
  0.0 3.1 %copy-start = (s32[1,4]{1,0:T(1,128)S(1)}, s32[1,4]{1,0:T(1,128)}, u32[]{:S(2)}) copy-start(s32[1,4]{1,0:T(1,128)} %param.8) | copy-start | bytes 52
  0.0 5.0 %copy-start.4 = (bf16[1,512,1024]{2,1,0:T(8,128)(2,1)S(1)}, bf16[1,512,1024]{2,1,0:T(8,128)(2,1)}, u32[]{:S(2)}) copy-start(bf16[1,512,1024]{2,1,0:T(8,128)(2,1)} %param.7) | copy-start | bytes 3145732
  1.2 3.8 %collective-permute-start = (bf16[256,1024]{1,0:T(8,128)(2,1)S(1)}, bf16[256,1024]{1,0:T(8,128)(2,1)S(1)}, u32[]{:S(2)}, u32[]{:S(2)}) collective-permute-start(bf16[256,1024]{1,0:T(8,128)(2,1)S(1)} %slice_bitcast_fusion), channel_id=1, source_target_pairs={{0,1},{1,0},{2,3},{3,2},{4,5},{5,4},{6,7},{7,6},{8,9},{9,8},{10,11... | collective-permute-start | bytes 1572872 | tf_op jit(solution)/shard_map/ppermute | solution.py:34
  5.9 5.8 %copy-start.1 = (bf16[1,64,4096]{2,1,0:T(8,128)(2,1)S(1)}, bf16[1,64,4096]{2,1,0:T(8,128)(2,1)}, u32[]{:S(2)}) copy-start(bf16[1,64,4096]{2,1,0:T(8,128)(2,1)} %param.5) | copy-start | bytes 1572868
  5.9 5.8 %copy-start.2 = (bf16[1,64,1024]{2,1,0:T(8,128)(2,1)S(1)}, bf16[1,64,1024]{2,1,0:T(8,128)(2,1)}, u32[]{:S(2)}) copy-start(bf16[1,64,1024]{2,1,0:T(8,128)(2,1)} %param.6) | copy-start | bytes 393220
  5.9 15.9 %all-to-all-start = ((bf16[8,32,1024]{2,1,0:T(8,128)(2,1)}), bf16[8,32,1024]{2,1,0:T(8,128)(2,1)S(1)}, u32[]{:S(2)}, u32[]{:S(2)}) async-start(bf16[8,32,1024]{2,1,0:T(8,128)(2,1)} %bitcast.5), calls=%async_computation | async-start | bytes 1048576 | tf_op jit(solution)/shard_map/all_to_all | solution.py:220
  11.9 18.5 %collective-permute-start.2 = (bf16[1024,256]{1,0:T(8,128)(2,1)S(1)}, bf16[1024,256]{1,0:T(8,128)(2,1)S(1)}, u32[]{:S(2)}, u32[]{:S(2)}) collective-permute-start(bf16[1024,256]{1,0:T(8,128)(2,1)S(1)} %get-tuple-element.9.own_ref), channel_id=1, source_target_pairs={{0,128},{128,0},{1,129},{129,1},{2,130},{130,2},{3,131},{131,3},{4... | collective-permute-start | bytes 1572872 | tf_op jit(solution)/shard_map/ppermute | solution.py:34
  21.8 8.5 %collective-permute-start.1 = (bf16[32,1024]{1,0:T(8,128)(2,1)S(1)}, bf16[32,1024]{1,0:T(8,128)(2,1)S(1)}, u32[]{:S(2)}, u32[]{:S(2)}) collective-permute-start(bf16[32,1024]{1,0:T(8,128)(2,1)S(1)} %reduce_sum.12), channel_id=1, source_target_pairs={{0,16},{16,0},{1,17},{17,1},{2,18},{18,2},{3,19},{19,3},{4,20},{20... | collective-permute-start | bytes 196616 | tf_op jit(solution)/shard_map/ppermute | solution.py:34
  49.3 5.4 %copy-start.3 = (s32[2,4]{1,0:T(2,128)S(1)}, s32[2,4]{1,0:T(2,128)}, u32[]{:S(2)}) copy-start(s32[2,4]{1,0:T(2,128)} %seg_ref.7) | copy-start | bytes 100
  49.3 5.4 %collective-permute-start.4 = (bf16[2,256,1024]{2,1,0:T(8,128)(2,1)S(1)}, bf16[2,256,1024]{2,1,0:T(8,128)(2,1)S(1)}, u32[]{:S(2)}, u32[]{:S(2)}) collective-permute-start(bf16[2,256,1024]{2,1,0:T(8,128)(2,1)S(1)} %bitcast.10), channel_id=1, source_target_pairs={{0,1},{1,0},{2,3},{3,2},{4,5},{5,4},{6,7},{7,6},{8,9},{9,8},{10,11... | collective-permute-start | bytes 3145736 | tf_op jit(solution)/shard_map/ppermute | solution.py:34
  51.4 7.8 %collective-permute-start.3 = (bf16[256,256]{1,0:T(8,128)(2,1)S(1)}, bf16[256,256]{1,0:T(8,128)(2,1)S(1)}, u32[]{:S(2)}, u32[]{:S(2)}) collective-permute-start(bf16[256,256]{1,0:T(8,128)(2,1)S(1)} %get-tuple-element.11.refs_0_), channel_id=1, source_target_pairs={{0,128},{128,0},{1,129},{129,1},{2,130},{130,2},{3,131},{131,3},{4... | collective-permute-start | bytes 393224 | tf_op jit(solution)/shard_map/ppermute | solution.py:34
  57.6 12.2 %collective-permute-start.6 = (bf16[512,256]{1,0:T(8,128)(2,1)S(1)}, bf16[512,256]{1,0:T(8,128)(2,1)S(1)}, u32[]{:S(2)}, u32[]{:S(2)}) collective-permute-start(bf16[512,256]{1,0:T(8,128)(2,1)S(1)} %shard_map.57), channel_id=1, source_target_pairs={{0,384},{128,256},{1,385},{129,257},{2,386},{130,258},{3,387},{131... | collective-permute-start | bytes 786440 | tf_op jit(solution)/shard_map/ppermute | solution.py:245
  62.0 12.8 %collective-permute-start.5 = (bf16[512,256]{1,0:T(8,128)(2,1)S(1)}, bf16[512,256]{1,0:T(8,128)(2,1)S(1)}, u32[]{:S(2)}, u32[]{:S(2)}) collective-permute-start(bf16[512,256]{1,0:T(8,128)(2,1)S(1)} %shard_map.56), channel_id=1, source_target_pairs={{0,384},{128,256},{1,385},{129,257},{2,386},{130,258},{3,387},{131... | collective-permute-start | bytes 786440 | tf_op jit(solution)/shard_map/ppermute | solution.py:245

commit v5 on v4

--- a/solution.py
+++ b/solution.py
@@ -107,7 +107,15 @@
     )(q, rkv)
 
 
-def pair_kernel(micro, seg_ref, own_ref, other_ref, *refs):
+def pair_kernel(micro, *refs):
+    pair_body(micro, *refs)
+
+
+def first_pair_kernel(micro, *refs):
+    pl.when(lax.axis_index("yh") == 0)(functools.partial(pair_body, micro, *refs))
+
+
+def pair_body(micro, seg_ref, own_ref, other_ref, *refs):
     late_refs, carried_ref, done_ref = (), None, None
     if micro == 1:
         *late_refs, refs = refs[0], refs[1], refs[2:]
@@ -197,7 +205,7 @@
         shape, out_spec = (MB * TOKM, WIDTH), pl.BlockSpec(memory_space=pl.ANY)
         scratch += [pltpu.VMEM((TOKM, WIDTH), jnp.bfloat16), pltpu.SemaphoreType.DMA((2,))]
     return pl.pallas_call(
-        functools.partial(pair_kernel, micro),
+        functools.partial(first_pair_kernel if carried is None else pair_kernel, micro),
         out_shape=jax.ShapeDtypeStruct(shape, jnp.bfloat16),
         in_specs=[vmem] * (len(fixed) + len(middle) + len(kv)),
         out_specs=out_spec,

time: 79 us -> 78.6 us (level)
  Pallas kernels: 12.7 us -> 6.93 us
  waiting for transfers between devices: 19.2 us -> 24.6 us
    pallas_call x4, Pallas kernels: 12.5 us -> 6.74 us  [attend_pair(): pl.pallas_call(functools.partial(first_pair_kernel if carried is None els...]
    ppermute x5, waiting for transfers between devices: 3.57 us -> 6.43 us  [swap(): return lax.ppermute(x, axis, [(0, 1), (1, 0)])]
    ppermute x2, waiting for transfers between devices: 8.45 us -> 11 us  [local(): lax.ppermute(attend_pair(m, fixed[m], kv), SECTION, hop)]
  transfers between devices with their start and end apart: 8 -> 8, of which waited for: 5 -> 5; matrix products, arithmetic and copies ran while one was open for 1% -> 1% of each run, Pallas kernels for 11% -> 4%
where the time goes in v5:
time: 78.6 us; the launch traced here: 78.1 us
  waiting for transfers between devices  24.6 us (31%)
  starting transfers between devices  23.5 us (30%)
  blocking collectives  18.8 us (24%)
  Pallas kernels  6.93 us (9%)
  local copies, waits for them, and re-layouts  1.88 us (2%)
  between operations  1.47 us (2%)
  other arithmetic  0.95 us (1%)
    all_to_all x1, blocking collectives, spread_prefix(): lax.all_to_all(jnp.broadcast_to(piece[None], (copies, *piece.shape)), SPR...  18.8 us
    ppermute x5, starting transfers between devices, swap(): return lax.ppermute(x, axis, [(0, 1), (1, 0)])  15.2 us
    ppermute x2, waiting for transfers between devices, local(): lax.ppermute(attend_pair(m, fixed[m], kv), SECTION, hop)  11 us
    all_to_all x1, waiting for transfers between devices, spread_prefix(): pieces = lax.all_to_all(mine.reshape(parts, half // parts, -1), PLANE, 0, 0)  7.22 us
    pallas_call x4, Pallas kernels, attend_pair(): pl.pallas_call(functools.partial(first_pair_kernel if carried is None els...  6.74 us
    ppermute x5, waiting for transfers between devices, swap(): return lax.ppermute(x, axis, [(0, 1), (1, 0)])  6.43 us
    all_to_all x1, starting transfers between devices, spread_prefix(): pieces = lax.all_to_all(mine.reshape(parts, half // parts, -1), PLANE, 0, 0)  5.79 us
    ppermute x2, starting transfers between devices, local(): lax.ppermute(attend_pair(m, fixed[m], kv), SECTION, hop)  2.57 us
  transfers between devices with their start and end apart: 8, of which 5 were waited for; matrix products, arithmetic and copies ran while one was open for 1% of the time, Pallas kernels for 4%

profile of v5, /device:TPU:24, one launch (start us, length us, event | category | flops | bytes accessed | tf_op | source)
XLA Modules:
  0.0 78.1 jit_solution(1245700957223635595)
XLA Ops:
  0.0 0.0 copy-start
  0.0 0.0 copy-start.4
  0.0 1.2 %slice_bitcast_fusion = bf16[256,1024]{1,0:T(8,128)(2,1)S(1)} fusion(bf16[1,512,1024]{2,1,0:T(8,128)(2,1)} %param.7), kind=kLoop, calls=%fused_computation.1 | loop fusion | bytes 1048576 | tf_op jit(solution)/shard_map/slice | solution.py:225
  1.2 1.9 %collective-permute-start = (bf16[256,1024]{1,0:T(8,128)(2,1)S(1)}, bf16[256,1024]{1,0:T(8,128)(2,1)S(1)}, u32[]{:S(2)}, u32[]{:S(2)}) collective-permute-start(bf16[256,1024]{1,0:T(8,128)(2,1)S(1)} %slice_bitcast_fusion), channel_id=1, source_target_pairs={{0,1},{1,0},{2,3},{3,2},{4,5},{5,4},{6,7},{7,6},{8,9},{9,8},{10,11... | collective-permute-start | bytes 1572872 | tf_op jit(solution)/shard_map/ppermute | solution.py:34
  3.1 0.0 copy-done
  3.1 0.6 constant_dynamic-slice_fusion
  5.0 0.0 collective-permute-done
  5.0 0.0 copy-done.4
  5.0 0.9 %bitcast_select_fusion = bf16[256,1024]{1,0:T(8,128)(2,1)} fusion(bf16[256,1024]{1,0:T(8,128)(2,1)S(1)} %collective-permute-done, bf16[1,512,1024]{2,1,0:T(8,128)(2,1)S(1)} %copy-done.4, pred[]{:T(512)S(6)} %eq.7, pred[]{:T(512)S(6)} %eq.6), kind=kLoop, calls=%fused_computation | loop fusion | flops 524288 | bytes 1572866 | tf_op jit(solution)/shard_map/jit(_where)/select_n | solution.py:227
  5.9 0.0 copy-start.1
  5.9 0.0 copy-start.2
  5.9 5.8 %all-to-all-start = ((bf16[8,32,1024]{2,1,0:T(8,128)(2,1)}), bf16[8,32,1024]{2,1,0:T(8,128)(2,1)S(1)}, u32[]{:S(2)}, u32[]{:S(2)}) async-start(bf16[8,32,1024]{2,1,0:T(8,128)(2,1)} %bitcast.5), calls=%async_computation | async-start | bytes 1048576 | tf_op jit(solution)/shard_map/all_to_all | solution.py:228
  11.7 0.0 copy-done.1
  11.7 0.0 copy-done.2
  11.7 0.2 shard_map.55
  11.9 2.7 %collective-permute-start.2 = (bf16[1024,256]{1,0:T(8,128)(2,1)S(1)}, bf16[1024,256]{1,0:T(8,128)(2,1)S(1)}, u32[]{:S(2)}, u32[]{:S(2)}) collective-permute-start(bf16[1024,256]{1,0:T(8,128)(2,1)S(1)} %get-tuple-element.9.refs_1_), channel_id=1, source_target_pairs={{0,128},{128,0},{1,129},{129,1},{2,130},{130,2},{3,131},{131,3},{4... | collective-permute-start | bytes 1572872 | tf_op jit(solution)/shard_map/ppermute | solution.py:34
  14.5 7.2 %all-to-all-done = bf16[8,32,1024]{2,1,0:T(8,128)(2,1)S(1)} async-done(((bf16[8,32,1024]{2,1,0:T(8,128)(2,1)}), bf16[8,32,1024]{2,1,0:T(8,128)(2,1)S(1)}, u32[]{:S(2)}, u32[]{:S(2)}) %all-to-all-start) | async-done | bytes 524320 | tf_op jit(solution)/shard_map/all_to_all | solution.py:228
  21.8 0.1 reduce_sum.12
  21.8 5.2 %collective-permute-start.1 = (bf16[32,1024]{1,0:T(8,128)(2,1)S(1)}, bf16[32,1024]{1,0:T(8,128)(2,1)S(1)}, u32[]{:S(2)}, u32[]{:S(2)}) collective-permute-start(bf16[32,1024]{1,0:T(8,128)(2,1)S(1)} %reduce_sum.12), channel_id=1, source_target_pairs={{0,16},{16,0},{1,17},{17,1},{2,18},{18,2},{3,19},{19,3},{4,20},{20... | collective-permute-start | bytes 196616 | tf_op jit(solution)/shard_map/ppermute | solution.py:34
  27.0 3.4 %collective-permute-done.1 = bf16[32,1024]{1,0:T(8,128)(2,1)S(1)} collective-permute-done((bf16[32,1024]{1,0:T(8,128)(2,1)S(1)}, bf16[32,1024]{1,0:T(8,128)(2,1)S(1)}, u32[]{:S(2)}, u32[]{:S(2)}) %collective-permute-start.1) | collective-permute-done | bytes 65568 | tf_op jit(solution)/shard_map/ppermute | solution.py:34
  30.4 0.0 collective-permute-done.2.refs_2_
  30.4 0.1 broadcast_in_dim.14
  30.5 18.8 %all_to_all.10 = bf16[16,32,1024]{2,1,0:T(8,128)(2,1)S(1)} all-to-all(bf16[16,32,1024]{2,1,0:T(8,128)(2,1)S(1)} %broadcast_in_dim.14), channel_id=1, replica_groups=mesh['yh'=2,'yl'=2,'p'=4,'zh'=2,'zl'=2,'x'=4,'c'=2] {'yl','zl','x'}, dimensions={0} | all-to-all | bytes 2097152 | tf_op jit(solution)/shard_map/all_to_all | solution.py:233
  49.3 0.0 copy-start.3
  49.3 2.0 %collective-permute-start.4 = (bf16[2,256,1024]{2,1,0:T(8,128)(2,1)S(1)}, bf16[2,256,1024]{2,1,0:T(8,128)(2,1)S(1)}, u32[]{:S(2)}, u32[]{:S(2)}) collective-permute-start(bf16[2,256,1024]{2,1,0:T(8,128)(2,1)S(1)} %bitcast.10), channel_id=1, source_target_pairs={{0,1},{1,0},{2,3},{3,2},{4,5},{5,4},{6,7},{7,6},{8,9},{9,8},{10,11... | collective-permute-start | bytes 3145736 | tf_op jit(solution)/shard_map/ppermute | solution.py:34
  51.4 3.4 %collective-permute-start.3 = (bf16[256,256]{1,0:T(8,128)(2,1)S(1)}, bf16[256,256]{1,0:T(8,128)(2,1)S(1)}, u32[]{:S(2)}, u32[]{:S(2)}) collective-permute-start(bf16[256,256]{1,0:T(8,128)(2,1)S(1)} %get-tuple-element.11.refs_3_), channel_id=1, source_target_pairs={{0,128},{128,0},{1,129},{129,1},{2,130},{130,2},{3,131},{131,3},{4... | collective-permute-start | bytes 393224 | tf_op jit(solution)/shard_map/ppermute | solution.py:34
  54.7 0.0 collective-permute-done.4.refs_6_.refs_4_.refs_5_.refs_8_
  54.7 0.0 copy-done.3
  54.8 1.3 %collective-permute-start.6 = (bf16[512,256]{1,0:T(8,128)(2,1)S(1)}, bf16[512,256]{1,0:T(8,128)(2,1)S(1)}, u32[]{:S(2)}, u32[]{:S(2)}) collective-permute-start(bf16[512,256]{1,0:T(8,128)(2,1)S(1)} %shard_map.57), channel_id=1, source_target_pairs={{0,384},{128,256},{1,385},{129,257},{2,386},{130,258},{3,387},{131... | collective-permute-start | bytes 786440 | tf_op jit(solution)/shard_map/ppermute | solution.py:253
  56.1 3.1 %collective-permute-done.3.refs_4_ = bf16[256,256]{1,0:T(8,128)(2,1)S(1)} collective-permute-done((bf16[256,256]{1,0:T(8,128)(2,1)S(1)}, bf16[256,256]{1,0:T(8,128)(2,1)S(1)}, u32[]{:S(2)}, u32[]{:S(2)}) %collective-permute-start.3) | collective-permute-done | bytes 131104 | tf_op jit(solution)/shard_map/ppermute | solution.py:34
  59.1 1.3 %collective-permute-start.5 = (bf16[512,256]{1,0:T(8,128)(2,1)S(1)}, bf16[512,256]{1,0:T(8,128)(2,1)S(1)}, u32[]{:S(2)}, u32[]{:S(2)}) collective-permute-start(bf16[512,256]{1,0:T(8,128)(2,1)S(1)} %shard_map.56), channel_id=1, source_target_pairs={{0,384},{128,256},{1,385},{129,257},{2,386},{130,258},{3,387},{131... | collective-permute-start | bytes 786440 | tf_op jit(solution)/shard_map/ppermute | solution.py:253
  60.4 8.8 %collective-permute-done.6.refs_3_ = bf16[512,256]{1,0:T(8,128)(2,1)S(1)} collective-permute-done((bf16[512,256]{1,0:T(8,128)(2,1)S(1)}, bf16[512,256]{1,0:T(8,128)(2,1)S(1)}, u32[]{:S(2)}, u32[]{:S(2)}) %collective-permute-start.6) | collective-permute-done | bytes 262176 | tf_op jit(solution)/shard_map/ppermute | solution.py:253
  69.2 3.0 %shard_map.58.refs_6_ = bf16[32,4096]{1,0:T(8,128)(2,1)S(1)} custom-call(s32[2,4]{1,0:T(2,128)S(1)} %copy-done.3, bf16[1024,256]{1,0:T(8,128)(2,1)S(1)} %get-tuple-element.9.refs_1_, bf16[1024,256]{1,0:T(8,128)(2,1)S(1)} %collective-permute-done.2.refs_2_, bf16[512,256]{1,0:T(8,128)(2,1)S(1)} %collective-permute-done.6.refs_3_, ...), custom_call_target="tpu_custom_call" | custom-call | flops 570425344 | bytes 4194304 | tf_op jit(solution)/shard_map/pallas_call | solution.py:207
  72.3 2.1 %collective-permute-done.5.refs_5_ = bf16[512,256]{1,0:T(8,128)(2,1)S(1)} collective-permute-done((bf16[512,256]{1,0:T(8,128)(2,1)S(1)}, bf16[512,256]{1,0:T(8,128)(2,1)S(1)}, u32[]{:S(2)}, u32[]{:S(2)}) %collective-permute-start.5) | collective-permute-done | bytes 262176 | tf_op jit(solution)/shard_map/ppermute | solution.py:253
  74.4 3.7 %shard_map.59 = bf16[64,4096]{1,0:T(8,128)(2,1)} custom-call(s32[2,4]{1,0:T(2,128)S(1)} %copy-done.3, bf16[1024,256]{1,0:T(8,128)(2,1)S(1)} %get-tuple-element.9.refs_1_, bf16[1024,256]{1,0:T(8,128)(2,1)S(1)} %collective-permute-done.2.refs_2_, bf16[256,256]{1,0:T(8,128)(2,1)S(1)} %get-tuple-element.11.refs_3_, ...), custom_call_target="tpu_custom_call" | custom-call | flops 570425344 | bytes 4194304 | tf_op jit(solution)/shard_map/pallas_call | solution.py:207
  (3 shorter events, 0.0 us)
Async XLA Ops:
  0.0 3.1 %copy-start = (s32[1,4]{1,0:T(1,128)S(1)}, s32[1,4]{1,0:T(1,128)}, u32[]{:S(2)}) copy-start(s32[1,4]{1,0:T(1,128)} %param.8) | copy-start | bytes 52
  0.0 5.0 %copy-start.4 = (bf16[1,512,1024]{2,1,0:T(8,128)(2,1)S(1)}, bf16[1,512,1024]{2,1,0:T(8,128)(2,1)}, u32[]{:S(2)}) copy-start(bf16[1,512,1024]{2,1,0:T(8,128)(2,1)} %param.7) | copy-start | bytes 3145732
  1.2 3.8 %collective-permute-start = (bf16[256,1024]{1,0:T(8,128)(2,1)S(1)}, bf16[256,1024]{1,0:T(8,128)(2,1)S(1)}, u32[]{:S(2)}, u32[]{:S(2)}) collective-permute-start(bf16[256,1024]{1,0:T(8,128)(2,1)S(1)} %slice_bitcast_fusion), channel_id=1, source_target_pairs={{0,1},{1,0},{2,3},{3,2},{4,5},{5,4},{6,7},{7,6},{8,9},{9,8},{10,11... | collective-permute-start | bytes 1572872 | tf_op jit(solution)/shard_map/ppermute | solution.py:34
  5.9 5.8 %copy-start.1 = (bf16[1,64,4096]{2,1,0:T(8,128)(2,1)S(1)}, bf16[1,64,4096]{2,1,0:T(8,128)(2,1)}, u32[]{:S(2)}) copy-start(bf16[1,64,4096]{2,1,0:T(8,128)(2,1)} %param.5) | copy-start | bytes 1572868
  5.9 5.8 %copy-start.2 = (bf16[1,64,1024]{2,1,0:T(8,128)(2,1)S(1)}, bf16[1,64,1024]{2,1,0:T(8,128)(2,1)}, u32[]{:S(2)}) copy-start(bf16[1,64,1024]{2,1,0:T(8,128)(2,1)} %param.6) | copy-start | bytes 393220
  5.9 15.9 %all-to-all-start = ((bf16[8,32,1024]{2,1,0:T(8,128)(2,1)}), bf16[8,32,1024]{2,1,0:T(8,128)(2,1)S(1)}, u32[]{:S(2)}, u32[]{:S(2)}) async-start(bf16[8,32,1024]{2,1,0:T(8,128)(2,1)} %bitcast.5), calls=%async_computation | async-start | bytes 1048576 | tf_op jit(solution)/shard_map/all_to_all | solution.py:228
  11.9 18.5 %collective-permute-start.2 = (bf16[1024,256]{1,0:T(8,128)(2,1)S(1)}, bf16[1024,256]{1,0:T(8,128)(2,1)S(1)}, u32[]{:S(2)}, u32[]{:S(2)}) collective-permute-start(bf16[1024,256]{1,0:T(8,128)(2,1)S(1)} %get-tuple-element.9.refs_1_), channel_id=1, source_target_pairs={{0,128},{128,0},{1,129},{129,1},{2,130},{130,2},{3,131},{131,3},{4... | collective-permute-start | bytes 1572872 | tf_op jit(solution)/shard_map/ppermute | solution.py:34
  21.8 8.5 %collective-permute-start.1 = (bf16[32,1024]{1,0:T(8,128)(2,1)S(1)}, bf16[32,1024]{1,0:T(8,128)(2,1)S(1)}, u32[]{:S(2)}, u32[]{:S(2)}) collective-permute-start(bf16[32,1024]{1,0:T(8,128)(2,1)S(1)} %reduce_sum.12), channel_id=1, source_target_pairs={{0,16},{16,0},{1,17},{17,1},{2,18},{18,2},{3,19},{19,3},{4,20},{20... | collective-permute-start | bytes 196616 | tf_op jit(solution)/shard_map/ppermute | solution.py:34
  49.3 5.4 %copy-start.3 = (s32[2,4]{1,0:T(2,128)S(1)}, s32[2,4]{1,0:T(2,128)}, u32[]{:S(2)}) copy-start(s32[2,4]{1,0:T(2,128)} %refs_0_.7) | copy-start | bytes 100
  49.3 5.4 %collective-permute-start.4 = (bf16[2,256,1024]{2,1,0:T(8,128)(2,1)S(1)}, bf16[2,256,1024]{2,1,0:T(8,128)(2,1)S(1)}, u32[]{:S(2)}, u32[]{:S(2)}) collective-permute-start(bf16[2,256,1024]{2,1,0:T(8,128)(2,1)S(1)} %bitcast.10), channel_id=1, source_target_pairs={{0,1},{1,0},{2,3},{3,2},{4,5},{5,4},{6,7},{7,6},{8,9},{9,8},{10,11... | collective-permute-start | bytes 3145736 | tf_op jit(solution)/shard_map/ppermute | solution.py:34
  51.4 7.8 %collective-permute-start.3 = (bf16[256,256]{1,0:T(8,128)(2,1)S(1)}, bf16[256,256]{1,0:T(8,128)(2,1)S(1)}, u32[]{:S(2)}, u32[]{:S(2)}) collective-permute-start(bf16[256,256]{1,0:T(8,128)(2,1)S(1)} %get-tuple-element.11.refs_3_), channel_id=1, source_target_pairs={{0,128},{128,0},{1,129},{129,1},{2,130},{130,2},{3,131},{131,3},{4... | collective-permute-start | bytes 393224 | tf_op jit(solution)/shard_map/ppermute | solution.py:34
  54.8 14.5 %collective-permute-start.6 = (bf16[512,256]{1,0:T(8,128)(2,1)S(1)}, bf16[512,256]{1,0:T(8,128)(2,1)S(1)}, u32[]{:S(2)}, u32[]{:S(2)}) collective-permute-start(bf16[512,256]{1,0:T(8,128)(2,1)S(1)} %shard_map.57), channel_id=1, source_target_pairs={{0,384},{128,256},{1,385},{129,257},{2,386},{130,258},{3,387},{131... | collective-permute-start | bytes 786440 | tf_op jit(solution)/shard_map/ppermute | solution.py:253
  59.1 15.2 %collective-permute-start.5 = (bf16[512,256]{1,0:T(8,128)(2,1)S(1)}, bf16[512,256]{1,0:T(8,128)(2,1)S(1)}, u32[]{:S(2)}, u32[]{:S(2)}) collective-permute-start(bf16[512,256]{1,0:T(8,128)(2,1)S(1)} %shard_map.56), channel_id=1, source_target_pairs={{0,384},{128,256},{1,385},{129,257},{2,386},{130,258},{3,387},{131... | collective-permute-start | bytes 786440 | tf_op jit(solution)/shard_map/ppermute | solution.py:253

commit v6 on v4

v6 whole, which is shorter than its diff:
```python
import functools
import math

import jax
import jax.numpy as jnp
from jax import lax
from jax.experimental import pallas as pl
from jax.experimental.pallas import tpu as pltpu
from jax.sharding import Mesh, PartitionSpec as P

HQ = 32
KVH = 4
GROUP = HQ // KVH
HEAD_SIZE = 128
WIDTH = HQ * HEAD_SIZE
KVW = KVH * HEAD_SIZE
PLEN = 512
TOKM = 32
MB = 2
LANES = GROUP * TOKM
CHUNKS = 2 * KVW // LANES
PARTS = ((0, 0, 32), (1, 0, 16), (1, 16, 16))
RESPS = 4
PROMPTS = 4
EPS = 1e-06
EXP2_SCALE = math.log2(math.e) / math.sqrt(HEAD_SIZE)

SECTION = ("yh", "yl")
RESP = ("p", "zh", "zl", "x", "c")
PLANE = ("zl", "x")
SPREAD = ("yl", *PLANE)


def swap(x, axis):
    return lax.ppermute(x, axis, [(0, 1), (1, 0)])


def product(a, b, a_over, b_over):
    over = (((a_over,), (b_over,)), ((), ()))
    return lax.dot_general(a, b, over, preferred_element_type=jnp.float32)


def over_rows(reduce, blocks):
    pair = jnp.maximum if reduce is jnp.max else jnp.add
    wide = reduce(pair(blocks[0], blocks[1]), axis=0, keepdims=True)
    return pair(wide, reduce(blocks[2], axis=0, keepdims=True))


def over_heads(total, widths):
    sums, first = [], 0
    for width in widths:
        part = total[:, first : first + width]
        reach = width // GROUP
        while reach < width:
            part = part + pltpu.roll(part, reach, 1)
            reach *= 2
        sums.append(part)
        first += width
    return jnp.concatenate(sums, axis=1)


def attend(x, widths, keys, values, near_mask, att_ref):
    groups = range(KVH)
    lanes = x[0].shape[1]
    scores = [[product(k, x[g], 1, 0) for k in keys(g)] for g in groups]
    for g in groups:
        scores[g][2] = scores[g][2] + near_mask
    top = [over_rows(jnp.max, scores[g]) for g in groups]
    raised = [[jnp.exp2((s - top[g]) * EXP2_SCALE) for s in scores[g]] for g in groups]
    share = [1.0 / over_rows(jnp.sum, raised[g]) for g in groups]
    weights = [[(e * share[g]).astype(jnp.bfloat16) for e in raised[g]] for g in groups]
    total = jnp.zeros((1, lanes), jnp.float32)
    for g in groups:
        out = sum(product(v, w, 0, 0) for v, w in zip(values(g), weights[g], strict=True))
        att_ref[g] = out
        total = total + jnp.sum(out * out, axis=0, keepdims=True)
    scaling = lax.rsqrt(over_heads(total, widths) * (1.0 / WIDTH) + EPS)
    return [(att_ref[g] * scaling).astype(jnp.bfloat16) for g in groups]


def pack_kernel(q_ref, rkv_ref, early_ref, late_ref):
    for part, (micro, first, count) in enumerate(PARTS):
        out_ref = late_ref if part == len(PARTS) - 1 else early_ref
        rows = pl.ds(micro * TOKM + first, count)
        for g in range(KVH):
            heads = [
                q_ref[rows, h * HEAD_SIZE : (h + 1) * HEAD_SIZE]
                for h in range(g * GROUP, (g + 1) * GROUP)
            ]
            out_ref[query_block(part, g)] = jnp.concatenate(heads, axis=0).T
    for micro in range(MB):
        rows = pl.ds(micro * TOKM, TOKM)
        for chunk in range(CHUNKS):
            early_ref[near_block(micro, chunk)] = rkv_ref[rows, chunk * LANES : (chunk + 1) * LANES]


def query_block(part, g):
    lanes = GROUP * PARTS[part][2]
    beside = LANES // lanes
    first = 0
    if part < len(PARTS) - 1:
        first = sum(KVH * GROUP * count * HEAD_SIZE // LANES for _, _, count in PARTS[:part])
    first += g // beside * HEAD_SIZE
    lane = g % beside * lanes
    return slice(first, first + HEAD_SIZE), slice(lane, lane + lanes)


def near_block(micro, chunk):
    first = query_block(len(PARTS) - 2, KVH - 1)[0].stop + (micro * CHUNKS + chunk) * TOKM
    return slice(first, first + TOKM), slice(None)


def packed(q, rkv):
    vmem = pl.BlockSpec(memory_space=pltpu.VMEM)
    sizes = near_block(MB - 1, CHUNKS - 1)[0].stop, query_block(len(PARTS) - 1, KVH - 1)[0].stop
    return pl.pallas_call(
        pack_kernel,
        out_shape=tuple(jax.ShapeDtypeStruct((size, LANES), jnp.bfloat16) for size in sizes),
        in_specs=[vmem, vmem],
        out_specs=(vmem, vmem),
        compiler_params=pltpu.CompilerParams(vmem_limit_bytes=12 * 1024 * 1024),
        cost_estimate=pl.CostEstimate(flops=0, bytes_accessed=1280 * 1024, transcendentals=0),
    )(q, rkv)


def pair_kernel(parts, hopped, ready, seg_ref, own_ref, other_ref, *refs):
    micro = PARTS[parts[0]][0]
    widths = [GROUP * PARTS[part][2] for part in parts]
    late_refs = ()
    if micro > 0:
        late_refs, refs = refs[:2], refs[2:]
    second, pair = lax.axis_index("yl"), lax.axis_index("yh")

    def group_rows(g):
        return slice(g * HEAD_SIZE, (g + 1) * HEAD_SIZE)

    def both_layers(carried_ref, kv0_ref, kv1_ref, att_ref):
        at_key = lax.broadcasted_iota(jnp.int32, (TOKM, sum(widths)), 0)
        at_query = []
        for part, width in zip(parts, widths, strict=True):
            _, first_row, count = PARTS[part]
            lane = lax.broadcasted_iota(jnp.int32, (TOKM, width), 1)
            at_query.append(lane % count + first_row)
        at_query = jnp.concatenate(at_query, axis=1)
        of_key, of_query = jnp.zeros_like(at_key), jnp.zeros_like(at_query)
        end = jnp.zeros((1, 1), jnp.int32)
        for i in range(RESPS):
            end = end + seg_ref[micro : micro + 1, i : i + 1]
            of_key = of_key + (at_key >= end).astype(jnp.int32)
            of_query = of_query + (at_query >= end).astype(jnp.int32)
        allowed = (of_key == of_query) & (at_key <= at_query)
        near_mask = jnp.where(allowed, 0.0, -jnp.inf).astype(jnp.float32)

        outs = []
        for layer in range(2):
            is_own = second == layer

            def one_of_both(refs, block, is_own=is_own):
                own, other = (ref[block] for ref in refs)
                return jnp.where(is_own, own, other)

            x = []
            for g in range(KVH):
                query = []
                for part in parts:
                    query_refs = late_refs if part == len(PARTS) - 1 else (own_ref, other_ref)
                    query.append(one_of_both(query_refs, query_block(part, g)))
                query = jnp.concatenate(query, axis=1)
                if layer == 1:
                    query = query.astype(jnp.float32) + outs[0][g].astype(jnp.float32)
                elif carried_ref is not None:
                    query = query.astype(jnp.float32) + carried_ref[group_rows(g)].astype(jnp.float32)
                x.append(query.astype(jnp.bfloat16))

            def blocks(column, layer=layer, one_of_both=one_of_both):
                def of_group(g):
                    lanes = slice(column + g * HEAD_SIZE, column + (g + 1) * HEAD_SIZE)
                    rows, _ = near_block(micro, lanes.start // LANES)
                    inside = slice(lanes.start % LANES, lanes.start % LANES + HEAD_SIZE)
                    near = one_of_both((own_ref, other_ref), (rows, inside))
                    return [kv0_ref[layer, :, lanes], kv1_ref[layer, :, lanes], near]

                return of_group

            outs.append(attend(x, widths, blocks(0), blocks(KVW), near_mask, att_ref))
        return outs[1], [jnp.where(second == 0, *both) for both in zip(*outs, strict=True)]

    if not hopped:
        kv0_ref, kv1_ref, *out_refs, att_ref = refs

        @pl.when(pair == 0)
        def _():
            outs = both_layers(None, kv0_ref, kv1_ref, att_ref)
            first = 0
            for i, width in enumerate(widths):
                for ref, groups in zip(out_refs[2 * i : 2 * i + 2], outs, strict=True):
                    for g in range(KVH):
                        ref[group_rows(g)] = groups[g][:, first : first + width]
                first += width

        return

    carried_ref, kept_ref, *refs = refs
    ready_refs, refs = refs[:ready], refs[ready:]
    kv0_ref, kv1_ref, out_ref, att_ref, *own_copies = refs
    copies = []
    rows_ref = out_ref
    if own_copies:
        rows_ref, sems = own_copies
        first = 0
        for i, source in enumerate((*ready_refs, rows_ref)):
            here = out_ref.at[first : first + source.shape[0]]
            copies.append(pltpu.make_async_copy(source, here, sems.at[i]))
            first += source.shape[0]
        for copy in copies[:-1]:
            copy.start()

    def lay_out(groups):
        _, _, count = PARTS[parts[0]]
        for g in range(KVH):
            normed = groups[g].T
            for at in range(GROUP):
                h = g * GROUP + at
                rows_ref[:, h * HEAD_SIZE : (h + 1) * HEAD_SIZE] = normed[at * count : (at + 1) * count]

    @pl.when(pair == 0)
    def _():
        lay_out([kept_ref[group_rows(g)] for g in range(KVH)])

    @pl.when(pair != 0)
    def _():
        lay_out(both_layers(carried_ref, kv0_ref, kv1_ref, att_ref)[1])

    if copies:
        copies[-1].start()
        for copy in copies:
            copy.wait()


def attend_pair(parts, fixed, kv, carried=(), ready=()):
    vmem = pl.BlockSpec(memory_space=pltpu.VMEM)
    middle = [*carried, *ready]
    counts = [PARTS[part][2] for part in parts]
    count = sum(counts)
    scratch = [pltpu.VMEM((KVH, HEAD_SIZE, GROUP * count), jnp.float32)]
    shapes, out_specs = [(count, WIDTH)], [vmem]
    if not carried:
        shapes = [(KVH * HEAD_SIZE, GROUP * n) for n in counts for _ in range(2)]
        out_specs = [vmem] * len(shapes)
    elif ready:
        shapes, out_specs = [(MB * TOKM, WIDTH)], [pl.BlockSpec(memory_space=pl.ANY)]
        scratch += [pltpu.VMEM((count, WIDTH), jnp.bfloat16), pltpu.SemaphoreType.DMA((len(PARTS),))]
    return pl.pallas_call(
        functools.partial(pair_kernel, parts, bool(carried), len(ready)),
        out_shape=[jax.ShapeDtypeStruct(shape, jnp.bfloat16) for shape in shapes],
        in_specs=[vmem] * (len(fixed) + len(middle) + len(kv)),
        out_specs=out_specs,
        scratch_shapes=scratch,
        compiler_params=pltpu.CompilerParams(vmem_limit_bytes=12 * 1024 * 1024),
        cost_estimate=pl.CostEstimate(
            flops=1_600_000_000 + 50_000_000 * count,
            bytes_accessed=4 * 1024 * 1024,
            transcendentals=2 * HQ * count * (PLEN + TOKM),
        ),
    )(*fixed, *middle, *kv)


def spread_prefix(prefix, is_owner, is_other_core, beside):
    half = PLEN // 2
    parts = math.prod(lax.axis_size(axis) for axis in PLANE)
    arrived = swap(prefix[half:], "c")
    zero = jnp.zeros((), jnp.bfloat16)
    mine = jnp.where(is_owner, prefix[:half], jnp.where(is_other_core, arrived, zero))
    pieces = lax.all_to_all(mine.reshape(parts, half // parts, -1), PLANE, 0, 0)
    piece = jnp.sum(pieces, axis=0)
    piece = piece + swap(piece, "zh")
    piece, beside = lax.optimization_barrier((piece, beside))
    copies = lax.axis_size("yl") * parts
    gathered = lax.all_to_all(jnp.broadcast_to(piece[None], (copies, *piece.shape)), SPREAD, 0, 0)
    gathered = gathered.reshape(lax.axis_size("yl"), -1, gathered.shape[2])
    return gathered, swap(gathered, "c"), beside


def local(queries, resp_kv, prefix_kv, owner, seg_len):
    at = {axis: lax.axis_index(axis) for axis in RESP}
    place = jnp.int32(0)
    for axis in RESP:
        place = place * lax.axis_size(axis) + at[axis]
    owner_here = lax.dynamic_index_in_dim(owner[0], at["p"], 0, keepdims=False)

    early, late = packed(queries[0], resp_kv[0])
    *kv, early_other = spread_prefix(
        prefix_kv[0], owner_here == place, owner_here == (place ^ 1), swap(early, "yl")
    )

    fixed = [(seg_len, early, early_other)]
    fixed += [(*fixed[0], late, swap(late, "yl"))] * (len(PARTS) - 1)
    parts = range(len(PARTS))
    carried = []
    for micro in range(MB):
        together = tuple(i for i in parts if PARTS[i][0] == micro)
        outs = attend_pair(together, fixed[together[0]], kv)
        for last, kept in zip(outs[::2], outs[1::2], strict=True):
            carried.append((lax.ppermute(last, SECTION, [(0, 3), (1, 2)]), kept))
    ready = []
    for i in parts[:-1]:
        ready += attend_pair((i,), fixed[i], kv, carried[i])
        ready[i], carried[i + 1] = lax.optimization_barrier((ready[i], carried[i + 1]))
    return attend_pair((parts[-1],), fixed[-1], kv, carried[-1], ready)[0][None]


def solution(mesh):
    fine = Mesh(mesh.devices.reshape(2, 2, PROMPTS, 2, 2, 4, 2), SECTION + RESP)
    return jax.shard_map(
        local,
        mesh=fine,
        in_specs=(
            P(SECTION, RESP, None),
            P(SECTION, RESP, None),
            P(SECTION, RESP, None),
            P(SECTION, None),
            P(RESP, None),
        ),
        out_specs=P(SECTION, RESP, None),
        check_vma=False,
    )
```

time: 79 us -> 78.1 us (0.989)
  Pallas kernels: 12.7 us -> 8.5 us
  waiting for transfers between devices: 19.2 us -> 21.2 us
  starting transfers between devices: 23.5 us -> 24.8 us
    pallas_call x4 -> x5, Pallas kernels: 12.5 us -> 8.31 us  [attend_pair(): pl.pallas_call(functools.partial(pair_kernel, parts, bool(carried), len(r...]
    ppermute x5, waiting for transfers between devices: 3.57 us -> 6.43 us  [swap(): return lax.ppermute(x, axis, [(0, 1), (1, 0)])]
    ppermute x2 -> x3, starting transfers between devices: 2.58 us -> 3.86 us  [local(): carried.append((lax.ppermute(last, SECTION, [(0, 3), (1, 2)]), kept))]
    ppermute x2 -> x3, waiting for transfers between devices: 8.45 us -> 7.56 us  [local(): carried.append((lax.ppermute(last, SECTION, [(0, 3), (1, 2)]), kept))]
  transfers between devices with their start and end apart: 8 -> 9, of which waited for: 5 -> 4; matrix products, arithmetic and copies ran while one was open for 1% -> 1% of each run, Pallas kernels for 11% -> 7%
where the time goes in v6:
time: 78.1 us; the launch traced here: 77.6 us
  starting transfers between devices  24.8 us (32%)
  waiting for transfers between devices  21.2 us (27%)
  blocking collectives  18.8 us (24%)
  Pallas kernels  8.5 us (11%)
  local copies, waits for them, and re-layouts  1.88 us (2%)
  between operations  1.5 us (2%)
  other arithmetic  0.95 us (1%)
    all_to_all x1, blocking collectives, spread_prefix(): lax.all_to_all(jnp.broadcast_to(piece[None], (copies, *piece.shape)), SPR...  18.8 us
    ppermute x5, starting transfers between devices, swap(): return lax.ppermute(x, axis, [(0, 1), (1, 0)])  15.2 us
    pallas_call x5, Pallas kernels, attend_pair(): pl.pallas_call(functools.partial(pair_kernel, parts, bool(carried), len(r...  8.31 us
    ppermute x3, waiting for transfers between devices, local(): carried.append((lax.ppermute(last, SECTION, [(0, 3), (1, 2)]), kept))  7.56 us
    all_to_all x1, waiting for transfers between devices, spread_prefix(): pieces = lax.all_to_all(mine.reshape(parts, half // parts, -1), PLANE, 0, 0)  7.22 us
    ppermute x5, waiting for transfers between devices, swap(): return lax.ppermute(x, axis, [(0, 1), (1, 0)])  6.43 us
    all_to_all x1, starting transfers between devices, spread_prefix(): pieces = lax.all_to_all(mine.reshape(parts, half // parts, -1), PLANE, 0, 0)  5.79 us
    ppermute x3, starting transfers between devices, local(): carried.append((lax.ppermute(last, SECTION, [(0, 3), (1, 2)]), kept))  3.86 us
  transfers between devices with their start and end apart: 9, of which 4 were waited for; matrix products, arithmetic and copies ran while one was open for 1% of the time, Pallas kernels for 7%

profile of v6, /device:TPU:24, one launch (start us, length us, event | category | flops | bytes accessed | tf_op | source)
XLA Modules:
  0.0 77.6 jit_solution(7349153709720934923)
XLA Ops:
  0.0 0.0 copy-start
  0.0 0.0 copy-start.4
  0.0 1.2 %slice_bitcast_fusion = bf16[256,1024]{1,0:T(8,128)(2,1)S(1)} fusion(bf16[1,512,1024]{2,1,0:T(8,128)(2,1)} %param.7), kind=kLoop, calls=%fused_computation.1 | loop fusion | bytes 1048576 | tf_op jit(solution)/shard_map/slice | solution.py:271
  1.2 1.9 %collective-permute-start = (bf16[256,1024]{1,0:T(8,128)(2,1)S(1)}, bf16[256,1024]{1,0:T(8,128)(2,1)S(1)}, u32[]{:S(2)}, u32[]{:S(2)}) collective-permute-start(bf16[256,1024]{1,0:T(8,128)(2,1)S(1)} %slice_bitcast_fusion), channel_id=1, source_target_pairs={{0,1},{1,0},{2,3},{3,2},{4,5},{5,4},{6,7},{7,6},{8,9},{9,8},{10,11... | collective-permute-start | bytes 1572872 | tf_op jit(solution)/shard_map/ppermute | solution.py:35
  3.1 0.0 copy-done
  3.1 0.6 constant_dynamic-slice_fusion
  5.0 0.0 collective-permute-done
  5.0 0.0 copy-done.4
  5.0 0.9 %bitcast_select_fusion = bf16[256,1024]{1,0:T(8,128)(2,1)} fusion(bf16[256,1024]{1,0:T(8,128)(2,1)S(1)} %collective-permute-done, bf16[1,512,1024]{2,1,0:T(8,128)(2,1)S(1)} %copy-done.4, pred[]{:T(512)S(6)} %eq.7, pred[]{:T(512)S(6)} %eq.6), kind=kLoop, calls=%fused_computation | loop fusion | flops 524288 | bytes 1572866 | tf_op jit(solution)/shard_map/jit(_where)/select_n | solution.py:273
  5.9 0.0 copy-start.1
  5.9 0.0 copy-start.2
  5.9 5.8 %all-to-all-start = ((bf16[8,32,1024]{2,1,0:T(8,128)(2,1)}), bf16[8,32,1024]{2,1,0:T(8,128)(2,1)S(1)}, u32[]{:S(2)}, u32[]{:S(2)}) async-start(bf16[8,32,1024]{2,1,0:T(8,128)(2,1)} %bitcast.5), calls=%async_computation | async-start | bytes 1048576 | tf_op jit(solution)/shard_map/all_to_all | solution.py:274
  11.7 0.0 copy-done.1
  11.7 0.0 copy-done.2
  11.7 0.2 shard_map.55
  11.9 2.7 %collective-permute-start.2 = (bf16[1024,256]{1,0:T(8,128)(2,1)S(1)}, bf16[1024,256]{1,0:T(8,128)(2,1)S(1)}, u32[]{:S(2)}, u32[]{:S(2)}) collective-permute-start(bf16[1024,256]{1,0:T(8,128)(2,1)S(1)} %get-tuple-element.21.own_ref), channel_id=1, source_target_pairs={{0,128},{128,0},{1,129},{129,1},{2,130},{130,2},{3,131},{131,3},{4... | collective-permute-start | bytes 1572872 | tf_op jit(solution)/shard_map/ppermute | solution.py:35
  14.5 7.2 %all-to-all-done = bf16[8,32,1024]{2,1,0:T(8,128)(2,1)S(1)} async-done(((bf16[8,32,1024]{2,1,0:T(8,128)(2,1)}), bf16[8,32,1024]{2,1,0:T(8,128)(2,1)S(1)}, u32[]{:S(2)}, u32[]{:S(2)}) %all-to-all-start) | async-done | bytes 524320 | tf_op jit(solution)/shard_map/all_to_all | solution.py:274
  21.8 0.1 reduce_sum.12
  21.8 5.2 %collective-permute-start.1 = (bf16[32,1024]{1,0:T(8,128)(2,1)S(1)}, bf16[32,1024]{1,0:T(8,128)(2,1)S(1)}, u32[]{:S(2)}, u32[]{:S(2)}) collective-permute-start(bf16[32,1024]{1,0:T(8,128)(2,1)S(1)} %reduce_sum.12), channel_id=1, source_target_pairs={{0,16},{16,0},{1,17},{17,1},{2,18},{18,2},{3,19},{19,3},{4,20},{20... | collective-permute-start | bytes 196616 | tf_op jit(solution)/shard_map/ppermute | solution.py:35
  27.0 3.4 %collective-permute-done.1 = bf16[32,1024]{1,0:T(8,128)(2,1)S(1)} collective-permute-done((bf16[32,1024]{1,0:T(8,128)(2,1)S(1)}, bf16[32,1024]{1,0:T(8,128)(2,1)S(1)}, u32[]{:S(2)}, u32[]{:S(2)}) %collective-permute-start.1) | collective-permute-done | bytes 65568 | tf_op jit(solution)/shard_map/ppermute | solution.py:35
  30.4 0.0 collective-permute-done.2.other_ref
  30.4 0.1 broadcast_in_dim.14
  30.5 18.8 %all_to_all.10 = bf16[16,32,1024]{2,1,0:T(8,128)(2,1)S(1)} all-to-all(bf16[16,32,1024]{2,1,0:T(8,128)(2,1)S(1)} %broadcast_in_dim.14), channel_id=1, replica_groups=mesh['yh'=2,'yl'=2,'p'=4,'zh'=2,'zl'=2,'x'=4,'c'=2] {'yl','zl','x'}, dimensions={0} | all-to-all | bytes 2097152 | tf_op jit(solution)/shard_map/all_to_all | solution.py:279
  49.3 0.0 copy-start.3
  49.3 2.0 %collective-permute-start.4 = (bf16[2,256,1024]{2,1,0:T(8,128)(2,1)S(1)}, bf16[2,256,1024]{2,1,0:T(8,128)(2,1)S(1)}, u32[]{:S(2)}, u32[]{:S(2)}) collective-permute-start(bf16[2,256,1024]{2,1,0:T(8,128)(2,1)S(1)} %bitcast.10), channel_id=1, source_target_pairs={{0,1},{1,0},{2,3},{3,2},{4,5},{5,4},{6,7},{7,6},{8,9},{9,8},{10,11... | collective-permute-start | bytes 3145736 | tf_op jit(solution)/shard_map/ppermute | solution.py:35
  51.4 3.4 %collective-permute-start.3 = (bf16[256,256]{1,0:T(8,128)(2,1)S(1)}, bf16[256,256]{1,0:T(8,128)(2,1)S(1)}, u32[]{:S(2)}, u32[]{:S(2)}) collective-permute-start(bf16[256,256]{1,0:T(8,128)(2,1)S(1)} %get-tuple-element.23.refs_0_), channel_id=1, source_target_pairs={{0,128},{128,0},{1,129},{129,1},{2,130},{130,2},{3,131},{131,3},{4... | collective-permute-start | bytes 393224 | tf_op jit(solution)/shard_map/ppermute | solution.py:35
  54.7 0.0 collective-permute-done.4.refs_1_.refs_3_.refs_5_.refs_7_
  54.7 0.0 copy-done.3
  54.8 1.3 %collective-permute-start.5 = (bf16[512,256]{1,0:T(8,128)(2,1)S(1)}, bf16[512,256]{1,0:T(8,128)(2,1)S(1)}, u32[]{:S(2)}, u32[]{:S(2)}) collective-permute-start(bf16[512,256]{1,0:T(8,128)(2,1)S(1)} %get-tuple-element.25), channel_id=1, source_target_pairs={{0,384},{128,256},{1,385},{129,257},{2,386},{130,258},{3,387},{131... | collective-permute-start | bytes 786440 | tf_op jit(solution)/shard_map/ppermute | solution.py:304
  56.1 3.1 %collective-permute-done.3.refs_1_ = bf16[256,256]{1,0:T(8,128)(2,1)S(1)} collective-permute-done((bf16[256,256]{1,0:T(8,128)(2,1)S(1)}, bf16[256,256]{1,0:T(8,128)(2,1)S(1)}, u32[]{:S(2)}, u32[]{:S(2)}) %collective-permute-start.3) | collective-permute-done | bytes 131104 | tf_op jit(solution)/shard_map/ppermute | solution.py:35
  59.1 1.3 %collective-permute-start.6 = (bf16[512,128]{1,0:T(8,128)(2,1)S(1)}, bf16[512,128]{1,0:T(8,128)(2,1)S(1)}, u32[]{:S(2)}, u32[]{:S(2)}) collective-permute-start(bf16[512,128]{1,0:T(8,128)(2,1)S(1)} %get-tuple-element.27), channel_id=1, source_target_pairs={{0,384},{128,256},{1,385},{129,257},{2,386},{130,258},{3,387},{131... | collective-permute-start | bytes 393224 | tf_op jit(solution)/shard_map/ppermute | solution.py:304
  60.4 1.3 %collective-permute-start.7 = (bf16[512,128]{1,0:T(8,128)(2,1)S(1)}, bf16[512,128]{1,0:T(8,128)(2,1)S(1)}, u32[]{:S(2)}, u32[]{:S(2)}) collective-permute-start(bf16[512,128]{1,0:T(8,128)(2,1)S(1)} %get-tuple-element.31), channel_id=1, source_target_pairs={{0,384},{128,256},{1,385},{129,257},{2,386},{130,258},{3,387},{131... | collective-permute-start | bytes 393224 | tf_op jit(solution)/shard_map/ppermute | solution.py:304
  61.7 7.6 %collective-permute-done.5.refs_0_ = bf16[512,256]{1,0:T(8,128)(2,1)S(1)} collective-permute-done((bf16[512,256]{1,0:T(8,128)(2,1)S(1)}, bf16[512,256]{1,0:T(8,128)(2,1)S(1)}, u32[]{:S(2)}, u32[]{:S(2)}) %collective-permute-start.5) | collective-permute-done | bytes 262176 | tf_op jit(solution)/shard_map/ppermute | solution.py:304
  69.3 3.0 %shard_map.57.refs_4_ = bf16[32,4096]{1,0:T(8,128)(2,1)S(1)} custom-call(s32[2,4]{1,0:T(2,128)S(1)} %copy-done.3, bf16[1024,256]{1,0:T(8,128)(2,1)S(1)} %get-tuple-element.21.own_ref, bf16[1024,256]{1,0:T(8,128)(2,1)S(1)} %collective-permute-done.2.other_ref, bf16[512,256]{1,0:T(8,128)(2,1)S(1)} %collective-permute-done.5.refs_0_, ...), custom_call_target="tpu_custom_call" | custom-call | flops 3200000000 | bytes 4194304 | tf_op jit(solution)/shard_map/pallas_call | solution.py:253
  72.3 0.0 collective-permute-done.6.refs_2_
  72.3 2.3 %shard_map.59.refs_5_ = bf16[16,4096]{1,0:T(8,128)(2,1)S(1)} custom-call(s32[2,4]{1,0:T(2,128)S(1)} %copy-done.3, bf16[1024,256]{1,0:T(8,128)(2,1)S(1)} %get-tuple-element.21.own_ref, bf16[1024,256]{1,0:T(8,128)(2,1)S(1)} %collective-permute-done.2.other_ref, bf16[256,256]{1,0:T(8,128)(2,1)S(1)} %get-tuple-element.23.refs_0_, ...), custom_call_target="tpu_custom_call" | custom-call | flops 2400000000 | bytes 4194304 | tf_op jit(solution)/shard_map/pallas_call | solution.py:253
  74.6 0.0 collective-permute-done.7.refs_2_
  74.6 3.0 %shard_map.60 = bf16[64,4096]{1,0:T(8,128)(2,1)} custom-call(s32[2,4]{1,0:T(2,128)S(1)} %copy-done.3, bf16[1024,256]{1,0:T(8,128)(2,1)S(1)} %get-tuple-element.21.own_ref, bf16[1024,256]{1,0:T(8,128)(2,1)S(1)} %collective-permute-done.2.other_ref, bf16[256,256]{1,0:T(8,128)(2,1)S(1)} %get-tuple-element.23.refs_0_, ...), custom_call_target="tpu_custom_call" | custom-call | flops 2400000000 | bytes 4194304 | tf_op jit(solution)/shard_map/pallas_call | solution.py:253
  (3 shorter events, 0.0 us)
Async XLA Ops:
  0.0 3.1 %copy-start = (s32[1,4]{1,0:T(1,128)S(1)}, s32[1,4]{1,0:T(1,128)}, u32[]{:S(2)}) copy-start(s32[1,4]{1,0:T(1,128)} %param.8) | copy-start | bytes 52
  0.0 5.0 %copy-start.4 = (bf16[1,512,1024]{2,1,0:T(8,128)(2,1)S(1)}, bf16[1,512,1024]{2,1,0:T(8,128)(2,1)}, u32[]{:S(2)}) copy-start(bf16[1,512,1024]{2,1,0:T(8,128)(2,1)} %param.7) | copy-start | bytes 3145732
  1.2 3.8 %collective-permute-start = (bf16[256,1024]{1,0:T(8,128)(2,1)S(1)}, bf16[256,1024]{1,0:T(8,128)(2,1)S(1)}, u32[]{:S(2)}, u32[]{:S(2)}) collective-permute-start(bf16[256,1024]{1,0:T(8,128)(2,1)S(1)} %slice_bitcast_fusion), channel_id=1, source_target_pairs={{0,1},{1,0},{2,3},{3,2},{4,5},{5,4},{6,7},{7,6},{8,9},{9,8},{10,11... | collective-permute-start | bytes 1572872 | tf_op jit(solution)/shard_map/ppermute | solution.py:35
  5.9 5.8 %copy-start.1 = (bf16[1,64,4096]{2,1,0:T(8,128)(2,1)S(1)}, bf16[1,64,4096]{2,1,0:T(8,128)(2,1)}, u32[]{:S(2)}) copy-start(bf16[1,64,4096]{2,1,0:T(8,128)(2,1)} %param.5) | copy-start | bytes 1572868
  5.9 5.8 %copy-start.2 = (bf16[1,64,1024]{2,1,0:T(8,128)(2,1)S(1)}, bf16[1,64,1024]{2,1,0:T(8,128)(2,1)}, u32[]{:S(2)}) copy-start(bf16[1,64,1024]{2,1,0:T(8,128)(2,1)} %param.6) | copy-start | bytes 393220
  5.9 15.9 %all-to-all-start = ((bf16[8,32,1024]{2,1,0:T(8,128)(2,1)}), bf16[8,32,1024]{2,1,0:T(8,128)(2,1)S(1)}, u32[]{:S(2)}, u32[]{:S(2)}) async-start(bf16[8,32,1024]{2,1,0:T(8,128)(2,1)} %bitcast.5), calls=%async_computation | async-start | bytes 1048576 | tf_op jit(solution)/shard_map/all_to_all | solution.py:274
  11.9 18.5 %collective-permute-start.2 = (bf16[1024,256]{1,0:T(8,128)(2,1)S(1)}, bf16[1024,256]{1,0:T(8,128)(2,1)S(1)}, u32[]{:S(2)}, u32[]{:S(2)}) collective-permute-start(bf16[1024,256]{1,0:T(8,128)(2,1)S(1)} %get-tuple-element.21.own_ref), channel_id=1, source_target_pairs={{0,128},{128,0},{1,129},{129,1},{2,130},{130,2},{3,131},{131,3},{4... | collective-permute-start | bytes 1572872 | tf_op jit(solution)/shard_map/ppermute | solution.py:35
  21.8 8.5 %collective-permute-start.1 = (bf16[32,1024]{1,0:T(8,128)(2,1)S(1)}, bf16[32,1024]{1,0:T(8,128)(2,1)S(1)}, u32[]{:S(2)}, u32[]{:S(2)}) collective-permute-start(bf16[32,1024]{1,0:T(8,128)(2,1)S(1)} %reduce_sum.12), channel_id=1, source_target_pairs={{0,16},{16,0},{1,17},{17,1},{2,18},{18,2},{3,19},{19,3},{4,20},{20... | collective-permute-start | bytes 196616 | tf_op jit(solution)/shard_map/ppermute | solution.py:35
  49.3 5.4 %copy-start.3 = (s32[2,4]{1,0:T(2,128)S(1)}, s32[2,4]{1,0:T(2,128)}, u32[]{:S(2)}) copy-start(s32[2,4]{1,0:T(2,128)} %seg_ref.9) | copy-start | bytes 100
  49.3 5.4 %collective-permute-start.4 = (bf16[2,256,1024]{2,1,0:T(8,128)(2,1)S(1)}, bf16[2,256,1024]{2,1,0:T(8,128)(2,1)S(1)}, u32[]{:S(2)}, u32[]{:S(2)}) collective-permute-start(bf16[2,256,1024]{2,1,0:T(8,128)(2,1)S(1)} %bitcast.10), channel_id=1, source_target_pairs={{0,1},{1,0},{2,3},{3,2},{4,5},{5,4},{6,7},{7,6},{8,9},{9,8},{10,11... | collective-permute-start | bytes 3145736 | tf_op jit(solution)/shard_map/ppermute | solution.py:35
  51.4 7.8 %collective-permute-start.3 = (bf16[256,256]{1,0:T(8,128)(2,1)S(1)}, bf16[256,256]{1,0:T(8,128)(2,1)S(1)}, u32[]{:S(2)}, u32[]{:S(2)}) collective-permute-start(bf16[256,256]{1,0:T(8,128)(2,1)S(1)} %get-tuple-element.23.refs_0_), channel_id=1, source_target_pairs={{0,128},{128,0},{1,129},{129,1},{2,130},{130,2},{3,131},{131,3},{4... | collective-permute-start | bytes 393224 | tf_op jit(solution)/shard_map/ppermute | solution.py:35
  54.8 14.5 %collective-permute-start.5 = (bf16[512,256]{1,0:T(8,128)(2,1)S(1)}, bf16[512,256]{1,0:T(8,128)(2,1)S(1)}, u32[]{:S(2)}, u32[]{:S(2)}) collective-permute-start(bf16[512,256]{1,0:T(8,128)(2,1)S(1)} %get-tuple-element.25), channel_id=1, source_target_pairs={{0,384},{128,256},{1,385},{129,257},{2,386},{130,258},{3,387},{131... | collective-permute-start | bytes 786440 | tf_op jit(solution)/shard_map/ppermute | solution.py:304
  59.1 13.1 %collective-permute-start.6 = (bf16[512,128]{1,0:T(8,128)(2,1)S(1)}, bf16[512,128]{1,0:T(8,128)(2,1)S(1)}, u32[]{:S(2)}, u32[]{:S(2)}) collective-permute-start(bf16[512,128]{1,0:T(8,128)(2,1)S(1)} %get-tuple-element.27), channel_id=1, source_target_pairs={{0,384},{128,256},{1,385},{129,257},{2,386},{130,258},{3,387},{131... | collective-permute-start | bytes 393224 | tf_op jit(solution)/shard_map/ppermute | solution.py:304
  60.4 14.2 %collective-permute-start.7 = (bf16[512,128]{1,0:T(8,128)(2,1)S(1)}, bf16[512,128]{1,0:T(8,128)(2,1)S(1)}, u32[]{:S(2)}, u32[]{:S(2)}) collective-permute-start(bf16[512,128]{1,0:T(8,128)(2,1)S(1)} %get-tuple-element.31), channel_id=1, source_target_pairs={{0,384},{128,256},{1,385},{129,257},{2,386},{130,258},{3,387},{131... | collective-permute-start | bytes 393224 | tf_op jit(solution)/shard_map/ppermute | solution.py:304

commit v7 on v6

--- a/solution.py
+++ b/solution.py
@@ -27,7 +27,7 @@
 
 SECTION = ("yh", "yl")
 RESP = ("p", "zh", "zl", "x", "c")
-PLANE = ("zl", "x")
+PLANE = ("x", "zl")
 SPREAD = ("yl", *PLANE)
 
 

time: 78.1 us -> 77.3 us (0.990)
  waiting for transfers between devices: 21.2 us -> 22.2 us
  blocking collectives: 18.8 us -> 17.9 us
  starting transfers between devices: 24.8 us -> 23.9 us
    ppermute x5, starting transfers between devices: 15.2 us -> 14.3 us  [swap(): return lax.ppermute(x, axis, [(0, 1), (1, 0)])]
    all_to_all x1, blocking collectives: 18.8 us -> 17.9 us  [spread_prefix(): lax.all_to_all(jnp.broadcast_to(piece[None], (copies, *piece.shape)), SPR...]
  transfers between devices with their start and end apart: 9 -> 9, of which waited for: 4 -> 5; matrix products, arithmetic and copies ran while one was open for 1% -> 1% of each run, Pallas kernels for 7% -> 7%
where the time goes in v7:
time: 77.3 us; the launch traced here: 76.8 us
  starting transfers between devices  23.9 us (31%)
  waiting for transfers between devices  22.2 us (29%)
  blocking collectives  17.9 us (23%)
  Pallas kernels  8.48 us (11%)
  local copies, waits for them, and re-layouts  1.88 us (2%)
  between operations  1.48 us (2%)
  other arithmetic  0.95 us (1%)
    all_to_all x1, blocking collectives, spread_prefix(): lax.all_to_all(jnp.broadcast_to(piece[None], (copies, *piece.shape)), SPR...  17.9 us
    ppermute x5, starting transfers between devices, swap(): return lax.ppermute(x, axis, [(0, 1), (1, 0)])  14.3 us
    pallas_call x5, Pallas kernels, attend_pair(): pl.pallas_call(functools.partial(pair_kernel, parts, bool(carried), len(r...  8.3 us
    all_to_all x1, waiting for transfers between devices, spread_prefix(): pieces = lax.all_to_all(mine.reshape(parts, half // parts, -1), PLANE, 0, 0)  7.88 us
    ppermute x3, waiting for transfers between devices, local(): carried.append((lax.ppermute(last, SECTION, [(0, 3), (1, 2)]), kept))  7.37 us
    ppermute x5, waiting for transfers between devices, swap(): return lax.ppermute(x, axis, [(0, 1), (1, 0)])  6.96 us
    all_to_all x1, starting transfers between devices, spread_prefix(): pieces = lax.all_to_all(mine.reshape(parts, half // parts, -1), PLANE, 0, 0)  5.79 us
    ppermute x3, starting transfers between devices, local(): carried.append((lax.ppermute(last, SECTION, [(0, 3), (1, 2)]), kept))  3.85 us
  transfers between devices with their start and end apart: 9, of which 5 were waited for; matrix products, arithmetic and copies ran while one was open for 1% of the time, Pallas kernels for 7%

profile of v7, /device:TPU:24, one launch (start us, length us, event | category | flops | bytes accessed | tf_op | source)
XLA Modules:
  0.0 76.8 jit_solution(15281462481706670147)
XLA Ops:
  0.0 0.0 copy-start
  0.0 0.0 copy-start.4
  0.0 1.2 %slice_bitcast_fusion = bf16[256,1024]{1,0:T(8,128)(2,1)S(1)} fusion(bf16[1,512,1024]{2,1,0:T(8,128)(2,1)} %param.7), kind=kLoop, calls=%fused_computation.1 | loop fusion | bytes 1048576 | tf_op jit(solution)/shard_map/slice | solution.py:271
  1.2 1.9 %collective-permute-start = (bf16[256,1024]{1,0:T(8,128)(2,1)S(1)}, bf16[256,1024]{1,0:T(8,128)(2,1)S(1)}, u32[]{:S(2)}, u32[]{:S(2)}) collective-permute-start(bf16[256,1024]{1,0:T(8,128)(2,1)S(1)} %slice_bitcast_fusion), channel_id=1, source_target_pairs={{0,1},{1,0},{2,3},{3,2},{4,5},{5,4},{6,7},{7,6},{8,9},{9,8},{10,11... | collective-permute-start | bytes 1572872 | tf_op jit(solution)/shard_map/ppermute | solution.py:35
  3.1 0.0 copy-done
  3.1 0.6 constant_dynamic-slice_fusion
  5.0 0.0 collective-permute-done
  5.0 0.0 copy-done.4
  5.0 0.9 %bitcast_select_fusion = bf16[256,1024]{1,0:T(8,128)(2,1)} fusion(bf16[256,1024]{1,0:T(8,128)(2,1)S(1)} %collective-permute-done, bf16[1,512,1024]{2,1,0:T(8,128)(2,1)S(1)} %copy-done.4, pred[]{:T(512)S(6)} %eq.7, pred[]{:T(512)S(6)} %eq.6), kind=kLoop, calls=%fused_computation | loop fusion | flops 524288 | bytes 1572866 | tf_op jit(solution)/shard_map/jit(_where)/select_n | solution.py:273
  5.9 0.0 copy-start.1
  5.9 0.0 copy-start.2
  5.9 5.8 %all-to-all-start = ((bf16[8,32,1024]{2,1,0:T(8,128)(2,1)}), bf16[8,32,1024]{2,1,0:T(8,128)(2,1)S(1)}, u32[]{:S(2)}, u32[]{:S(2)}) async-start(bf16[8,32,1024]{2,1,0:T(8,128)(2,1)} %bitcast.5), calls=%async_computation | async-start | bytes 1048576 | tf_op jit(solution)/shard_map/all_to_all | solution.py:274
  11.7 0.0 copy-done.1
  11.7 0.0 copy-done.2
  11.7 0.2 shard_map.55
  11.9 2.7 %collective-permute-start.2 = (bf16[1024,256]{1,0:T(8,128)(2,1)S(1)}, bf16[1024,256]{1,0:T(8,128)(2,1)S(1)}, u32[]{:S(2)}, u32[]{:S(2)}) collective-permute-start(bf16[1024,256]{1,0:T(8,128)(2,1)S(1)} %get-tuple-element.21.own_ref), channel_id=1, source_target_pairs={{0,128},{128,0},{1,129},{129,1},{2,130},{130,2},{3,131},{131,3},{4... | collective-permute-start | bytes 1572872 | tf_op jit(solution)/shard_map/ppermute | solution.py:35
  14.5 7.9 %all-to-all-done = bf16[8,32,1024]{2,1,0:T(8,128)(2,1)S(1)} async-done(((bf16[8,32,1024]{2,1,0:T(8,128)(2,1)}), bf16[8,32,1024]{2,1,0:T(8,128)(2,1)S(1)}, u32[]{:S(2)}, u32[]{:S(2)}) %all-to-all-start) | async-done | bytes 524320 | tf_op jit(solution)/shard_map/all_to_all | solution.py:274
  22.4 0.1 reduce_sum.12
  22.5 5.2 %collective-permute-start.1 = (bf16[32,1024]{1,0:T(8,128)(2,1)S(1)}, bf16[32,1024]{1,0:T(8,128)(2,1)S(1)}, u32[]{:S(2)}, u32[]{:S(2)}) collective-permute-start(bf16[32,1024]{1,0:T(8,128)(2,1)S(1)} %reduce_sum.12), channel_id=1, source_target_pairs={{0,16},{16,0},{1,17},{17,1},{2,18},{18,2},{3,19},{19,3},{4,20},{20... | collective-permute-start | bytes 196616 | tf_op jit(solution)/shard_map/ppermute | solution.py:35
  27.7 2.9 %collective-permute-done.1 = bf16[32,1024]{1,0:T(8,128)(2,1)S(1)} collective-permute-done((bf16[32,1024]{1,0:T(8,128)(2,1)S(1)}, bf16[32,1024]{1,0:T(8,128)(2,1)S(1)}, u32[]{:S(2)}, u32[]{:S(2)}) %collective-permute-start.1) | collective-permute-done | bytes 65568 | tf_op jit(solution)/shard_map/ppermute | solution.py:35
  30.6 0.0 collective-permute-done.2.other_ref
  30.6 0.1 broadcast_in_dim.14
  30.8 17.9 %all_to_all.10 = bf16[16,32,1024]{2,1,0:T(8,128)(2,1)S(1)} all-to-all(bf16[16,32,1024]{2,1,0:T(8,128)(2,1)S(1)} %broadcast_in_dim.14), channel_id=1, replica_groups=mesh['yh'=2,'yl'=2,'p'=4,'zh'=2,'zl'=2,'x'=4,'c'=2] {'yl','x','zl'}, dimensions={0} | all-to-all | bytes 2097152 | tf_op jit(solution)/shard_map/all_to_all | solution.py:279
  48.7 0.0 copy-start.3
  48.7 2.0 %collective-permute-start.4 = (bf16[2,256,1024]{2,1,0:T(8,128)(2,1)S(1)}, bf16[2,256,1024]{2,1,0:T(8,128)(2,1)S(1)}, u32[]{:S(2)}, u32[]{:S(2)}) collective-permute-start(bf16[2,256,1024]{2,1,0:T(8,128)(2,1)S(1)} %bitcast.10), channel_id=1, source_target_pairs={{0,1},{1,0},{2,3},{3,2},{4,5},{5,4},{6,7},{7,6},{8,9},{9,8},{10,11... | collective-permute-start | bytes 3145736 | tf_op jit(solution)/shard_map/ppermute | solution.py:35
  50.7 2.5 %collective-permute-start.3 = (bf16[256,256]{1,0:T(8,128)(2,1)S(1)}, bf16[256,256]{1,0:T(8,128)(2,1)S(1)}, u32[]{:S(2)}, u32[]{:S(2)}) collective-permute-start(bf16[256,256]{1,0:T(8,128)(2,1)S(1)} %get-tuple-element.23.refs_0_), channel_id=1, source_target_pairs={{0,128},{128,0},{1,129},{129,1},{2,130},{130,2},{3,131},{131,3},{4... | collective-permute-start | bytes 393224 | tf_op jit(solution)/shard_map/ppermute | solution.py:35
  53.2 0.2 collective-permute-done.4.refs_1_.refs_3_.refs_5_.refs_7_
  53.3 0.0 copy-done.3
  53.3 1.3 %collective-permute-start.5 = (bf16[512,256]{1,0:T(8,128)(2,1)S(1)}, bf16[512,256]{1,0:T(8,128)(2,1)S(1)}, u32[]{:S(2)}, u32[]{:S(2)}) collective-permute-start(bf16[512,256]{1,0:T(8,128)(2,1)S(1)} %get-tuple-element.25), channel_id=1, source_target_pairs={{0,384},{128,256},{1,385},{129,257},{2,386},{130,258},{3,387},{131... | collective-permute-start | bytes 786440 | tf_op jit(solution)/shard_map/ppermute | solution.py:304
  54.6 3.9 %collective-permute-done.3.refs_1_ = bf16[256,256]{1,0:T(8,128)(2,1)S(1)} collective-permute-done((bf16[256,256]{1,0:T(8,128)(2,1)S(1)}, bf16[256,256]{1,0:T(8,128)(2,1)S(1)}, u32[]{:S(2)}, u32[]{:S(2)}) %collective-permute-start.3) | collective-permute-done | bytes 131104 | tf_op jit(solution)/shard_map/ppermute | solution.py:35
  58.5 1.3 %collective-permute-start.6 = (bf16[512,128]{1,0:T(8,128)(2,1)S(1)}, bf16[512,128]{1,0:T(8,128)(2,1)S(1)}, u32[]{:S(2)}, u32[]{:S(2)}) collective-permute-start(bf16[512,128]{1,0:T(8,128)(2,1)S(1)} %get-tuple-element.27), channel_id=1, source_target_pairs={{0,384},{128,256},{1,385},{129,257},{2,386},{130,258},{3,387},{131... | collective-permute-start | bytes 393224 | tf_op jit(solution)/shard_map/ppermute | solution.py:304
  59.8 1.3 %collective-permute-start.7 = (bf16[512,128]{1,0:T(8,128)(2,1)S(1)}, bf16[512,128]{1,0:T(8,128)(2,1)S(1)}, u32[]{:S(2)}, u32[]{:S(2)}) collective-permute-start(bf16[512,128]{1,0:T(8,128)(2,1)S(1)} %get-tuple-element.31), channel_id=1, source_target_pairs={{0,384},{128,256},{1,385},{129,257},{2,386},{130,258},{3,387},{131... | collective-permute-start | bytes 393224 | tf_op jit(solution)/shard_map/ppermute | solution.py:304
  61.1 7.4 %collective-permute-done.5.refs_0_ = bf16[512,256]{1,0:T(8,128)(2,1)S(1)} collective-permute-done((bf16[512,256]{1,0:T(8,128)(2,1)S(1)}, bf16[512,256]{1,0:T(8,128)(2,1)S(1)}, u32[]{:S(2)}, u32[]{:S(2)}) %collective-permute-start.5) | collective-permute-done | bytes 262176 | tf_op jit(solution)/shard_map/ppermute | solution.py:304
  68.5 3.0 %shard_map.57.refs_4_ = bf16[32,4096]{1,0:T(8,128)(2,1)S(1)} custom-call(s32[2,4]{1,0:T(2,128)S(1)} %copy-done.3, bf16[1024,256]{1,0:T(8,128)(2,1)S(1)} %get-tuple-element.21.own_ref, bf16[1024,256]{1,0:T(8,128)(2,1)S(1)} %collective-permute-done.2.other_ref, bf16[512,256]{1,0:T(8,128)(2,1)S(1)} %collective-permute-done.5.refs_0_, ...), custom_call_target="tpu_custom_call" | custom-call | flops 3200000000 | bytes 4194304 | tf_op jit(solution)/shard_map/pallas_call | solution.py:253
  71.4 0.0 collective-permute-done.6.refs_2_
  71.5 2.3 %shard_map.59.refs_5_ = bf16[16,4096]{1,0:T(8,128)(2,1)S(1)} custom-call(s32[2,4]{1,0:T(2,128)S(1)} %copy-done.3, bf16[1024,256]{1,0:T(8,128)(2,1)S(1)} %get-tuple-element.21.own_ref, bf16[1024,256]{1,0:T(8,128)(2,1)S(1)} %collective-permute-done.2.other_ref, bf16[256,256]{1,0:T(8,128)(2,1)S(1)} %get-tuple-element.23.refs_0_, ...), custom_call_target="tpu_custom_call" | custom-call | flops 2400000000 | bytes 4194304 | tf_op jit(solution)/shard_map/pallas_call | solution.py:253
  73.8 0.0 collective-permute-done.7.refs_2_
  73.8 3.0 %shard_map.60 = bf16[64,4096]{1,0:T(8,128)(2,1)} custom-call(s32[2,4]{1,0:T(2,128)S(1)} %copy-done.3, bf16[1024,256]{1,0:T(8,128)(2,1)S(1)} %get-tuple-element.21.own_ref, bf16[1024,256]{1,0:T(8,128)(2,1)S(1)} %collective-permute-done.2.other_ref, bf16[256,256]{1,0:T(8,128)(2,1)S(1)} %get-tuple-element.23.refs_0_, ...), custom_call_target="tpu_custom_call" | custom-call | flops 2400000000 | bytes 4194304 | tf_op jit(solution)/shard_map/pallas_call | solution.py:253
  (3 shorter events, 0.0 us)
Async XLA Ops:
  0.0 3.1 %copy-start = (s32[1,4]{1,0:T(1,128)S(1)}, s32[1,4]{1,0:T(1,128)}, u32[]{:S(2)}) copy-start(s32[1,4]{1,0:T(1,128)} %param.8) | copy-start | bytes 52
  0.0 5.0 %copy-start.4 = (bf16[1,512,1024]{2,1,0:T(8,128)(2,1)S(1)}, bf16[1,512,1024]{2,1,0:T(8,128)(2,1)}, u32[]{:S(2)}) copy-start(bf16[1,512,1024]{2,1,0:T(8,128)(2,1)} %param.7) | copy-start | bytes 3145732
  1.2 3.8 %collective-permute-start = (bf16[256,1024]{1,0:T(8,128)(2,1)S(1)}, bf16[256,1024]{1,0:T(8,128)(2,1)S(1)}, u32[]{:S(2)}, u32[]{:S(2)}) collective-permute-start(bf16[256,1024]{1,0:T(8,128)(2,1)S(1)} %slice_bitcast_fusion), channel_id=1, source_target_pairs={{0,1},{1,0},{2,3},{3,2},{4,5},{5,4},{6,7},{7,6},{8,9},{9,8},{10,11... | collective-permute-start | bytes 1572872 | tf_op jit(solution)/shard_map/ppermute | solution.py:35
  5.9 5.8 %copy-start.1 = (bf16[1,64,4096]{2,1,0:T(8,128)(2,1)S(1)}, bf16[1,64,4096]{2,1,0:T(8,128)(2,1)}, u32[]{:S(2)}) copy-start(bf16[1,64,4096]{2,1,0:T(8,128)(2,1)} %param.5) | copy-start | bytes 1572868
  5.9 5.8 %copy-start.2 = (bf16[1,64,1024]{2,1,0:T(8,128)(2,1)S(1)}, bf16[1,64,1024]{2,1,0:T(8,128)(2,1)}, u32[]{:S(2)}) copy-start(bf16[1,64,1024]{2,1,0:T(8,128)(2,1)} %param.6) | copy-start | bytes 393220
  5.9 16.5 %all-to-all-start = ((bf16[8,32,1024]{2,1,0:T(8,128)(2,1)}), bf16[8,32,1024]{2,1,0:T(8,128)(2,1)S(1)}, u32[]{:S(2)}, u32[]{:S(2)}) async-start(bf16[8,32,1024]{2,1,0:T(8,128)(2,1)} %bitcast.5), calls=%async_computation | async-start | bytes 1048576 | tf_op jit(solution)/shard_map/all_to_all | solution.py:274
  11.9 18.8 %collective-permute-start.2 = (bf16[1024,256]{1,0:T(8,128)(2,1)S(1)}, bf16[1024,256]{1,0:T(8,128)(2,1)S(1)}, u32[]{:S(2)}, u32[]{:S(2)}) collective-permute-start(bf16[1024,256]{1,0:T(8,128)(2,1)S(1)} %get-tuple-element.21.own_ref), channel_id=1, source_target_pairs={{0,128},{128,0},{1,129},{129,1},{2,130},{130,2},{3,131},{131,3},{4... | collective-permute-start | bytes 1572872 | tf_op jit(solution)/shard_map/ppermute | solution.py:35
  22.5 8.1 %collective-permute-start.1 = (bf16[32,1024]{1,0:T(8,128)(2,1)S(1)}, bf16[32,1024]{1,0:T(8,128)(2,1)S(1)}, u32[]{:S(2)}, u32[]{:S(2)}) collective-permute-start(bf16[32,1024]{1,0:T(8,128)(2,1)S(1)} %reduce_sum.12), channel_id=1, source_target_pairs={{0,16},{16,0},{1,17},{17,1},{2,18},{18,2},{3,19},{19,3},{4,20},{20... | collective-permute-start | bytes 196616 | tf_op jit(solution)/shard_map/ppermute | solution.py:35
  48.7 4.7 %copy-start.3 = (s32[2,4]{1,0:T(2,128)S(1)}, s32[2,4]{1,0:T(2,128)}, u32[]{:S(2)}) copy-start(s32[2,4]{1,0:T(2,128)} %seg_ref.9) | copy-start | bytes 100
  48.7 4.7 %collective-permute-start.4 = (bf16[2,256,1024]{2,1,0:T(8,128)(2,1)S(1)}, bf16[2,256,1024]{2,1,0:T(8,128)(2,1)S(1)}, u32[]{:S(2)}, u32[]{:S(2)}) collective-permute-start(bf16[2,256,1024]{2,1,0:T(8,128)(2,1)S(1)} %bitcast.10), channel_id=1, source_target_pairs={{0,1},{1,0},{2,3},{3,2},{4,5},{5,4},{6,7},{7,6},{8,9},{9,8},{10,11... | collective-permute-start | bytes 3145736 | tf_op jit(solution)/shard_map/ppermute | solution.py:35
  50.7 7.8 %collective-permute-start.3 = (bf16[256,256]{1,0:T(8,128)(2,1)S(1)}, bf16[256,256]{1,0:T(8,128)(2,1)S(1)}, u32[]{:S(2)}, u32[]{:S(2)}) collective-permute-start(bf16[256,256]{1,0:T(8,128)(2,1)S(1)} %get-tuple-element.23.refs_0_), channel_id=1, source_target_pairs={{0,128},{128,0},{1,129},{129,1},{2,130},{130,2},{3,131},{131,3},{4... | collective-permute-start | bytes 393224 | tf_op jit(solution)/shard_map/ppermute | solution.py:35
  53.3 15.1 %collective-permute-start.5 = (bf16[512,256]{1,0:T(8,128)(2,1)S(1)}, bf16[512,256]{1,0:T(8,128)(2,1)S(1)}, u32[]{:S(2)}, u32[]{:S(2)}) collective-permute-start(bf16[512,256]{1,0:T(8,128)(2,1)S(1)} %get-tuple-element.25), channel_id=1, source_target_pairs={{0,384},{128,256},{1,385},{129,257},{2,386},{130,258},{3,387},{131... | collective-permute-start | bytes 786440 | tf_op jit(solution)/shard_map/ppermute | solution.py:304
  58.5 12.9 %collective-permute-start.6 = (bf16[512,128]{1,0:T(8,128)(2,1)S(1)}, bf16[512,128]{1,0:T(8,128)(2,1)S(1)}, u32[]{:S(2)}, u32[]{:S(2)}) collective-permute-start(bf16[512,128]{1,0:T(8,128)(2,1)S(1)} %get-tuple-element.27), channel_id=1, source_target_pairs={{0,384},{128,256},{1,385},{129,257},{2,386},{130,258},{3,387},{131... | collective-permute-start | bytes 393224 | tf_op jit(solution)/shard_map/ppermute | solution.py:304
  59.8 14.0 %collective-permute-start.7 = (bf16[512,128]{1,0:T(8,128)(2,1)S(1)}, bf16[512,128]{1,0:T(8,128)(2,1)S(1)}, u32[]{:S(2)}, u32[]{:S(2)}) collective-permute-start(bf16[512,128]{1,0:T(8,128)(2,1)S(1)} %get-tuple-element.31), channel_id=1, source_target_pairs={{0,384},{128,256},{1,385},{129,257},{2,386},{130,258},{3,387},{131... | collective-permute-start | bytes 393224 | tf_op jit(solution)/shard_map/ppermute | solution.py:304

commit v8 on v6

--- a/solution.py
+++ b/solution.py
@@ -28,7 +28,7 @@
 SECTION = ("yh", "yl")
 RESP = ("p", "zh", "zl", "x", "c")
 PLANE = ("zl", "x")
-SPREAD = ("yl", *PLANE)
+SPREAD = ("yl", "x", "zl")
 
 
 def swap(x, axis):

time: 78.1 us -> 77.3 us (0.990)
  starting transfers between devices: 24.8 us -> 23.9 us
  waiting for transfers between devices: 21.2 us -> 22.1 us
    ppermute x5, waiting for transfers between devices: 6.43 us -> 7.39 us  [swap(): return lax.ppermute(x, axis, [(0, 1), (1, 0)])]
    ppermute x5, starting transfers between devices: 15.2 us -> 14.3 us  [swap(): return lax.ppermute(x, axis, [(0, 1), (1, 0)])]
  transfers between devices with their start and end apart: 9 -> 9, of which waited for: 4 -> 5; matrix products, arithmetic and copies ran while one was open for 1% -> 1% of each run, Pallas kernels for 7% -> 7%
where the time goes in v8:
time: 77.3 us; the launch traced here: 76.8 us
  starting transfers between devices  23.9 us (31%)
  waiting for transfers between devices  22.1 us (29%)
  blocking collectives  18.1 us (23%)
  Pallas kernels  8.49 us (11%)
  local copies, waits for them, and re-layouts  1.88 us (2%)
  between operations  1.48 us (2%)
  other arithmetic  0.95 us (1%)
    all_to_all x1, blocking collectives, spread_prefix(): lax.all_to_all(jnp.broadcast_to(piece[None], (copies, *piece.shape)), SPR...  18.1 us
    ppermute x5, starting transfers between devices, swap(): return lax.ppermute(x, axis, [(0, 1), (1, 0)])  14.3 us
    pallas_call x5, Pallas kernels, attend_pair(): pl.pallas_call(functools.partial(pair_kernel, parts, bool(carried), len(r...  8.3 us
    ppermute x3, waiting for transfers between devices, local(): carried.append((lax.ppermute(last, SECTION, [(0, 3), (1, 2)]), kept))  7.44 us
    ppermute x5, waiting for transfers between devices, swap(): return lax.ppermute(x, axis, [(0, 1), (1, 0)])  7.39 us
    all_to_all x1, waiting for transfers between devices, spread_prefix(): pieces = lax.all_to_all(mine.reshape(parts, half // parts, -1), PLANE, 0, 0)  7.22 us
    all_to_all x1, starting transfers between devices, spread_prefix(): pieces = lax.all_to_all(mine.reshape(parts, half // parts, -1), PLANE, 0, 0)  5.79 us
    ppermute x3, starting transfers between devices, local(): carried.append((lax.ppermute(last, SECTION, [(0, 3), (1, 2)]), kept))  3.85 us
  transfers between devices with their start and end apart: 9, of which 5 were waited for; matrix products, arithmetic and copies ran while one was open for 1% of the time, Pallas kernels for 7%

profile of v8, /device:TPU:24, one launch (start us, length us, event | category | flops | bytes accessed | tf_op | source)
XLA Modules:
  0.0 76.8 jit_solution(231995693309495522)
XLA Ops:
  0.0 0.0 copy-start
  0.0 0.0 copy-start.4
  0.0 1.2 %slice_bitcast_fusion = bf16[256,1024]{1,0:T(8,128)(2,1)S(1)} fusion(bf16[1,512,1024]{2,1,0:T(8,128)(2,1)} %param.7), kind=kLoop, calls=%fused_computation.1 | loop fusion | bytes 1048576 | tf_op jit(solution)/shard_map/slice | solution.py:271
  1.2 1.9 %collective-permute-start = (bf16[256,1024]{1,0:T(8,128)(2,1)S(1)}, bf16[256,1024]{1,0:T(8,128)(2,1)S(1)}, u32[]{:S(2)}, u32[]{:S(2)}) collective-permute-start(bf16[256,1024]{1,0:T(8,128)(2,1)S(1)} %slice_bitcast_fusion), channel_id=1, source_target_pairs={{0,1},{1,0},{2,3},{3,2},{4,5},{5,4},{6,7},{7,6},{8,9},{9,8},{10,11... | collective-permute-start | bytes 1572872 | tf_op jit(solution)/shard_map/ppermute | solution.py:35
  3.1 0.0 copy-done
  3.1 0.6 constant_dynamic-slice_fusion
  5.0 0.0 collective-permute-done
  5.0 0.0 copy-done.4
  5.0 0.9 %bitcast_select_fusion = bf16[256,1024]{1,0:T(8,128)(2,1)} fusion(bf16[256,1024]{1,0:T(8,128)(2,1)S(1)} %collective-permute-done, bf16[1,512,1024]{2,1,0:T(8,128)(2,1)S(1)} %copy-done.4, pred[]{:T(512)S(6)} %eq.7, pred[]{:T(512)S(6)} %eq.6), kind=kLoop, calls=%fused_computation | loop fusion | flops 524288 | bytes 1572866 | tf_op jit(solution)/shard_map/jit(_where)/select_n | solution.py:273
  5.9 0.0 copy-start.1
  5.9 0.0 copy-start.2
  5.9 5.8 %all-to-all-start = ((bf16[8,32,1024]{2,1,0:T(8,128)(2,1)}), bf16[8,32,1024]{2,1,0:T(8,128)(2,1)S(1)}, u32[]{:S(2)}, u32[]{:S(2)}) async-start(bf16[8,32,1024]{2,1,0:T(8,128)(2,1)} %bitcast.5), calls=%async_computation | async-start | bytes 1048576 | tf_op jit(solution)/shard_map/all_to_all | solution.py:274
  11.7 0.0 copy-done.1
  11.7 0.0 copy-done.2
  11.7 0.2 shard_map.55
  11.9 2.7 %collective-permute-start.2 = (bf16[1024,256]{1,0:T(8,128)(2,1)S(1)}, bf16[1024,256]{1,0:T(8,128)(2,1)S(1)}, u32[]{:S(2)}, u32[]{:S(2)}) collective-permute-start(bf16[1024,256]{1,0:T(8,128)(2,1)S(1)} %get-tuple-element.21.own_ref), channel_id=1, source_target_pairs={{0,128},{128,0},{1,129},{129,1},{2,130},{130,2},{3,131},{131,3},{4... | collective-permute-start | bytes 1572872 | tf_op jit(solution)/shard_map/ppermute | solution.py:35
  14.5 7.2 %all-to-all-done = bf16[8,32,1024]{2,1,0:T(8,128)(2,1)S(1)} async-done(((bf16[8,32,1024]{2,1,0:T(8,128)(2,1)}), bf16[8,32,1024]{2,1,0:T(8,128)(2,1)S(1)}, u32[]{:S(2)}, u32[]{:S(2)}) %all-to-all-start) | async-done | bytes 524320 | tf_op jit(solution)/shard_map/all_to_all | solution.py:274
  21.8 0.1 reduce_sum.12
  21.8 5.2 %collective-permute-start.1 = (bf16[32,1024]{1,0:T(8,128)(2,1)S(1)}, bf16[32,1024]{1,0:T(8,128)(2,1)S(1)}, u32[]{:S(2)}, u32[]{:S(2)}) collective-permute-start(bf16[32,1024]{1,0:T(8,128)(2,1)S(1)} %reduce_sum.12), channel_id=1, source_target_pairs={{0,16},{16,0},{1,17},{17,1},{2,18},{18,2},{3,19},{19,3},{4,20},{20... | collective-permute-start | bytes 196616 | tf_op jit(solution)/shard_map/ppermute | solution.py:35
  27.0 3.4 %collective-permute-done.1 = bf16[32,1024]{1,0:T(8,128)(2,1)S(1)} collective-permute-done((bf16[32,1024]{1,0:T(8,128)(2,1)S(1)}, bf16[32,1024]{1,0:T(8,128)(2,1)S(1)}, u32[]{:S(2)}, u32[]{:S(2)}) %collective-permute-start.1) | collective-permute-done | bytes 65568 | tf_op jit(solution)/shard_map/ppermute | solution.py:35
  30.4 0.0 collective-permute-done.2.other_ref
  30.4 0.1 broadcast_in_dim.14
  30.5 18.1 %all_to_all.10 = bf16[16,32,1024]{2,1,0:T(8,128)(2,1)S(1)} all-to-all(bf16[16,32,1024]{2,1,0:T(8,128)(2,1)S(1)} %broadcast_in_dim.14), channel_id=1, replica_groups=mesh['yh'=2,'yl'=2,'p'=4,'zh'=2,'zl'=2,'x'=4,'c'=2] {'yl','x','zl'}, dimensions={0} | all-to-all | bytes 2097152 | tf_op jit(solution)/shard_map/all_to_all | solution.py:279
  48.6 0.0 copy-start.3
  48.6 2.0 %collective-permute-start.4 = (bf16[2,256,1024]{2,1,0:T(8,128)(2,1)S(1)}, bf16[2,256,1024]{2,1,0:T(8,128)(2,1)S(1)}, u32[]{:S(2)}, u32[]{:S(2)}) collective-permute-start(bf16[2,256,1024]{2,1,0:T(8,128)(2,1)S(1)} %bitcast.10), channel_id=1, source_target_pairs={{0,1},{1,0},{2,3},{3,2},{4,5},{5,4},{6,7},{7,6},{8,9},{9,8},{10,11... | collective-permute-start | bytes 3145736 | tf_op jit(solution)/shard_map/ppermute | solution.py:35
  50.7 2.5 %collective-permute-start.3 = (bf16[256,256]{1,0:T(8,128)(2,1)S(1)}, bf16[256,256]{1,0:T(8,128)(2,1)S(1)}, u32[]{:S(2)}, u32[]{:S(2)}) collective-permute-start(bf16[256,256]{1,0:T(8,128)(2,1)S(1)} %get-tuple-element.23.refs_0_), channel_id=1, source_target_pairs={{0,128},{128,0},{1,129},{129,1},{2,130},{130,2},{3,131},{131,3},{4... | collective-permute-start | bytes 393224 | tf_op jit(solution)/shard_map/ppermute | solution.py:35
  53.1 0.2 collective-permute-done.4.refs_1_.refs_3_.refs_5_.refs_7_
  53.3 0.0 copy-done.3
  53.3 1.3 %collective-permute-start.5 = (bf16[512,256]{1,0:T(8,128)(2,1)S(1)}, bf16[512,256]{1,0:T(8,128)(2,1)S(1)}, u32[]{:S(2)}, u32[]{:S(2)}) collective-permute-start(bf16[512,256]{1,0:T(8,128)(2,1)S(1)} %get-tuple-element.25), channel_id=1, source_target_pairs={{0,384},{128,256},{1,385},{129,257},{2,386},{130,258},{3,387},{131... | collective-permute-start | bytes 786440 | tf_op jit(solution)/shard_map/ppermute | solution.py:304
  54.6 3.9 %collective-permute-done.3.refs_1_ = bf16[256,256]{1,0:T(8,128)(2,1)S(1)} collective-permute-done((bf16[256,256]{1,0:T(8,128)(2,1)S(1)}, bf16[256,256]{1,0:T(8,128)(2,1)S(1)}, u32[]{:S(2)}, u32[]{:S(2)}) %collective-permute-start.3) | collective-permute-done | bytes 131104 | tf_op jit(solution)/shard_map/ppermute | solution.py:35
  58.5 1.3 %collective-permute-start.6 = (bf16[512,128]{1,0:T(8,128)(2,1)S(1)}, bf16[512,128]{1,0:T(8,128)(2,1)S(1)}, u32[]{:S(2)}, u32[]{:S(2)}) collective-permute-start(bf16[512,128]{1,0:T(8,128)(2,1)S(1)} %get-tuple-element.27), channel_id=1, source_target_pairs={{0,384},{128,256},{1,385},{129,257},{2,386},{130,258},{3,387},{131... | collective-permute-start | bytes 393224 | tf_op jit(solution)/shard_map/ppermute | solution.py:304
  59.7 1.3 %collective-permute-start.7 = (bf16[512,128]{1,0:T(8,128)(2,1)S(1)}, bf16[512,128]{1,0:T(8,128)(2,1)S(1)}, u32[]{:S(2)}, u32[]{:S(2)}) collective-permute-start(bf16[512,128]{1,0:T(8,128)(2,1)S(1)} %get-tuple-element.31), channel_id=1, source_target_pairs={{0,384},{128,256},{1,385},{129,257},{2,386},{130,258},{3,387},{131... | collective-permute-start | bytes 393224 | tf_op jit(solution)/shard_map/ppermute | solution.py:304
  61.0 7.4 %collective-permute-done.5.refs_0_ = bf16[512,256]{1,0:T(8,128)(2,1)S(1)} collective-permute-done((bf16[512,256]{1,0:T(8,128)(2,1)S(1)}, bf16[512,256]{1,0:T(8,128)(2,1)S(1)}, u32[]{:S(2)}, u32[]{:S(2)}) %collective-permute-start.5) | collective-permute-done | bytes 262176 | tf_op jit(solution)/shard_map/ppermute | solution.py:304
  68.5 3.0 %shard_map.57.refs_4_ = bf16[32,4096]{1,0:T(8,128)(2,1)S(1)} custom-call(s32[2,4]{1,0:T(2,128)S(1)} %copy-done.3, bf16[1024,256]{1,0:T(8,128)(2,1)S(1)} %get-tuple-element.21.own_ref, bf16[1024,256]{1,0:T(8,128)(2,1)S(1)} %collective-permute-done.2.other_ref, bf16[512,256]{1,0:T(8,128)(2,1)S(1)} %collective-permute-done.5.refs_0_, ...), custom_call_target="tpu_custom_call" | custom-call | flops 3200000000 | bytes 4194304 | tf_op jit(solution)/shard_map/pallas_call | solution.py:253
  71.5 0.0 collective-permute-done.6.refs_2_
  71.5 2.3 %shard_map.59.refs_5_ = bf16[16,4096]{1,0:T(8,128)(2,1)S(1)} custom-call(s32[2,4]{1,0:T(2,128)S(1)} %copy-done.3, bf16[1024,256]{1,0:T(8,128)(2,1)S(1)} %get-tuple-element.21.own_ref, bf16[1024,256]{1,0:T(8,128)(2,1)S(1)} %collective-permute-done.2.other_ref, bf16[256,256]{1,0:T(8,128)(2,1)S(1)} %get-tuple-element.23.refs_0_, ...), custom_call_target="tpu_custom_call" | custom-call | flops 2400000000 | bytes 4194304 | tf_op jit(solution)/shard_map/pallas_call | solution.py:253
  73.8 0.0 collective-permute-done.7.refs_2_
  73.8 3.0 %shard_map.60 = bf16[64,4096]{1,0:T(8,128)(2,1)} custom-call(s32[2,4]{1,0:T(2,128)S(1)} %copy-done.3, bf16[1024,256]{1,0:T(8,128)(2,1)S(1)} %get-tuple-element.21.own_ref, bf16[1024,256]{1,0:T(8,128)(2,1)S(1)} %collective-permute-done.2.other_ref, bf16[256,256]{1,0:T(8,128)(2,1)S(1)} %get-tuple-element.23.refs_0_, ...), custom_call_target="tpu_custom_call" | custom-call | flops 2400000000 | bytes 4194304 | tf_op jit(solution)/shard_map/pallas_call | solution.py:253
  (3 shorter events, 0.0 us)
Async XLA Ops:
  0.0 3.1 %copy-start = (s32[1,4]{1,0:T(1,128)S(1)}, s32[1,4]{1,0:T(1,128)}, u32[]{:S(2)}) copy-start(s32[1,4]{1,0:T(1,128)} %param.8) | copy-start | bytes 52
  0.0 5.0 %copy-start.4 = (bf16[1,512,1024]{2,1,0:T(8,128)(2,1)S(1)}, bf16[1,512,1024]{2,1,0:T(8,128)(2,1)}, u32[]{:S(2)}) copy-start(bf16[1,512,1024]{2,1,0:T(8,128)(2,1)} %param.7) | copy-start | bytes 3145732
  1.2 3.8 %collective-permute-start = (bf16[256,1024]{1,0:T(8,128)(2,1)S(1)}, bf16[256,1024]{1,0:T(8,128)(2,1)S(1)}, u32[]{:S(2)}, u32[]{:S(2)}) collective-permute-start(bf16[256,1024]{1,0:T(8,128)(2,1)S(1)} %slice_bitcast_fusion), channel_id=1, source_target_pairs={{0,1},{1,0},{2,3},{3,2},{4,5},{5,4},{6,7},{7,6},{8,9},{9,8},{10,11... | collective-permute-start | bytes 1572872 | tf_op jit(solution)/shard_map/ppermute | solution.py:35
  5.9 5.8 %copy-start.1 = (bf16[1,64,4096]{2,1,0:T(8,128)(2,1)S(1)}, bf16[1,64,4096]{2,1,0:T(8,128)(2,1)}, u32[]{:S(2)}) copy-start(bf16[1,64,4096]{2,1,0:T(8,128)(2,1)} %param.5) | copy-start | bytes 1572868
  5.9 5.8 %copy-start.2 = (bf16[1,64,1024]{2,1,0:T(8,128)(2,1)S(1)}, bf16[1,64,1024]{2,1,0:T(8,128)(2,1)}, u32[]{:S(2)}) copy-start(bf16[1,64,1024]{2,1,0:T(8,128)(2,1)} %param.6) | copy-start | bytes 393220
  5.9 15.9 %all-to-all-start = ((bf16[8,32,1024]{2,1,0:T(8,128)(2,1)}), bf16[8,32,1024]{2,1,0:T(8,128)(2,1)S(1)}, u32[]{:S(2)}, u32[]{:S(2)}) async-start(bf16[8,32,1024]{2,1,0:T(8,128)(2,1)} %bitcast.5), calls=%async_computation | async-start | bytes 1048576 | tf_op jit(solution)/shard_map/all_to_all | solution.py:274
  11.9 18.5 %collective-permute-start.2 = (bf16[1024,256]{1,0:T(8,128)(2,1)S(1)}, bf16[1024,256]{1,0:T(8,128)(2,1)S(1)}, u32[]{:S(2)}, u32[]{:S(2)}) collective-permute-start(bf16[1024,256]{1,0:T(8,128)(2,1)S(1)} %get-tuple-element.21.own_ref), channel_id=1, source_target_pairs={{0,128},{128,0},{1,129},{129,1},{2,130},{130,2},{3,131},{131,3},{4... | collective-permute-start | bytes 1572872 | tf_op jit(solution)/shard_map/ppermute | solution.py:35
  21.8 8.5 %collective-permute-start.1 = (bf16[32,1024]{1,0:T(8,128)(2,1)S(1)}, bf16[32,1024]{1,0:T(8,128)(2,1)S(1)}, u32[]{:S(2)}, u32[]{:S(2)}) collective-permute-start(bf16[32,1024]{1,0:T(8,128)(2,1)S(1)} %reduce_sum.12), channel_id=1, source_target_pairs={{0,16},{16,0},{1,17},{17,1},{2,18},{18,2},{3,19},{19,3},{4,20},{20... | collective-permute-start | bytes 196616 | tf_op jit(solution)/shard_map/ppermute | solution.py:35
  48.6 4.7 %copy-start.3 = (s32[2,4]{1,0:T(2,128)S(1)}, s32[2,4]{1,0:T(2,128)}, u32[]{:S(2)}) copy-start(s32[2,4]{1,0:T(2,128)} %seg_ref.9) | copy-start | bytes 100
  48.6 4.7 %collective-permute-start.4 = (bf16[2,256,1024]{2,1,0:T(8,128)(2,1)S(1)}, bf16[2,256,1024]{2,1,0:T(8,128)(2,1)S(1)}, u32[]{:S(2)}, u32[]{:S(2)}) collective-permute-start(bf16[2,256,1024]{2,1,0:T(8,128)(2,1)S(1)} %bitcast.10), channel_id=1, source_target_pairs={{0,1},{1,0},{2,3},{3,2},{4,5},{5,4},{6,7},{7,6},{8,9},{9,8},{10,11... | collective-permute-start | bytes 3145736 | tf_op jit(solution)/shard_map/ppermute | solution.py:35
  50.7 7.8 %collective-permute-start.3 = (bf16[256,256]{1,0:T(8,128)(2,1)S(1)}, bf16[256,256]{1,0:T(8,128)(2,1)S(1)}, u32[]{:S(2)}, u32[]{:S(2)}) collective-permute-start(bf16[256,256]{1,0:T(8,128)(2,1)S(1)} %get-tuple-element.23.refs_0_), channel_id=1, source_target_pairs={{0,128},{128,0},{1,129},{129,1},{2,130},{130,2},{3,131},{131,3},{4... | collective-permute-start | bytes 393224 | tf_op jit(solution)/shard_map/ppermute | solution.py:35
  53.3 15.2 %collective-permute-start.5 = (bf16[512,256]{1,0:T(8,128)(2,1)S(1)}, bf16[512,256]{1,0:T(8,128)(2,1)S(1)}, u32[]{:S(2)}, u32[]{:S(2)}) collective-permute-start(bf16[512,256]{1,0:T(8,128)(2,1)S(1)} %get-tuple-element.25), channel_id=1, source_target_pairs={{0,384},{128,256},{1,385},{129,257},{2,386},{130,258},{3,387},{131... | collective-permute-start | bytes 786440 | tf_op jit(solution)/shard_map/ppermute | solution.py:304
  58.5 13.0 %collective-permute-start.6 = (bf16[512,128]{1,0:T(8,128)(2,1)S(1)}, bf16[512,128]{1,0:T(8,128)(2,1)S(1)}, u32[]{:S(2)}, u32[]{:S(2)}) collective-permute-start(bf16[512,128]{1,0:T(8,128)(2,1)S(1)} %get-tuple-element.27), channel_id=1, source_target_pairs={{0,384},{128,256},{1,385},{129,257},{2,386},{130,258},{3,387},{131... | collective-permute-start | bytes 393224 | tf_op jit(solution)/shard_map/ppermute | solution.py:304
  59.7 14.1 %collective-permute-start.7 = (bf16[512,128]{1,0:T(8,128)(2,1)S(1)}, bf16[512,128]{1,0:T(8,128)(2,1)S(1)}, u32[]{:S(2)}, u32[]{:S(2)}) collective-permute-start(bf16[512,128]{1,0:T(8,128)(2,1)S(1)} %get-tuple-element.31), channel_id=1, source_target_pairs={{0,384},{128,256},{1,385},{129,257},{2,386},{130,258},{3,387},{131... | collective-permute-start | bytes 393224 | tf_op jit(solution)/shard_map/ppermute | solution.py:304
